TPU v7x, 256 devices: a whole 4x4x8 slice. The times are simulated.
256 devices in a mesh: outer: 8 (over x, core), inner: 4 (over y), heads: 8 (over z).
Axes of the slice: x: 4, y: 4, z: 8, core: 2. Of those that a mesh axis runs over, the one named last changes fastest.
Arguments:
- x_in: bfloat16 [8192, 8192], P(('outer', 'inner'), 'heads'), may hold values from -6 to 6
- b_in: bfloat16 [8192, 1024], P(('outer', 'inner'), 'heads'), may hold values from -1.796875 to 1.796875
- c_in: bfloat16 [8192, 1024], P(('outer', 'inner'), 'heads'), may hold values from -1.796875 to 1.796875
- decay_log: float32 [8192, 128], P(('outer', 'inner'), 'heads'), may hold values from -0.8 to 0, as said below
- d_skip: float32 [128], P('heads'), may hold values from 0.5 to 1.5
- gate: bfloat16 [8192, 8192], P(('outer', 'inner'), 'heads'), may hold values from -11 to 11
- norm_weight: float32 [8192], P('heads'), may hold values from 0.5 to 1.5
- d_out: bfloat16 [8192, 8192], P(('outer', 'inner'), 'heads'), may hold values from -40 to 40
Outputs:
- grad_x: bfloat16 [8192, 8192], P(('outer', 'inner'), 'heads')
- grad_b: float32 [8192, 1024], P(('outer', 'inner'), 'heads')
- grad_c: float32 [8192, 1024], P(('outer', 'inner'), 'heads')
- grad_decay: float32 [8192, 128], P(('outer', 'inner'), 'heads')
- grad_skip: float32 [128], P('heads')
- grad_gate: bfloat16 [8192, 8192], P(('outer', 'inner'), 'heads')
- grad_norm_weight: float32 [8192], P('heads')
Inputs may be any that keep to these rules, and one draw needn't show every extreme that they name: `decay_log`: strictly negative.
All inputs are finite; a program needn't handle non-finite values.
Results may differ from a plain program's by a relative error of at most 0.0014.
Values sent between devices are 32-bit elements; how exact they have to be, the bound alone decides.
No kernel may reach another device: no remote copies, remote signals or barrier semaphores. Data moves between devices by JAX's collectives and lax.ppermute only.
A program may use at most 128 MiB of HBM per device.

v0:
```python
import jax
import jax.numpy as jnp
from jax import lax
from jax.sharding import PartitionSpec as P

HEADS = 128
P_SIZE = 64
STATE = 128
SPAN = 256


EPS = 1e-05
HIGH = lax.Precision.HIGHEST


def entering(part, axis, combine, identity, reverse):
    count = lax.axis_size(axis)
    place = lax.axis_index(axis)
    ahead = count - 1 - place if reverse else place
    gathered = jax.tree.map(lambda a: lax.all_gather(a, axis), part)
    state = jax.tree.map(lambda a, e: jnp.zeros_like(a) + jnp.asarray(e, a.dtype), part, identity)

    def one(step, state):
        source = count - 1 - step if reverse else step
        return combine(
            state, jax.tree.map(lambda a: lax.dynamic_index_in_dim(a, source, 0, False), gathered)
        )

    return lax.fori_loop(0, ahead, one, state)


def combine(earlier, later):
    return (earlier[0] * later[0], later[0][:, None, None] * earlier[1] + later[1])


def forward_prefix(pair, identity):
    return entering(pair, ("outer", "inner"), combine, identity, False)[1]


def backward_suffix(pair, identity):
    return entering(pair, ("outer", "inner"), combine, identity, True)[1]


def on_device(x_in, b_in, c_in, decay_log, d_skip, gate, norm_weight, d_out):
    length, heads_dev = decay_log.shape
    groups_dev = b_in.shape[1] // STATE
    heads_per = heads_dev // groups_dev
    blocks = length // SPAN
    x_all = x_in.astype(jnp.float32).reshape(blocks, SPAN, heads_dev, P_SIZE)
    b_all = b_in.astype(jnp.float32).reshape(blocks, SPAN, groups_dev, STATE)
    c_all = c_in.astype(jnp.float32).reshape(blocks, SPAN, groups_dev, STATE)
    b_half = b_in.reshape(blocks, SPAN, groups_dev, STATE)
    c_half = c_in.reshape(blocks, SPAN, groups_dev, STATE)
    l_all = decay_log.reshape(blocks, SPAN, heads_dev)
    rows = lax.broadcasted_iota(jnp.int32, (SPAN, SPAN), 0)
    cols = lax.broadcasted_iota(jnp.int32, (SPAN, SPAN), 1)
    lower = rows >= cols
    identity = (
        jnp.ones((heads_dev,), jnp.float32),
        jnp.zeros((heads_dev, STATE, P_SIZE), jnp.float32),
    )
    blk = 0
    cumul = jnp.cumsum(l_all[blk], axis=0)
    last = cumul[-1]
    diff = cumul.T[:, :, None] - cumul.T[:, None, :]
    decay = jnp.where(lower, jnp.exp(jnp.where(lower, diff, 0.0)), 0.0)
    inner = jnp.einsum("ign,jgn->gij", c_half[blk], b_half[blk], preferred_element_type=jnp.float32)
    mixing = jnp.repeat(inner, heads_per, axis=0) * decay
    b_heads = jnp.repeat(b_all[blk], heads_per, axis=1)
    c_heads = jnp.repeat(c_all[blk], heads_per, axis=1)
    tail = jnp.exp(last[None, :] - cumul)
    local_state = jnp.einsum("jhn,jhp->hnp", b_heads * tail[:, :, None], x_all[blk], precision=HIGH)
    pairs = [(jnp.exp(last), local_state)]
    saved = [(cumul, last, decay, mixing, b_heads, c_heads, tail)]
    device_pair = identity
    pair = pairs[0]
    device_pair = combine(device_pair, pair)
    carried = forward_prefix(device_pair, identity)
    blk = 0
    cumul, last, decay, mixing, b_heads, c_heads, tail = saved[blk]
    prev_states = [carried]
    from_state = jnp.einsum("ihn,hnp->ihp", c_heads, carried, precision=HIGH)
    c_state = [from_state]
    y_val = jnp.einsum("hij,jhp->ihp", mixing, x_all[blk], precision=HIGH)
    y_val = y_val + jnp.exp(cumul)[:, :, None] * from_state + d_skip[None, :, None] * x_all[blk]
    y_flat = y_val.reshape(length, heads_dev * P_SIZE)
    z_val = gate.astype(jnp.float32)
    sig = jax.nn.sigmoid(z_val)
    gated = y_flat * z_val * sig
    scaled_out = d_out.astype(jnp.float32) * norm_weight[None, :]
    squares, products = lax.psum(
        (jnp.sum(gated * gated, axis=1), jnp.sum(scaled_out * gated, axis=1)), "heads"
    )
    channels = HEADS * P_SIZE
    inv_rms = lax.rsqrt(squares / channels + EPS)
    grad_weight_local = jnp.sum(d_out.astype(jnp.float32) * gated * inv_rms[:, None], axis=0)
    d_gated = inv_rms[:, None] * scaled_out - gated * (inv_rms**3 * products / channels)[:, None]
    d_y = d_gated * z_val * sig
    grad_gate = (d_gated * y_flat * sig * (1.0 + z_val * (1.0 - sig))).astype(jnp.bfloat16)
    dy_all = d_y.reshape(blocks, SPAN, heads_dev, P_SIZE)
    blk = 0
    cumul, last, decay, mixing, b_heads, c_heads, tail = saved[blk]
    local_back = jnp.einsum(
        "ihn,ihp->hnp", c_heads * jnp.exp(cumul)[:, :, None], dy_all[blk], precision=HIGH
    )
    back_pairs = [(pairs[blk][0], local_back)]
    device_back = identity
    blk = 0
    device_back = combine(device_back, back_pairs[blk])
    incoming = backward_suffix(device_back, identity)
    after_states = [None] * blocks
    blk = 0
    after_states[blk] = incoming
    grad_skip_local = jnp.zeros((heads_dev,), jnp.float32)
    blk = 0
    cumul, last, decay, mixing, b_heads, c_heads, tail = saved[blk]
    x_blk = x_all[blk]
    dy_blk = dy_all[blk]
    after = after_states[blk]
    before = prev_states[blk]
    dot_table = jnp.einsum("ihp,jhp->hij", dy_blk, x_blk, precision=HIGH)
    weighted = decay * dot_table
    terms = mixing * dot_table
    b_after = jnp.einsum("jhn,hnp->jhp", b_heads, after, precision=HIGH)
    grad_x_blk = jnp.einsum("hij,ihp->jhp", mixing, dy_blk, precision=HIGH)
    grad_x_blk = grad_x_blk + tail[:, :, None] * b_after + d_skip[None, :, None] * dy_blk
    grad_x_blocks = grad_x_blk.reshape(SPAN, heads_dev * P_SIZE)
    group_weighted = weighted.reshape(groups_dev, heads_per, SPAN, SPAN).sum(axis=1)
    b_far = jnp.einsum("hnp,jhp->jhn", after, x_blk * tail[:, :, None], precision=HIGH)
    grad_b_blk = jnp.einsum("gij,ign->jgn", group_weighted, c_all[blk], precision=HIGH)
    grad_b_blk = grad_b_blk + b_far.reshape(SPAN, groups_dev, heads_per, STATE).sum(axis=2)
    grad_b_blocks = grad_b_blk.reshape(SPAN, groups_dev * STATE)
    c_far = jnp.einsum("hnp,ihp->ihn", before, dy_blk * jnp.exp(cumul)[:, :, None], precision=HIGH)
    grad_c_blk = jnp.einsum("gij,jgn->ign", group_weighted, b_all[blk], precision=HIGH)
    grad_c_blk = grad_c_blk + c_far.reshape(SPAN, groups_dev, heads_per, STATE).sum(axis=2)
    grad_c_blocks = grad_c_blk.reshape(SPAN, groups_dev * STATE)
    early = jnp.sum(c_state[blk] * dy_blk, axis=2)
    late = jnp.sum(b_after * x_blk, axis=2)
    start_term = jnp.sum(before * after, axis=(1, 2))
    d_cumul = jnp.sum(terms, axis=2).T - jnp.sum(terms, axis=1).T
    d_cumul = d_cumul + jnp.exp(cumul) * early - tail * late
    end_term = jnp.exp(last) * start_term + jnp.sum(tail * late, axis=0)
    d_cumul = d_cumul.at[-1].add(end_term)
    gradient_mixing_blocks = jnp.cumsum(d_cumul[::-1], axis=0)[::-1]
    grad_skip_local = grad_skip_local + jnp.sum(dy_blk * x_blk, axis=(0, 2))
    grad_weight, grad_skip = lax.psum((grad_weight_local, grad_skip_local), ("outer", "inner"))
    grad_x = grad_x_blocks.astype(jnp.bfloat16)
    return (
        grad_x,
        grad_b_blocks,
        grad_c_blocks,
        gradient_mixing_blocks,
        grad_skip,
        grad_gate,
        grad_weight,
    )


def solution(mesh):
    in_specs = (
        P(("outer", "inner"), "heads"),
        P(("outer", "inner"), "heads"),
        P(("outer", "inner"), "heads"),
        P(("outer", "inner"), "heads"),
        P("heads"),
        P(("outer", "inner"), "heads"),
        P("heads"),
        P(("outer", "inner"), "heads"),
    )
    out_specs = (
        P(("outer", "inner"), "heads"),
        P(("outer", "inner"), "heads"),
        P(("outer", "inner"), "heads"),
        P(("outer", "inner"), "heads"),
        P("heads"),
        P(("outer", "inner"), "heads"),
        P("heads"),
    )
    return jax.shard_map(
        on_device, mesh=mesh, in_specs=in_specs, out_specs=out_specs, check_vma=False
    )
```

profile of v0, /device:TPU:32, one launch (start us, length us, event | category | flops | bytes accessed | tf_op | source)
XLA Modules:
  0.0 485.0 jit_solution(6849077943121143297)
XLA Ops:
  12.4 2.0 fusion.45
  14.4 2.2 copy.96
  16.7 35.9 %all-gather.2 = f32[32,1,16]{2,1,0:T(1,128)} all-gather(f32[1,1,16]{2,1,0:T(1,128)S(1)} %bitcast.159), channel_id=1, replica_groups=mesh['outer'=8,'inner'=4,'heads'=8] {'outer','inner'}, dimensions={0}, use_global_device_ids=true | all-gather | bytes 2112 | tf_op jit(solution)/shard_map/all_gather | solution.py:20
  54.2 40.5 %all-gather.6.cloned.1.call-done = f32[512,128,64]{1,2,0:T(8,128)} async-done(((f32[16,128,64]{1,2,0:T(8,128)}), f32[512,128,64]{1,2,0:T(8,128)}) %all-gather.6.cloned.1.call-update) | async-done | bytes 16777232 | tf_op jit(solution)/shard_map/all_gather | solution.py:20
  94.7 2.2 convolution_bitcast_fusion.1
  97.0 6.0 %fusion.31 = f32[256,16,64]{0,2,1:T(8,128)} fusion(bf16[256,16,64]{0,2,1:T(8,128)(2,1)S(1)} %bitcast.152, f32[16,256]{1,0:T(8,128)} %get-tuple-element.271, f32[256,256]{1,0:T(8,128)} %fusion.85, pred[256,256]{1,0:T(8,128)(4,1)} %iota_compare_fusion, f32[256,16,64]{0,2,1:T(8,128)} %bitcast.148, f32[256,16,64]{0,2,1:T(8,128)S(1)} %convolution_bitcast_fusion.1, ...), kind=kOutput, calls=%fused_computation.37 | convolution fusion | flops 810549248 | bytes 4030528 | tf_op jit(solution)/shard_map/hij,jhp->ihp/dot_general | solution.py:84
  105.6 16.7 %psum.28 = f32[256]{0:T(256)} all-reduce(f32[256]{0:T(256)} %multiply_reduce_fusion.5), channel_id=1, replica_groups=mesh['outer'=8,'inner'=4,'heads'=8] {'heads'}, use_global_device_ids=true, to_apply=%region_5.6 | all-reduce | flops 256 | bytes 2048 | tf_op jit(solution)/shard_map/psum | solution.py:91
  123.6 2.2 fusion.58
  125.8 16.7 %psum.29 = f32[256]{0:T(256)} all-reduce(f32[256]{0:T(256)} %get-tuple-element.238), channel_id=1, replica_groups=mesh['outer'=8,'inner'=4,'heads'=8] {'heads'}, use_global_device_ids=true, to_apply=%region_7.8 | all-reduce | flops 256 | bytes 2048 | tf_op jit(solution)/shard_map/psum | solution.py:91
  143.2 3.6 multiply_reduce_fusion.1
  148.5 3.2 fusion.48
  151.9 170.4 %all-reduce = (f32[16]{0:T(128)}, f32[1024]{0:T(1024)}) all-reduce(f32[16]{0:T(128)S(1)} %reduce_sum.137, f32[1024]{0:T(1024)S(1)} %copy-done.23), channel_id=1, replica_groups=mesh['outer'=8,'inner'=4,'heads'=8] {'outer','inner'}, use_global_device_ids=true, to_apply=%region_21.22 | all-reduce | flops 1040 | bytes 8320 | tf_op jit(solution)/shard_map/psum | solution.py:146
  322.3 4.7 fusion.6
  327.9 4.1 fusion.54
  332.1 130.5 %while.28 = (s32[]{:T(128)}, f32[16,128,64]{2,1,0:T(8,128)S(1)}, s32[]{:T(128)}, f32[32,16]{1,0:T(8,128)}, f32[32,16,128,64]{2,3,1,0:T(8,128)}, /*index=5*/s32[]{:T(128)}, s32[]{:T(128)}, s32[]{:T(128)}, s32[]{:T(128)}) while((s32[]{:T(128)}, f32[16,128,64]{2,1,0:T(8,128)S(1)}, s32[]{:T(128)}, f32[32,16]{1,0:T(8,128)}, ...), condition=%wide.region_9.10_spmd, body=%wide.region_8.9_spmd.sunk | while | flops 262150 | bytes 3670363 | solution.py:29
  345.5 1.9 constant_dynamic-slice_fusion.5
  362.3 1.9 constant_dynamic-slice_fusion.5
  417.0 1.9 constant_dynamic-slice_fusion.5
  442.2 1.9 constant_dynamic-slice_fusion.5
  446.4 1.9 constant_dynamic-slice_fusion.5
  450.6 1.9 constant_dynamic-slice_fusion.5
  463.0 3.6 multiply_reduce_fusion.3
  466.6 4.1 fusion.52
  470.9 3.9 fusion.40
  (237 shorter events, 135.7 us)
Async XLA Ops:
  7.2 46.1 %copy-start.8 = (bf16[256,128]{1,0:T(8,128)(2,1)S(1)}, bf16[256,128]{1,0:T(8,128)(2,1)}, u32[]{:S(2)}) copy-start(bf16[256,128]{1,0:T(8,128)(2,1)} %param.15) | copy-start | bytes 196612
  7.2 9.5 %copy-start.9 = (bf16[256,128]{1,0:T(8,128)(2,1)S(1)}, bf16[256,128]{1,0:T(8,128)(2,1)}, u32[]{:S(2)}) copy-start(bf16[256,128]{1,0:T(8,128)(2,1)} %param.16) | copy-start | bytes 196612
  7.2 87.4 %all-gather.6.cloned.1.call-start = ((), (), s32[]{:S(2)}) async-start(), calls=%async_computation | async-start | bytes 17301504 | tf_op jit(solution)/shard_map/all_gather | solution.py:20
  8.5 86.2 %copy-start.12 = (f32[16,2,128]{2,0,1:T(8,128)}, f32[16,2,128]{2,0,1:T(8,128)S(1)}, u32[]{:S(2)}) copy-start(f32[16,2,128]{2,0,1:T(8,128)S(1)} %reduce-window.14) | copy-start | bytes 49156
  8.7 8.0 %copy-start.24 = (f32[16,2]{0,1:T(2,128)}, f32[16,2]{0,1:T(2,128)S(1)}, u32[]{:S(2)}) copy-start(f32[16,2]{0,1:T(2,128)S(1)} %slice.33) | copy-start | bytes 388
  9.4 85.3 %copy-start.19 = (f32[256,16]{0,1:T(8,128)}, f32[256,16]{0,1:T(8,128)S(1)}, u32[]{:S(2)}) copy-start(f32[256,16]{0,1:T(8,128)S(1)} %get-tuple-element.270) | copy-start | bytes 49156
  9.5 7.1 %copy-start.32 = (f32[16]{0:T(128)}, f32[16]{0:T(128)S(1)}, u32[]{:S(2)}) copy-start(f32[16]{0:T(128)S(1)} %get-tuple-element.239) | copy-start | bytes 196
  9.6 7.1 %copy-start.34 = (f32[16]{0:T(128)}, f32[16]{0:T(128)S(1)}, u32[]{:S(2)}) copy-start(f32[16]{0:T(128)S(1)} %exponential_multiply_fusion) | copy-start | bytes 196
  10.3 6.4 %copy-start.17 = (f32[256,16]{0,1:T(8,128)}, f32[256,16]{0,1:T(8,128)S(1)}, u32[]{:S(2)}) copy-start(f32[256,16]{0,1:T(8,128)S(1)} %get-tuple-element.269) | copy-start | bytes 49156
  12.4 84.6 %copy-start.10 = (bf16[256,1024]{0,1:T(8,128)(2,1)}, bf16[256,1024]{0,1:T(8,128)(2,1)S(1)}, u32[]{:S(2)}) copy-start(bf16[256,1024]{0,1:T(8,128)(2,1)S(1)} %copy.93) | copy-start | bytes 1572868
  14.4 317.7 %all-gather.8.cloned.1.call-start = ((), (), s32[]{:S(2)}) async-start(), calls=%async_computation.1 | async-start | bytes 17301504 | tf_op jit(solution)/shard_map/all_gather | solution.py:20
  97.0 6.0 %copy-start.6 = (f32[256,16,64]{0,2,1:T(8,128)}, f32[256,16,64]{0,2,1:T(8,128)S(1)}, u32[]{:S(2)}) copy-start(f32[256,16,64]{0,2,1:T(8,128)S(1)} %convolution_bitcast_fusion.1) | copy-start | bytes 3145732
  97.0 7.6 %copy-start.5 = (bf16[256,1024]{1,0:T(8,128)(2,1)S(1)}, bf16[256,1024]{1,0:T(8,128)(2,1)}, u32[]{:S(2)}) copy-start(bf16[256,1024]{1,0:T(8,128)(2,1)} %param.19) | copy-start | bytes 1572868
  103.0 40.2 %copy-start.4 = (bf16[256,1024]{1,0:T(8,128)(2,1)S(1)}, bf16[256,1024]{1,0:T(8,128)(2,1)}, u32[]{:S(2)}) copy-start(bf16[256,1024]{1,0:T(8,128)(2,1)} %param.14) | copy-start | bytes 1572868
  146.8 175.5 %copy-start.11 = (bf16[256,1024]{0,1:T(8,128)(2,1)S(1)}, bf16[256,1024]{0,1:T(8,128)(2,1)}, u32[]{:S(2)}) copy-start(bf16[256,1024]{0,1:T(8,128)(2,1)} %copy-done.10) | copy-start | bytes 1572868
  146.8 175.5 %copy-start.14 = (f32[256,256]{1,0:T(8,128)S(1)}, f32[256,256]{1,0:T(8,128)}, u32[]{:S(2)}) copy-start(f32[256,256]{1,0:T(8,128)} %fusion.85) | copy-start | bytes 786436
  146.8 175.5 %copy-start.21 = (pred[256,256]{1,0:T(8,128)(4,1)S(1)}, pred[256,256]{1,0:T(8,128)(4,1)}, u32[]{:S(2)}) copy-start(pred[256,256]{1,0:T(8,128)(4,1)} %iota_compare_fusion) | copy-start | bytes 196612
  146.8 175.5 %copy-start.26 = (f32[16,256]{1,0:T(8,128)S(1)}, f32[16,256]{1,0:T(8,128)}, u32[]{:S(2)}) copy-start(f32[16,256]{1,0:T(8,128)} %get-tuple-element.271) | copy-start | bytes 49156
  148.4 179.5 %copy-start.1 = (f32[256,1024]{0,1:T(8,128)}, f32[256,1024]{0,1:T(8,128)S(1)}, u32[]{:S(2)}) copy-start(f32[256,1024]{0,1:T(8,128)S(1)} %copy.98) | copy-start | bytes 3145732
  462.7 8.1 %copy-start.2 = (f32[256,1024]{0,1:T(8,128)S(1)}, f32[256,1024]{0,1:T(8,128)}, u32[]{:S(2)}) copy-start(f32[256,1024]{0,1:T(8,128)} %copy-done.1) | copy-start | bytes 3145732
  462.7 8.1 %copy-start.15 = (f32[256,256]{1,0:T(8,128)S(1)}, f32[256,256]{1,0:T(8,128)}, u32[]{:S(2)}) copy-start(f32[256,256]{1,0:T(8,128)} %fusion.85) | copy-start | bytes 786436
  462.7 8.0 %copy-start.22 = (pred[256,256]{1,0:T(8,128)(4,1)S(1)}, pred[256,256]{1,0:T(8,128)(4,1)}, u32[]{:S(2)}) copy-start(pred[256,256]{1,0:T(8,128)(4,1)} %iota_compare_fusion) | copy-start | bytes 196612
  462.7 8.0 %copy-start.27 = (f32[16,256]{1,0:T(8,128)S(1)}, f32[16,256]{1,0:T(8,128)}, u32[]{:S(2)}) copy-start(f32[16,256]{1,0:T(8,128)} %get-tuple-element.271) | copy-start | bytes 49156
  462.8 8.0 %copy-start.35 = (f32[16]{0:T(128)S(1)}, f32[16]{0:T(128)}, u32[]{:S(2)}) copy-start(f32[16]{0:T(128)} %param.18) | copy-start | bytes 196
  (14 other events, 60.6 us)
Sparse Core Ops, SparseCore 0:
  14.5 80.0 all-gather.5
  151.8 177.5 all-gather.7
where the time goes:
time: 490 us; the launch traced here: 485 us
  blocking collectives  240 us (49%)
  local copies, waits for them, and re-layouts  133 us (27%)
  waiting for transfers between devices  40.5 us (8%)
  matrix products  35.4 us (7%)
  other arithmetic  19.9 us (4%)
  between operations  14.5 us (3%)
    psum x1, blocking collectives, on_device(): lax.psum((grad_weight_local, grad_skip_local), ('outer', 'inner'))  170 us
    dynamic_slice x62, local copies, waits for them, and re-layouts, one(): lax.dynamic_index_in_dim(a, source, 0, False)  101 us
    all_gather x2, waiting for transfers between devices, entering(): gathered = jax.tree.map(lambda a: lax.all_gather(a, axis), part)  40.5 us
    all_gather x1, blocking collectives, entering(): gathered = jax.tree.map(lambda a: lax.all_gather(a, axis), part)  35.9 us
    psum x2, blocking collectives, on_device(): lax.psum((jnp.sum(gated * gated, axis=1), jnp.sum(scaled_out * gated, axi...  33.4 us
    mul x31, local copies, waits for them, and re-layouts, combine(): later[0][:, None, None] * earlier[1] + later[1]  21.4 us
  transfers between devices with their start and end apart: 2, of which 1 were waited for; matrix products, arithmetic and copies ran while one was open for 3% of the time, Pallas kernels for 0%

commit v1 on v0

v1 whole, which is shorter than its diff:
```python
import jax
import jax.numpy as jnp
from jax import lax
from jax.experimental import pallas as pl
from jax.experimental.pallas import tpu as pltpu
from jax.sharding import PartitionSpec as P

P_SIZE = 64
EPS = 1e-05
F32 = jnp.float32
BF16 = jnp.bfloat16
CHUNKS = ("outer", "inner")
VMEM = pl.BlockSpec(memory_space=pltpu.VMEM)
HALF = 128


def mm(a, b, ca=1, cb=0):
    return lax.dot_general(a, b, (((ca,), (cb,)), ((), ())), preferred_element_type=F32)


def split2(a):
    hi = a.astype(BF16)
    return hi, (a - hi.astype(F32)).astype(BF16)


def split3(a):
    hi = a.astype(BF16)
    rest = a - hi.astype(F32)
    mid = rest.astype(BF16)
    return hi, mid, (rest - mid.astype(F32)).astype(BF16)


def mm2(a, b, ca=1, cb=0):
    hi, lo = split2(a)
    return mm(hi, b, ca, cb) + mm(lo, b, ca, cb)


def iota(shape, dim):
    return lax.broadcasted_iota(jnp.int32, shape, dim)


def head_map(heads, width):
    return jnp.where(iota((heads, width), 1) // P_SIZE == iota((heads, width), 0), 1.0, 0.0).astype(BF16)


def expand(a, spread):
    hi, mid, lo = split3(a)
    return mm(hi, spread) + mm(mid, spread) + mm(lo, spread)


def segment(a, spread):
    hi, lo = split2(a)
    return mm(hi, spread, 1, 1) + mm(lo, spread, 1, 1)


def triangle(n, keep):
    return jnp.where(keep(iota((n, n), 0), iota((n, n), 1)), 1.0, 0.0).astype(BF16)


def mm_tri(tri, a):
    hi, mid, lo = split3(a)
    return mm(tri, hi) + mm(tri, mid) + mm(tri, lo)


def store_state(out_ref, state):
    for r in range(16):
        for f in range(2):
            out_ref[2 * r + f, :, 0:512] = state[8 * r : 8 * r + 8, 512 * f : 512 * f + 512]


def load_state(ref):
    rows = []
    for r in range(16):
        rows.append(jnp.concatenate([ref[2 * r, :, 0:512], ref[2 * r + 1, :, 0:512]], axis=1))
    return jnp.concatenate(rows, axis=0)


def start_kernel(l_ref, x_ref, b_ref, pay_ref, cum_ref, tail_ref):
    length, heads = l_ref.shape
    width = x_ref.shape[1]
    spread = head_map(heads, width)
    cum = mm_tri(triangle(length, lambda i, j: i >= j), l_ref[...])
    cum_ref[...] = cum
    last = cum[length - 1 : length, :]
    tail = expand(jnp.exp(last - cum), spread)
    tail_ref[...] = tail
    hi, lo = split2(x_ref[...].astype(F32) * tail)
    b_val = b_ref[...]
    state = mm(b_val, hi, 0, 0) + mm(b_val, lo, 0, 0)
    store_state(pay_ref, state)
    whole = expand(jnp.broadcast_to(jnp.exp(last), (8, heads)), spread)[0:1, :]
    for f in range(2):
        rows = [whole[:, 512 * f + HALF * j : 512 * f + HALF * (j + 1)] for j in range(4)]
        tile = jnp.concatenate(rows + [jnp.zeros((4, HALF), F32)], axis=0)
        for r in range(16):
            pay_ref[2 * r + f, :, 512:640] = tile


def local_kernel(cum_ref, x_ref, b_ref, c_ref, z_ref, d_ref, yn_ref, base_ref, silu_ref, esilu_ref, ecum_ref):
    length, heads = cum_ref.shape
    width = x_ref.shape[1]
    spread = head_map(heads, width)
    cum = cum_ref[...]
    cum_t = cum.T
    ecum = expand(jnp.exp(cum), spread)
    ecum_ref[...] = ecum
    z_val = z_ref[...].astype(F32)
    silu = z_val * (1.0 / (1.0 + jnp.exp(-z_val)))
    silu_ref[...] = silu
    esilu_ref[...] = ecum * silu
    skip = expand(jnp.broadcast_to(d_ref[...], (8, heads)), spread)[0:1, :]
    inner = mm(c_ref[...], b_ref[...], 1, 1)
    top, left, right = inner[:HALF, :HALF], inner[HALF:, :HALF], inner[HALF:, HALF:]
    lower = iota((HALF, HALF), 0) >= iota((HALF, HALF), 1)
    first = iota((length, HALF), 1) < P_SIZE
    for q in range(width // HALF):
        cols = slice(HALF * q, HALF * (q + 1))
        x_pair = x_ref[:, cols]
        parts = []
        for h in (2 * q, 2 * q + 1):
            col, row = cum[:, h : h + 1], cum_t[h : h + 1, :]
            up = jnp.where(lower, jnp.exp(col[:HALF] - row[:, :HALF]), 0.0) * top
            dl = jnp.exp(col[HALF:] - row[:, :HALF]) * left
            dr = jnp.where(lower, jnp.exp(col[HALF:] - row[:, HALF:]), 0.0) * right
            down = jnp.concatenate([dl, dr], axis=1)
            parts.append(jnp.concatenate([mm2(up, x_pair[:HALF]), mm2(down, x_pair)], axis=0))
        yn = jnp.where(first, parts[0], parts[1])
        yn_ref[:, cols] = yn
        base_ref[:, cols] = (yn + skip[:, cols] * x_pair.astype(F32)) * silu_ref[:, cols]


def prefix_kernel(in_ref, out_ref, dec_ref):
    count = in_ref.shape[0]
    state = jnp.zeros((8, 512), F32)
    for p in range(count):
        out_ref[p] = state
        if p < count - 1:
            tile = in_ref[p, :, 512:640]
            decay = jnp.concatenate([tile[j : j + 1, :] for j in range(4)], axis=1)
            state = decay * state + in_ref[p, :, 0:512]
    dec_ref[...] = in_ref[:, :, 512:640]


def suffix_kernel(in_ref, dec_ref, skip_ref, out_ref, weight_ref):
    count = in_ref.shape[0]
    state = jnp.zeros((8, 512), F32)
    weight = jnp.zeros((8, HALF), F32)
    for p in range(count - 1, -1, -1):
        out_ref[p, :, 0:512] = state
        out_ref[p, :, 512:640] = skip_ref[...]
        weight = weight + in_ref[p, :, 512:640]
        if p > 0:
            tile = dec_ref[p]
            decay = jnp.concatenate([tile[j : j + 1, :] for j in range(4)], axis=1)
            state = decay * state + in_ref[p, :, 0:512]
    weight_ref[...] = weight


def gate_kernel(s_ref, c_ref, base_ref, esilu_ref, dout_ref, w_ref, gated_ref, cs_ref, sums_ref):
    hi, lo = split2(load_state(s_ref))
    c_val = c_ref[...]
    length, width = base_ref.shape
    squares = jnp.zeros((length, HALF), F32)
    products = jnp.zeros((length, HALF), F32)
    for q in range(width // 256):
        big = slice(256 * q, 256 * (q + 1))
        c_state = mm(c_val, hi[:, big]) + mm(c_val, lo[:, big])
        cs_ref[:, big] = c_state
        gated = base_ref[:, big] + esilu_ref[:, big] * c_state
        gated_ref[:, big] = gated
        sq = gated * gated
        pr = dout_ref[:, big].astype(F32) * w_ref[:, big] * gated
        squares = squares + sq[:, :HALF] + sq[:, HALF:]
        products = products + pr[:, :HALF] + pr[:, HALF:]
    sq_row = jnp.sum(squares.T, axis=0, keepdims=True)
    pr_row = jnp.sum(products.T, axis=0, keepdims=True)
    tile = jnp.concatenate([sq_row, pr_row, jnp.zeros((6, length), F32)], axis=0)
    for i in range(sums_ref.shape[0]):
        sums_ref[i] = tile


def back_kernel(channels, sums_ref, gated_ref, silu_ref, ecum_ref, dout_ref, w_ref, x_ref, c_ref, pay_ref, scal_ref, skip_ref):
    length, width = gated_ref.shape
    total = sums_ref[0]
    for i in range(1, sums_ref.shape[0]):
        total = total + sums_ref[i]
    squares, products = total[0:1, :], total[1:2, :]
    inv = lax.rsqrt(squares / channels + EPS)
    fall = inv * inv * inv * products / channels
    both = jnp.concatenate([inv, fall, jnp.zeros((HALF - 2, length), F32)], axis=0).T
    scal_ref[...] = both
    inv_col, fall_col = both[:, 0:1], both[:, 1:2]
    c_val = c_ref[...]
    weights, skips = [], []
    for q in range(width // 256):
        big = slice(256 * q, 256 * (q + 1))
        gated = gated_ref[:, big]
        d_inv = dout_ref[:, big].astype(F32) * inv_col
        dy = (d_inv * w_ref[:, big] - gated * fall_col) * silu_ref[:, big]
        weights.append(jnp.sum(d_inv * gated, axis=0, keepdims=True))
        skips.append(jnp.sum(dy * x_ref[:, big].astype(F32), axis=0, keepdims=True))
        hi, lo = split2(dy * ecum_ref[:, big])
        back = mm(c_val, hi, 0, 0) + mm(c_val, lo, 0, 0)
        f, off = q // 2, 256 * (q % 2)
        for r in range(16):
            pay_ref[2 * r + f, :, off : off + 256] = back[8 * r : 8 * r + 8, :]
    weight = jnp.concatenate(weights, axis=1)
    tile = jnp.concatenate([weight[:, HALF * j : HALF * (j + 1)] for j in range(8)], axis=0)
    for i in range(pay_ref.shape[0]):
        pay_ref[i, :, 512:640] = tile
    heads = width // P_SIZE
    skip = jnp.broadcast_to(jnp.concatenate(skips, axis=1), (8, width))
    spread = head_map(HALF, width)
    hi, mid, lo = split3(skip)
    skip_ref[...] = mm(hi, spread, 1, 1) + mm(mid, spread, 1, 1) + mm(lo, spread, 1, 1)


def grads_kernel(
    cum_ref, scal_ref, gated_ref, silu_ref, ecum_ref, dout_ref, w_ref, x_ref, z_ref, b_ref, c_ref, d_ref, yn_ref, cs_ref, s_ref,
    gx_ref, gz_ref, gb_ref, gc_ref, gl_ref, dy_ref, dot_ref,
):
    length, heads = cum_ref.shape
    width = x_ref.shape[1]
    spread = head_map(heads, width)
    cum = cum_ref[...]
    cum_t = cum.T
    inv_col, fall_col = scal_ref[:, 0:1], scal_ref[:, 1:2]
    skip = expand(jnp.broadcast_to(d_ref[...], (8, heads)), spread)[0:1, :]
    inner_t = mm(b_ref[...], c_ref[...], 1, 1)
    left, right, low = inner_t[:HALF, :HALF], inner_t[:HALF, HALF:], inner_t[HALF:, HALF:]
    upper = iota((HALF, HALF), 0) <= iota((HALF, HALF), 1)
    first = iota((length, HALF), 1) < P_SIZE
    w_left = jnp.zeros((HALF, HALF), F32)
    w_right = jnp.zeros((HALF, HALF), F32)
    w_low = jnp.zeros((HALF, HALF), F32)
    for q in range(width // HALF):
        cols = slice(HALF * q, HALF * (q + 1))
        gated, silu = gated_ref[:, cols], silu_ref[:, cols]
        d_gated = inv_col * (dout_ref[:, cols].astype(F32) * w_ref[:, cols]) - gated * fall_col
        dy = d_gated * silu
        dy_ref[:, cols] = dy * ecum_ref[:, cols]
        x_pair = x_ref[:, cols]
        x_val = x_pair.astype(F32)
        z_val = z_ref[:, cols].astype(F32)
        sig = 1.0 / (1.0 + jnp.exp(-z_val))
        y_near = yn_ref[:, cols] + ecum_ref[:, cols] * cs_ref[:, cols]
        y_val = y_near + skip[:, cols] * x_val
        gz_ref[:, cols] = (d_gated * y_val * sig * (1.0 + z_val * (1.0 - sig))).astype(BF16)
        hi, lo = split2(dy)
        parts = []
        for k in range(2):
            h = 2 * q + k
            col, row = cum[:, h : h + 1], cum_t[h : h + 1, :]
            x_one = jnp.where(first if k == 0 else ~first, x_val, 0.0).astype(BF16)
            dec_left = jnp.where(upper, jnp.exp(row[:, :HALF] - col[:HALF]), 0.0)
            dec_right = jnp.exp(row[:, HALF:] - col[:HALF])
            dec_low = jnp.where(upper, jnp.exp(row[:, HALF:] - col[HALF:]), 0.0)
            dot_up = mm(x_one[:HALF], hi, 1, 1) + mm(x_one[:HALF], lo, 1, 1)
            dot_low = mm(x_one[HALF:], hi[HALF:], 1, 1) + mm(x_one[HALF:], lo[HALF:], 1, 1)
            w_left = w_left + dec_left * dot_up[:, :HALF]
            w_right = w_right + dec_right * dot_up[:, HALF:]
            w_low = w_low + dec_low * dot_low
            mix_up = jnp.concatenate([dec_left * left, dec_right * right], axis=1)
            mix_low = dec_low * low
            up_hi, up_lo = split2(mix_up)
            low_hi, low_lo = split2(mix_low)
            g_up = mm(up_hi, hi) + mm(up_hi, lo) + mm(up_lo, hi)
            g_low = mm(low_hi, hi[HALF:]) + mm(low_hi, lo[HALF:]) + mm(low_lo, hi[HALF:])
            parts.append(jnp.concatenate([g_up, g_low], axis=0))
        g_near = jnp.where(first, parts[0], parts[1])
        gx_ref[:, cols] = g_near + skip[:, cols] * dy
        dot_ref[:, cols] = dy * y_near - x_val * g_near
    gl_ref[...] = mm_tri(triangle(length, lambda i, j: i <= j), segment(dot_ref[...], spread))
    e_hi, e_lo = split2(dy_ref[...])
    s_hi, s_lo = split2(load_state(s_ref))
    far = mm(e_hi, s_hi, 1, 1) + mm(e_hi, s_lo, 1, 1) + mm(e_lo, s_hi, 1, 1)
    w_up = jnp.concatenate([w_left, w_right], axis=1)
    b_val, c_val = b_ref[...], c_ref[...]
    gb_ref[:HALF, :] = mm2(w_up, c_val)
    gb_ref[HALF:, :] = mm2(w_low, c_val[HALF:])
    low_part = mm2(w_right.T, b_val[:HALF]) + mm2(w_low.T, b_val[HALF:])
    gc_ref[...] = far + jnp.concatenate([mm2(w_left.T, b_val[:HALF]), low_part], axis=0)


def final_kernel(a_ref, s_ref, cum_ref, tail_ref, x_ref, b_ref, gx_ref, gb_ref, gl_ref, ox_ref, ob_ref, ol_ref, skip_ref):
    length, heads = cum_ref.shape
    width = x_ref.shape[1]
    spread = head_map(heads, width)
    after = load_state(a_ref)
    a_hi, a_lo = split2(after)
    b_val = b_ref[...]
    tail = tail_ref[...]
    b_after = (mm(b_val, a_hi) + mm(b_val, a_lo)) * tail
    x_val = x_ref[...].astype(F32)
    ox_ref[...] = (gx_ref[...] + b_after).astype(BF16)
    late = segment(x_val * b_after, spread)
    x_hi, x_lo = split2(x_val * tail)
    ob_ref[...] = gb_ref[...] + (mm(x_hi, a_hi, 1, 1) + mm(x_hi, a_lo, 1, 1) + mm(x_lo, a_hi, 1, 1))
    start = jnp.broadcast_to(jnp.sum(load_state(s_ref) * after, axis=0, keepdims=True), (8, width))
    hi, mid, lo = split3(start)
    start = (mm(hi, spread, 1, 1) + mm(mid, spread, 1, 1) + mm(lo, spread, 1, 1))[0:1, :]
    whole = jnp.exp(cum_ref[length - 1 : length, :])
    ol_ref[...] = gl_ref[...] + mm_tri(triangle(length, lambda i, j: i > j), late) + whole * start
    total = a_ref[0, :, 512:640]
    for i in range(1, a_ref.shape[0]):
        total = total + a_ref[i, :, 512:640]
    skip_ref[...] = total


def call(kernel, name, outs, *args, flops=0, scratch=()):
    nbytes = sum(a.size * a.dtype.itemsize for a in (*args, *outs))
    return pl.pallas_call(
        kernel,
        name=name,
        out_shape=outs,
        in_specs=[VMEM] * len(args),
        out_specs=[VMEM] * len(outs),
        scratch_shapes=list(scratch),
        compiler_params=pltpu.CompilerParams(vmem_limit_bytes=48 * 1024 * 1024),
        cost_estimate=pl.CostEstimate(flops=flops, bytes_accessed=nbytes, transcendentals=0),
    )(*args)


def on_device(x_in, b_in, c_in, decay_log, d_skip, gate, norm_weight, d_out):
    length, heads = decay_log.shape
    width = x_in.shape[1]
    chunks = lax.axis_size(CHUNKS)
    groups = lax.axis_size("heads")
    shape = jax.ShapeDtypeStruct
    wide = shape((length, width), F32)
    small = shape((length, heads), F32)
    weight = norm_weight.reshape(1, width)
    d_row = d_skip.reshape(1, heads)

    pay, cum, tail = call(
        start_kernel, "start", [shape((chunks, 8, 640), F32), small, wide], decay_log, x_in, b_in, flops=10**9
    )
    got = lax.all_to_all(pay, CHUNKS, 0, 0)
    y_near, base, silu, esilu, ecum = call(
        local_kernel, "local", [wide] * 5, cum, x_in, b_in, c_in, gate, d_row, flops=8 * 10**9
    )
    spread, decays = call(
        prefix_kernel, "prefix", [shape((chunks, 8, 512), F32), shape((chunks, 8, HALF), F32)], got
    )
    before = lax.all_to_all(spread, CHUNKS, 0, 0)
    gated, c_state, sums = call(
        gate_kernel, "gated", [wide, wide, shape((groups, 8, length), F32)],
        before, c_in, base, esilu, d_out, weight, flops=10**9,
    )
    sums = lax.all_to_all(sums, "heads", 0, 0)

    def back(*refs):
        back_kernel(float(width * groups), *refs)

    pay, scalars, skip = call(
        back, "back", [shape((chunks, 8, 640), F32), shape((length, HALF), F32), shape((8, HALF), F32)],
        sums, gated, silu, ecum, d_out, weight, x_in, c_in, flops=10**9,
    )
    got = lax.all_to_all(pay, CHUNKS, 0, 0)
    gx, grad_gate, gb, grad_c, gl = call(
        grads_kernel, "grads",
        [wide, shape((length, width), BF16), shape(b_in.shape, F32), shape(c_in.shape, F32), small],
        cum, scalars, gated, silu, ecum, d_out, weight, x_in, gate, b_in, c_in, d_row, y_near, c_state, before,
        flops=16 * 10**9, scratch=[pltpu.VMEM((length, width), F32)] * 2,
    )
    spread, grad_weight = call(
        suffix_kernel, "suffix", [shape((chunks, 8, 640), F32), shape((8, HALF), F32)], got, decays, skip
    )
    after = lax.all_to_all(spread, CHUNKS, 0, 0)
    grad_x, grad_b, grad_decay, grad_skip = call(
        final_kernel, "final",
        [shape((length, width), BF16), shape(b_in.shape, F32), small, shape((8, HALF), F32)],
        after, before, cum, tail, x_in, b_in, gx, gb, gl, flops=2 * 10**9,
    )
    return (
        grad_x,
        grad_b,
        grad_c,
        grad_decay,
        grad_skip[0, :heads],
        grad_gate,
        grad_weight.reshape(width),
    )


def solution(mesh):
    tokens = P(CHUNKS, "heads")
    in_specs = (tokens, tokens, tokens, tokens, P("heads"), tokens, P("heads"), tokens)
    out_specs = (tokens, tokens, tokens, tokens, P("heads"), tokens, P("heads"))
    return jax.shard_map(on_device, mesh=mesh, in_specs=in_specs, out_specs=out_specs, check_vma=False)
```

time: 490 us -> 112 us (0.23)
  the two profiles are of different devices: /device:TPU:32 before, /device:TPU:1 now
where the time goes in v1:
time: 112 us; the launch traced here: 111 us
  blocking collectives  53.8 us (48%)
  local copies, waits for them, and re-layouts  25.5 us (23%)
  Pallas kernels  17.2 us (15%)
  starting transfers between devices  9.49 us (8%)
  waiting for transfers between devices  4.45 us (4%)
    all_to_all x2, blocking collectives, on_device(): got = lax.all_to_all(pay, CHUNKS, 0, 0)  38.6 us
    unnamed x68, local copies, waits for them, and re-layouts  25 us
    pallas_call x8, Pallas kernels, call(): pl.pallas_call(kernel, name=name, out_shape=outs, in_specs=[VMEM] * len(a...  17.2 us
    all_to_all x1, blocking collectives, on_device(): sums = lax.all_to_all(sums, 'heads', 0, 0)  15.2 us
    all_to_all x1, starting transfers between devices, on_device(): before = lax.all_to_all(spread, CHUNKS, 0, 0)  4.8 us
    all_to_all x1, starting transfers between devices, on_device(): after = lax.all_to_all(spread, CHUNKS, 0, 0)  4.69 us
    all_to_all x1, waiting for transfers between devices, on_device(): before = lax.all_to_all(spread, CHUNKS, 0, 0)  4.45 us
  transfers between devices with their start and end apart: 2, of which 1 were waited for; matrix products, arithmetic and copies ran while one was open for 0% of the time, Pallas kernels for 10%

profile of v1, /device:TPU:1, one launch (start us, length us, event | category | flops | bytes accessed | tf_op | source)
XLA Modules:
  0.0 111.2 jit_solution(4131739244491931055)
XLA Ops:
  1.5 1.0 copy-done.2
  2.5 1.1 %start.1 = (f32[32,8,640]{2,1,0:T(8,128)S(1)}, f32[256,16]{1,0:T(8,128)S(1)}, f32[256,1024]{1,0:T(8,128)S(1)}) custom-call(f32[256,16]{1,0:T(8,128)S(1)} %copy.15.l_ref, bf16[256,1024]{1,0:T(8,128)(2,1)S(1)} %copy-done.2, bf16[256,128]{1,0:T(8,128)(2,1)S(1)} %copy-done.14), custom_call_target="tpu_custom_call" | custom-call | flops 1000000000 | bytes 2326528 | tf_op jit(solution)/shard_map/start/pallas_call | solution.py:312
  4.7 20.6 %all_to_all.25.in_ref = f32[32,8,640]{2,1,0:T(8,128)S(1)} all-to-all(f32[32,8,640]{2,1,0:T(8,128)S(1)} %get-tuple-element.34), channel_id=1, replica_groups=mesh['outer'=8,'inner'=4,'heads'=8] {'outer','inner'}, dimensions={0} | all-to-all | bytes 1310720 | tf_op jit(solution)/shard_map/all_to_all | solution.py:338
  26.2 4.8 %all-to-all-start.1 = ((f32[32,8,512]{2,1,0:T(8,128)}), f32[32,8,512]{2,1,0:T(8,128)S(1)}, u32[]{:S(2)}, u32[]{:S(2)}) async-start(f32[32,8,512]{2,1,0:T(8,128)} %get-tuple-element.35), calls=%async_computation.1 | async-start | bytes 1048576 | tf_op jit(solution)/shard_map/all_to_all | solution.py:345
  31.6 3.0 %local.1 = (f32[256,1024]{1,0:T(8,128)S(1)}, f32[256,1024]{1,0:T(8,128)S(1)}, f32[256,1024]{1,0:T(8,128)S(1)}, f32[256,1024]{1,0:T(8,128)S(1)}, f32[256,1024]{1,0:T(8,128)}) custom-call(f32[256,16]{1,0:T(8,128)S(1)} %get-tuple-element.36.cum_ref, bf16[256,1024]{1,0:T(8,128)(2,1)S(1)} %copy-done.3, bf16[256,128]{1,0:T(8,128)(2,1)S(1)} %copy-done.14, ...), custom_call_target="tpu_custom_call" | custom-call | flops 8000000000 | bytes 6438976 | tf_op jit(solution)/shard_map/local/pallas_call | solution.py:312
  35.6 1.0 copy-done.19
  36.7 1.0 copy-done.32
  37.6 4.4 %all-to-all-done.1.s_ref = f32[32,8,512]{2,1,0:T(8,128)S(1)} async-done(((f32[32,8,512]{2,1,0:T(8,128)}), f32[32,8,512]{2,1,0:T(8,128)S(1)}, u32[]{:S(2)}, u32[]{:S(2)}) %all-to-all-start.1) | async-done | bytes 524320 | tf_op jit(solution)/shard_map/all_to_all | solution.py:345
  42.9 1.0 copy-done.7
  43.9 1.2 %copy-done.18 = f32[256,1024]{1,0:T(8,128)S(1)} copy-done((f32[256,1024]{1,0:T(8,128)S(1)}, f32[256,1024]{1,0:T(8,128)}, u32[]{:S(2)}) %copy-start.18) | copy-done | bytes 1048600
  45.2 1.2 %copy-done.20 = f32[256,1024]{1,0:T(8,128)S(1)} copy-done((f32[256,1024]{1,0:T(8,128)S(1)}, f32[256,1024]{1,0:T(8,128)}, u32[]{:S(2)}) %copy-start.20) | copy-done | bytes 1048600
  47.0 15.2 %all_to_all.26.refs_0_ = f32[8,8,256]{2,1,0:T(8,128)S(1)} all-to-all(f32[8,8,256]{2,1,0:T(8,128)S(1)} %get-tuple-element.39), channel_id=1, replica_groups=mesh['outer'=8,'inner'=4,'heads'=8] {'heads'}, dimensions={0} | all-to-all | bytes 131072 | tf_op jit(solution)/shard_map/all_to_all | solution.py:350
  63.2 18.0 %all_to_all.27.in_ref = f32[32,8,640]{2,1,0:T(8,128)S(1)} all-to-all(f32[32,8,640]{2,1,0:T(8,128)S(1)} %get-tuple-element.43), channel_id=1, replica_groups=mesh['outer'=8,'inner'=4,'heads'=8] {'outer','inner'}, dimensions={0} | all-to-all | bytes 1310720 | tf_op jit(solution)/shard_map/all_to_all | solution.py:359
  82.1 4.7 %all-to-all-start.4 = ((f32[32,8,640]{2,1,0:T(8,128)}), f32[32,8,640]{2,1,0:T(8,128)S(1)}, u32[]{:S(2)}, u32[]{:S(2)}) async-start(f32[32,8,640]{2,1,0:T(8,128)} %get-tuple-element.46), calls=%async_computation.4 | async-start | bytes 1310720 | tf_op jit(solution)/shard_map/all_to_all | solution.py:369
  86.8 1.0 copy-done.4
  87.8 1.0 copy-done.8
  88.9 1.0 copy-done.13
  90.8 7.7 %grads.1 = (f32[256,1024]{1,0:T(8,128)S(1)}, bf16[256,1024]{1,0:T(8,128)(2,1)}, f32[256,128]{1,0:T(8,128)S(1)}, f32[256,128]{1,0:T(8,128)}, f32[256,16]{1,0:T(8,128)S(1)}) custom-call(f32[256,16]{1,0:T(8,128)S(1)} %copy-done.26, f32[256,128]{1,0:T(8,128)S(1)} %get-tuple-element.48.scal_ref, f32[256,1024]{1,0:T(8,128)S(1)} %get-tuple-element.40.refs_1_.gated_ref, ...), custom_call_target="tpu_custom_call" | custom-call | flops 16000000000 | bytes 9474112 | tf_op jit(solution)/shard_map/grads/pallas_call | solution.py:312
  98.5 1.0 copy-done.23
  100.8 1.0 copy-done.5
  101.8 1.0 copy-done.9
  102.9 1.2 %copy-done.22 = f32[256,1024]{1,0:T(8,128)S(1)} copy-done((f32[256,1024]{1,0:T(8,128)S(1)}, f32[256,1024]{1,0:T(8,128)}, u32[]{:S(2)}) %copy-start.22) | copy-done | bytes 1048600
  104.1 1.2 %copy-done.24 = f32[256,1024]{1,0:T(8,128)S(1)} copy-done((f32[256,1024]{1,0:T(8,128)S(1)}, f32[256,1024]{1,0:T(8,128)}, u32[]{:S(2)}) %copy-start.24) | copy-done | bytes 1048600
  108.0 2.0 %final.1 = (bf16[256,1024]{1,0:T(8,128)(2,1)}, f32[256,128]{1,0:T(8,128)}, f32[256,16]{1,0:T(8,128)S(1)}, f32[8,128]{1,0:T(8,128)S(1)}) custom-call(f32[32,8,640]{2,1,0:T(8,128)S(1)} %all-to-all-done.4.a_ref, f32[32,8,512]{2,1,0:T(8,128)S(1)} %copy-done.9, f32[256,16]{1,0:T(8,128)S(1)} %copy-done.27, f32[256,1024]{1,0:T(8,128)S(1)} %copy-done.22, ...), custom_call_target="tpu_custom_call" | custom-call | flops 2000000000 | bytes 4706304 | tf_op jit(solution)/shard_map/final/pallas_call | solution.py:312
  (60 shorter events, 13.7 us)
Async XLA Ops:
  1.5 1.0 copy-start.2
  3.7 1.0 copy-start.21
  4.7 26.3 %copy-start.25 = (f32[256,16]{1,0:T(8,128)}, f32[256,16]{1,0:T(8,128)S(1)}, u32[]{:S(2)}) copy-start(f32[256,16]{1,0:T(8,128)S(1)} %get-tuple-element.36.cum_ref) | copy-start | bytes 49156
  25.3 5.7 %copy-start.12 = (bf16[256,1024]{1,0:T(8,128)(2,1)S(1)}, bf16[256,1024]{1,0:T(8,128)(2,1)}, u32[]{:S(2)}) copy-start(bf16[256,1024]{1,0:T(8,128)(2,1)} %z_ref.3) | copy-start | bytes 1572868
  26.1 4.8 %copy-start.3 = (bf16[256,1024]{1,0:T(8,128)(2,1)S(1)}, bf16[256,1024]{1,0:T(8,128)(2,1)}, u32[]{:S(2)}) copy-start(bf16[256,1024]{1,0:T(8,128)(2,1)} %x_ref.7) | copy-start | bytes 1572868
  26.1 4.9 %copy-start.10 = (bf16[256,128]{1,0:T(8,128)(2,1)S(1)}, bf16[256,128]{1,0:T(8,128)(2,1)}, u32[]{:S(2)}) copy-start(bf16[256,128]{1,0:T(8,128)(2,1)} %c_ref.5) | copy-start | bytes 196612
  26.2 15.9 %all-to-all-start.1 = ((f32[32,8,512]{2,1,0:T(8,128)}), f32[32,8,512]{2,1,0:T(8,128)S(1)}, u32[]{:S(2)}, u32[]{:S(2)}) async-start(f32[32,8,512]{2,1,0:T(8,128)} %get-tuple-element.35), calls=%async_computation.1 | async-start | bytes 1048576 | tf_op jit(solution)/shard_map/all_to_all | solution.py:345
  31.6 11.3 %copy-start.1 = (bf16[256,1024]{1,0:T(8,128)(2,1)S(1)}, bf16[256,1024]{1,0:T(8,128)(2,1)}, u32[]{:S(2)}) copy-start(bf16[256,1024]{1,0:T(8,128)(2,1)} %dout_ref.3) | copy-start | bytes 1572868
  35.6 1.0 copy-start.19
  37.6 5.3 %copy-start.11 = (f32[1024]{0:T(1024)S(1)}, f32[1024]{0:T(1024)}, u32[]{:S(2)}) copy-start(f32[1024]{0:T(1024)} %param.14) | copy-start | bytes 12292
  42.9 1.0 copy-start.7
  43.9 1.2 %copy-start.18 = (f32[256,1024]{1,0:T(8,128)S(1)}, f32[256,1024]{1,0:T(8,128)}, u32[]{:S(2)}) copy-start(f32[256,1024]{1,0:T(8,128)} %copy-done.17) | copy-start | bytes 3145732
  45.2 1.2 %copy-start.20 = (f32[256,1024]{1,0:T(8,128)S(1)}, f32[256,1024]{1,0:T(8,128)}, u32[]{:S(2)}) copy-start(f32[256,1024]{1,0:T(8,128)} %copy-done.19) | copy-start | bytes 3145732
  46.4 15.8 %copy-start = (f32[256,1024]{1,0:T(8,128)S(1)}, f32[256,1024]{1,0:T(8,128)}, u32[]{:S(2)}) copy-start(f32[256,1024]{1,0:T(8,128)} %get-tuple-element.42.refs_3_.ecum_ref) | copy-start | bytes 3145732
  47.0 16.2 %copy-start.16 = (f32[256,1024]{1,0:T(8,128)}, f32[256,1024]{1,0:T(8,128)S(1)}, u32[]{:S(2)}) copy-start(f32[256,1024]{1,0:T(8,128)S(1)} %get-tuple-element.50.cs_ref) | copy-start | bytes 3145732
  82.1 18.7 %all-to-all-start.4 = ((f32[32,8,640]{2,1,0:T(8,128)}), f32[32,8,640]{2,1,0:T(8,128)S(1)}, u32[]{:S(2)}, u32[]{:S(2)}) async-start(f32[32,8,640]{2,1,0:T(8,128)} %get-tuple-element.46), calls=%async_computation.4 | async-start | bytes 1310720 | tf_op jit(solution)/shard_map/all_to_all | solution.py:369
  86.8 1.0 copy-start.4
  87.8 1.0 copy-start.8
  88.9 1.0 copy-start.13
  98.5 1.0 copy-start.23
  100.8 1.0 copy-start.5
  101.8 1.0 copy-start.9
  102.9 1.2 %copy-start.22 = (f32[256,1024]{1,0:T(8,128)S(1)}, f32[256,1024]{1,0:T(8,128)}, u32[]{:S(2)}) copy-start(f32[256,1024]{1,0:T(8,128)} %copy-done.21) | copy-start | bytes 3145732
  104.1 1.2 %copy-start.24 = (f32[256,1024]{1,0:T(8,128)S(1)}, f32[256,1024]{1,0:T(8,128)}, u32[]{:S(2)}) copy-start(f32[256,1024]{1,0:T(8,128)} %copy-done.23) | copy-start | bytes 3145732
  (11 other events, 9.2 us)

commit v2 on v1

v2 whole, which is shorter than its diff:
```python
import jax
import jax.numpy as jnp
from jax import lax
from jax.experimental import pallas as pl
from jax.experimental.pallas import tpu as pltpu
from jax.sharding import PartitionSpec as P

P_SIZE = 64
EPS = 1e-05
F32 = jnp.float32
BF16 = jnp.bfloat16
CHUNKS = ("outer", "inner")
VMEM = pl.BlockSpec(memory_space=pltpu.VMEM)
HBM = pl.BlockSpec(memory_space=pltpu.HBM)
HALF = 128


def mm(a, b, ca=1, cb=0):
    return lax.dot_general(a, b, (((ca,), (cb,)), ((), ())), preferred_element_type=F32)


def split2(a):
    hi = a.astype(BF16)
    return hi, (a - hi.astype(F32)).astype(BF16)


def split3(a):
    hi = a.astype(BF16)
    rest = a - hi.astype(F32)
    mid = rest.astype(BF16)
    return hi, mid, (rest - mid.astype(F32)).astype(BF16)


def mm2(a, b, ca=1, cb=0):
    hi, lo = split2(a)
    return mm(hi, b, ca, cb) + mm(lo, b, ca, cb)


def iota(shape, dim):
    return lax.broadcasted_iota(jnp.int32, shape, dim)


def head_map(heads, width):
    return jnp.where(iota((heads, width), 1) // P_SIZE == iota((heads, width), 0), 1.0, 0.0).astype(BF16)


def expand(a, spread, ca=1):
    hi, mid, lo = split3(a)
    return mm(hi, spread, ca) + mm(mid, spread, ca) + mm(lo, spread, ca)


def segment(a, spread):
    hi, lo = split2(a)
    return mm(spread, hi, 1, 1) + mm(spread, lo, 1, 1)


def triangle(n, keep):
    return jnp.where(keep(iota((n, n), 0), iota((n, n), 1)), 1.0, 0.0).astype(BF16)


def mm_by(a, tri):
    hi, mid, lo = split3(a)
    return mm(hi, tri) + mm(mid, tri) + mm(lo, tri)


def store_state(out_ref, state, rows):
    for q in range(state.shape[1] // HALF):
        for r in range(4):
            at = rows * (4 * q + r)
            out_ref[at : at + 32, :] = state[32 * r : 32 * r + 32, HALF * q : HALF * (q + 1)]


def load_state(ref, rows):
    cols = []
    for q in range(8):
        at = [rows * (4 * q + r) for r in range(4)]
        cols.append(jnp.concatenate([ref[i : i + 32, :] for i in at], axis=0))
    return jnp.concatenate(cols, axis=1)


def start_kernel(lt_ref, x_hbm, b_ref, pay_ref, cum_ref, tail_ref, x_ref, sems):
    heads, length = lt_ref.shape
    width = x_hbm.shape[1]
    copies = []
    for k in range(4):
        cols = pl.ds(256 * k, 256)
        copies.append(pltpu.make_async_copy(x_hbm.at[:, cols], x_ref.at[:, cols], sems.at[k]))
        copies[-1].start()
    spread = head_map(heads, width)
    cum = mm_by(lt_ref[...], triangle(length, lambda i, j: i <= j))
    cum_ref[...] = cum
    last = cum[:, length - 1 : length]
    tail = expand(jnp.exp(last - cum), spread, 0)
    tail_ref[...] = tail
    whole = expand(jnp.broadcast_to(jnp.exp(last), (heads, HALF)), spread, 0)[0:1, :]
    b_val = b_ref[...]
    for k in range(4):
        copies[k].wait()
        big = slice(256 * k, 256 * (k + 1))
        hi, lo = split2(x_ref[:, big].astype(F32) * tail[:, big])
        state = mm(b_val, hi, 0, 0) + mm(b_val, lo, 0, 0)
        for q in (2 * k, 2 * k + 1):
            for r in range(4):
                at = 33 * (4 * q + r)
                off = HALF * (q - 2 * k)
                pay_ref[at : at + 32, :] = state[32 * r : 32 * r + 32, off : off + HALF]
                pay_ref[at + 32 : at + 33, :] = whole[:, HALF * q : HALF * (q + 1)]


def local_kernel(cum_ref, x_ref, b_ref, c_ref, z_ref, d_ref, yn_ref, base_ref, silu_ref, esilu_ref, ecum_ref):
    heads, length = cum_ref.shape
    width = x_ref.shape[1]
    spread = head_map(heads, width)
    cum_t = cum_ref[...]
    cum = cum_t.T
    ecum = expand(jnp.exp(cum_t), spread, 0)
    ecum_ref[...] = ecum
    z_val = z_ref[...].astype(F32)
    silu = z_val * (1.0 / (1.0 + jnp.exp(-z_val)))
    silu_ref[...] = silu
    esilu_ref[...] = ecum * silu
    skip = expand(jnp.broadcast_to(d_ref[...], (8, heads)), spread)[0:1, :]
    inner = mm(c_ref[...], b_ref[...], 1, 1)
    top, left, right = inner[:HALF, :HALF], inner[HALF:, :HALF], inner[HALF:, HALF:]
    lower = iota((HALF, HALF), 0) >= iota((HALF, HALF), 1)
    first = iota((length, HALF), 1) < P_SIZE
    for q in range(width // HALF):
        cols = slice(HALF * q, HALF * (q + 1))
        x_pair = x_ref[:, cols]
        parts = []
        for h in (2 * q, 2 * q + 1):
            col, row = cum[:, h : h + 1], cum_t[h : h + 1, :]
            up = jnp.where(lower, jnp.exp(col[:HALF] - row[:, :HALF]), 0.0) * top
            dl = jnp.exp(col[HALF:] - row[:, :HALF]) * left
            dr = jnp.where(lower, jnp.exp(col[HALF:] - row[:, HALF:]), 0.0) * right
            down = jnp.concatenate([dl, dr], axis=1)
            parts.append(jnp.concatenate([mm2(up, x_pair[:HALF]), mm2(down, x_pair)], axis=0))
        yn = jnp.where(first, parts[0], parts[1])
        yn_ref[:, cols] = yn
        base_ref[:, cols] = (yn + skip[:, cols] * x_pair.astype(F32)) * silu_ref[:, cols]


def prefix_kernel(in_ref, out_ref, dec_ref):
    count = dec_ref.shape[0]
    state = jnp.zeros((32, HALF), F32)
    for p in range(count):
        out_ref[32 * p : 32 * p + 32, :] = state
        decay = in_ref[33 * p + 32 : 33 * p + 33, :]
        dec_ref[p : p + 1, :] = decay
        if p < count - 1:
            state = decay * state + in_ref[33 * p : 33 * p + 32, :]


def suffix_kernel(in_ref, dec_ref, out_ref):
    count = dec_ref.shape[0]
    state = jnp.zeros((32, HALF), F32)
    sums = in_ref[32:34, :]
    for p in range(1, count):
        sums = sums + in_ref[34 * p + 32 : 34 * p + 34, :]
    for p in range(count - 1, -1, -1):
        out_ref[34 * p : 34 * p + 32, :] = state
        out_ref[34 * p + 32 : 34 * p + 34, :] = sums
        if p > 0:
            state = dec_ref[p : p + 1, :] * state + in_ref[34 * p : 34 * p + 32, :]


def gate_kernel(s_ref, c_ref, base_ref, esilu_ref, dout_ref, w_ref, gated_ref, cs_ref, sums_ref):
    hi, lo = split2(load_state(s_ref, 32))
    c_val = c_ref[...]
    length, width = base_ref.shape
    squares = jnp.zeros((length, HALF), F32)
    products = jnp.zeros((length, HALF), F32)
    for q in range(width // 256):
        big = slice(256 * q, 256 * (q + 1))
        c_state = mm(c_val, hi[:, big]) + mm(c_val, lo[:, big])
        cs_ref[:, big] = c_state
        gated = base_ref[:, big] + esilu_ref[:, big] * c_state
        gated_ref[:, big] = gated
        sq = gated * gated
        pr = dout_ref[:, big].astype(F32) * w_ref[:, big] * gated
        squares = squares + sq[:, :HALF] + sq[:, HALF:]
        products = products + pr[:, :HALF] + pr[:, HALF:]
    sq_row = jnp.sum(squares.T, axis=0, keepdims=True)
    pr_row = jnp.sum(products.T, axis=0, keepdims=True)
    tile = jnp.concatenate([sq_row, pr_row, jnp.zeros((6, length), F32)], axis=0)
    for i in range(sums_ref.shape[0]):
        sums_ref[i] = tile


def back_kernel(channels, sums_ref, gated_ref, silu_ref, ecum_ref, dout_ref, w_ref, x_ref, c_ref, pay_ref, scal_ref):
    length, width = gated_ref.shape
    total = sums_ref[0]
    for i in range(1, sums_ref.shape[0]):
        total = total + sums_ref[i]
    squares, products = total[0:1, :], total[1:2, :]
    inv = lax.rsqrt(squares / channels + EPS)
    fall = inv * inv * inv * products / channels
    both = jnp.concatenate([inv, fall, jnp.zeros((HALF - 2, length), F32)], axis=0).T
    scal_ref[...] = both
    inv_col, fall_col = both[:, 0:1], both[:, 1:2]
    c_val = c_ref[...]
    for k in range(width // 256):
        big = slice(256 * k, 256 * (k + 1))
        gated = gated_ref[:, big]
        d_inv = dout_ref[:, big].astype(F32) * inv_col
        dy = (d_inv * w_ref[:, big] - gated * fall_col) * silu_ref[:, big]
        weight = jnp.sum(d_inv * gated, axis=0, keepdims=True)
        skip = jnp.sum(dy * x_ref[:, big].astype(F32), axis=0, keepdims=True)
        hi, lo = split2(dy * ecum_ref[:, big])
        back = mm(c_val, hi, 0, 0) + mm(c_val, lo, 0, 0)
        for q in (2 * k, 2 * k + 1):
            off = HALF * (q - 2 * k)
            for r in range(4):
                at = 34 * (4 * q + r)
                pay_ref[at : at + 32, :] = back[32 * r : 32 * r + 32, off : off + HALF]
                pay_ref[at + 32 : at + 33, :] = weight[:, off : off + HALF]
                pay_ref[at + 33 : at + 34, :] = skip[:, off : off + HALF]


def grads_kernel(
    cum_ref, scal_ref, gated_ref, silu_ref, ecum_ref, dout_ref, w_ref, x_ref, z_ref, b_ref, c_ref, d_ref, yn_ref, cs_ref, s_ref,
    gx_ref, gz_ref, gb_ref, gc_ref, gl_ref, dy_ref, dot_ref,
):
    heads, length = cum_ref.shape
    width = x_ref.shape[1]
    spread = head_map(heads, width)
    cum_t = cum_ref[...]
    cum = cum_t.T
    inv_col, fall_col = scal_ref[:, 0:1], scal_ref[:, 1:2]
    skip = expand(jnp.broadcast_to(d_ref[...], (8, heads)), spread)[0:1, :]
    inner_t = mm(b_ref[...], c_ref[...], 1, 1)
    left, right, low = inner_t[:HALF, :HALF], inner_t[:HALF, HALF:], inner_t[HALF:, HALF:]
    upper = iota((HALF, HALF), 0) <= iota((HALF, HALF), 1)
    first = iota((length, HALF), 1) < P_SIZE
    w_left = jnp.zeros((HALF, HALF), F32)
    w_right = jnp.zeros((HALF, HALF), F32)
    w_low = jnp.zeros((HALF, HALF), F32)
    for q in range(width // HALF):
        cols = slice(HALF * q, HALF * (q + 1))
        gated, silu = gated_ref[:, cols], silu_ref[:, cols]
        d_gated = inv_col * (dout_ref[:, cols].astype(F32) * w_ref[:, cols]) - gated * fall_col
        dy = d_gated * silu
        dy_ref[:, cols] = dy * ecum_ref[:, cols]
        x_pair = x_ref[:, cols]
        x_val = x_pair.astype(F32)
        z_val = z_ref[:, cols].astype(F32)
        sig = 1.0 / (1.0 + jnp.exp(-z_val))
        y_near = yn_ref[:, cols] + ecum_ref[:, cols] * cs_ref[:, cols]
        y_val = y_near + skip[:, cols] * x_val
        gz_ref[:, cols] = (d_gated * y_val * sig * (1.0 + z_val * (1.0 - sig))).astype(BF16)
        hi, lo = split2(dy)
        parts = []
        for k in range(2):
            h = 2 * q + k
            col, row = cum[:, h : h + 1], cum_t[h : h + 1, :]
            x_one = jnp.where(first if k == 0 else ~first, x_val, 0.0).astype(BF16)
            dec_left = jnp.where(upper, jnp.exp(row[:, :HALF] - col[:HALF]), 0.0)
            dec_right = jnp.exp(row[:, HALF:] - col[:HALF])
            dec_low = jnp.where(upper, jnp.exp(row[:, HALF:] - col[HALF:]), 0.0)
            dot_up = mm(x_one[:HALF], hi, 1, 1) + mm(x_one[:HALF], lo, 1, 1)
            dot_low = mm(x_one[HALF:], hi[HALF:], 1, 1) + mm(x_one[HALF:], lo[HALF:], 1, 1)
            w_left = w_left + dec_left * dot_up[:, :HALF]
            w_right = w_right + dec_right * dot_up[:, HALF:]
            w_low = w_low + dec_low * dot_low
            mix_up = jnp.concatenate([dec_left * left, dec_right * right], axis=1)
            mix_low = dec_low * low
            up_hi, up_lo = split2(mix_up)
            low_hi, low_lo = split2(mix_low)
            g_up = mm(up_hi, hi) + mm(up_hi, lo) + mm(up_lo, hi)
            g_low = mm(low_hi, hi[HALF:]) + mm(low_hi, lo[HALF:]) + mm(low_lo, hi[HALF:])
            parts.append(jnp.concatenate([g_up, g_low], axis=0))
        g_near = jnp.where(first, parts[0], parts[1])
        gx_ref[:, cols] = g_near + skip[:, cols] * dy
        dot_ref[:, cols] = dy * y_near - x_val * g_near
    gl_ref[...] = mm_by(segment(dot_ref[...], spread), triangle(length, lambda i, j: i >= j))
    e_hi, e_lo = split2(dy_ref[...])
    s_hi, s_lo = split2(load_state(s_ref, 32))
    far = mm(e_hi, s_hi, 1, 1) + mm(e_hi, s_lo, 1, 1) + mm(e_lo, s_hi, 1, 1)
    w_up = jnp.concatenate([w_left, w_right], axis=1)
    b_val, c_val = b_ref[...], c_ref[...]
    gb_ref[:HALF, :] = mm2(w_up, c_val)
    gb_ref[HALF:, :] = mm2(w_low, c_val[HALF:])
    low_part = mm2(w_right.T, b_val[:HALF]) + mm2(w_low.T, b_val[HALF:])
    gc_ref[...] = far + jnp.concatenate([mm2(w_left.T, b_val[:HALF]), low_part], axis=0)


def final_kernel(
    a_ref, s_ref, cum_ref, tail_ref, x_ref, b_ref, gx_ref, gb_ref, gl_ref,
    ox_hbm, ob_ref, ol_ref, skip_ref, weight_ref, ox_ref, sems,
):
    heads, length = cum_ref.shape
    width = x_ref.shape[1]
    spread = head_map(heads, width)
    after = load_state(a_ref, 34)
    a_hi, a_lo = split2(after)
    b_val = b_ref[...]
    copies = []
    late = jnp.zeros((heads, length), F32)
    far = jnp.zeros(ob_ref.shape, F32)
    for k in range(width // 256):
        big = slice(256 * k, 256 * (k + 1))
        tail, x_val = tail_ref[:, big], x_ref[:, big].astype(F32)
        one_hi, one_lo = a_hi[:, big], a_lo[:, big]
        b_after = (mm(b_val, one_hi) + mm(b_val, one_lo)) * tail
        ox_ref[:, big] = (gx_ref[:, big] + b_after).astype(BF16)
        cols = pl.ds(256 * k, 256)
        copies.append(pltpu.make_async_copy(ox_ref.at[:, cols], ox_hbm.at[:, cols], sems.at[k]))
        copies[-1].start()
        late = late + segment(x_val * b_after, spread[:, big])
        x_hi, x_lo = split2(x_val * tail)
        far = far + (mm(x_hi, one_hi, 1, 1) + mm(x_hi, one_lo, 1, 1) + mm(x_lo, one_hi, 1, 1))
    ob_ref[...] = gb_ref[...] + far
    start = jnp.broadcast_to(jnp.sum(load_state(s_ref, 32) * after, axis=0, keepdims=True), (HALF, width))
    hi, mid, lo = split3(start)
    start = (mm(spread, hi, 1, 1) + mm(spread, mid, 1, 1) + mm(spread, lo, 1, 1))[:, 0:1]
    whole = jnp.exp(cum_ref[:, length - 1 : length])
    ol_ref[...] = gl_ref[...] + mm_by(late, triangle(length, lambda i, j: i < j)) + whole * start
    sums = [a_ref[34 * 4 * q + 32 : 34 * 4 * q + 34, :] for q in range(8)]
    weight_ref[...] = jnp.concatenate([one[0:1, :] for one in sums], axis=0)
    skip = jnp.concatenate([one[1:2, :] for one in sums], axis=0)
    halves = jnp.where(iota((HALF, heads), 0) // P_SIZE == iota((HALF, heads), 1) % 2, 1.0, 0.0).astype(BF16)
    skip = mm_by(skip, halves)
    skip = jnp.where(iota((8, heads), 1) // 2 == iota((8, heads), 0), skip, 0.0)
    skip_ref[...] = jnp.sum(skip, axis=0, keepdims=True)
    for copy in copies:
        copy.wait()


def call(kernel, name, outs, *args, flops=0, scratch=(), hbm_in=(), hbm_out=(), mib=16):
    nbytes = sum(a.size * a.dtype.itemsize for a in (*args, *outs))
    return pl.pallas_call(
        kernel,
        name=name,
        out_shape=outs,
        in_specs=[HBM if i in hbm_in else VMEM for i in range(len(args))],
        out_specs=[HBM if i in hbm_out else VMEM for i in range(len(outs))],
        scratch_shapes=list(scratch),
        compiler_params=pltpu.CompilerParams(vmem_limit_bytes=mib * 1024 * 1024),
        cost_estimate=pl.CostEstimate(flops=flops, bytes_accessed=nbytes, transcendentals=0),
    )(*args)


def exchange(messages, rows):
    count = lax.axis_size(CHUNKS)
    got = lax.all_to_all(messages.reshape(count, 1, rows * HALF), CHUNKS, 0, 0)
    return got.reshape(count * rows, HALF)


def on_device(x_in, b_in, c_in, decay_log, d_skip, gate, norm_weight, d_out):
    length, heads = decay_log.shape
    width = x_in.shape[1]
    chunks = lax.axis_size(CHUNKS)
    groups = lax.axis_size("heads")
    shape = jax.ShapeDtypeStruct
    wide = shape((length, width), F32)
    half_wide = shape((length, width), BF16)
    small = shape((heads, length), F32)
    weight = norm_weight.reshape(1, width)
    d_row = d_skip.reshape(1, heads)
    pieces = [pltpu.VMEM((length, width), BF16), pltpu.SemaphoreType.DMA((4,))]

    pay, cum, tail = call(
        start_kernel, "start", [shape((chunks * 33, HALF), F32), small, wide], decay_log.T, x_in, b_in,
        flops=10**9, scratch=pieces, hbm_in=(1,),
    )
    got = exchange(pay, 33)
    y_near, base, silu, esilu, ecum = call(
        local_kernel, "local", [wide] * 5, cum, x_in, b_in, c_in, gate, d_row, flops=8 * 10**9, mib=24
    )
    spread, decays = call(
        prefix_kernel, "prefix", [shape((chunks * 32, HALF), F32), shape((chunks, HALF), F32)], got
    )
    before = exchange(spread, 32)
    gated, c_state, sums = call(
        gate_kernel, "gated", [wide, wide, shape((groups, 8, length), F32)],
        before, c_in, base, esilu, d_out, weight, flops=10**9,
    )
    sums = lax.all_to_all(sums, "heads", 0, 0)

    def back(*refs):
        back_kernel(float(width * groups), *refs)

    pay, scalars = call(
        back, "back", [shape((chunks * 34, HALF), F32), shape((length, HALF), F32)],
        sums, gated, silu, ecum, d_out, weight, x_in, c_in, flops=10**9,
    )
    got = exchange(pay, 34)
    gx, grad_gate, gb, grad_c, gl = call(
        grads_kernel, "grads",
        [wide, half_wide, shape(b_in.shape, F32), shape(c_in.shape, F32), small],
        cum, scalars, gated, silu, ecum, d_out, weight, x_in, gate, b_in, c_in, d_row, y_near, c_state, before,
        flops=16 * 10**9, scratch=[pltpu.VMEM((length, width), F32)] * 2, mib=28,
    )
    (spread,) = call(suffix_kernel, "suffix", [shape((chunks * 34, HALF), F32)], got, decays)
    after = exchange(spread, 34)
    grad_x, grad_b, grad_decay, grad_skip, grad_weight = call(
        final_kernel, "final",
        [half_wide, shape(b_in.shape, F32), small, shape((1, heads), F32), shape((8, HALF), F32)],
        after, before, cum, tail, x_in, b_in, gx, gb, gl, flops=2 * 10**9, scratch=pieces, hbm_out=(0,),
    )
    return (
        grad_x,
        grad_b,
        grad_c,
        grad_decay.T,
        grad_skip.reshape(heads),
        grad_gate,
        grad_weight.reshape(width),
    )


def solution(mesh):
    tokens = P(CHUNKS, "heads")
    in_specs = (tokens, tokens, tokens, tokens, P("heads"), tokens, P("heads"), tokens)
    out_specs = (tokens, tokens, tokens, tokens, P("heads"), tokens, P("heads"))
    return jax.shard_map(on_device, mesh=mesh, in_specs=in_specs, out_specs=out_specs, check_vma=False)
```

time: 112 us -> 113 us (level)
  blocking collectives: 53.8 us -> 51.8 us
  local copies, waits for them, and re-layouts: 25.5 us -> 27.2 us
    unnamed x68 -> x66, local copies, waits for them, and re-layouts: 25 us -> 27.2 us
    all_to_all x2, blocking collectives: 38.6 us -> 36.6 us  [exchange(): got = lax.all_to_all(messages.reshape(count, 1, rows * HALF), CHUNKS, 0, 0)]
  transfers between devices with their start and end apart: 2 -> 2, of which waited for: 1 -> 1; matrix products, arithmetic and copies ran while one was open for 0% -> 0% of each run, Pallas kernels for 10% -> 7%
where the time goes in v2:
time: 113 us; the launch traced here: 112 us
  blocking collectives  51.8 us (46%)
  local copies, waits for them, and re-layouts  27.2 us (24%)
  Pallas kernels  17.3 us (15%)
  starting transfers between devices  9.99 us (9%)
  waiting for transfers between devices  4.28 us (4%)
    all_to_all x2, blocking collectives, exchange(): got = lax.all_to_all(messages.reshape(count, 1, rows * HALF), CHUNKS, 0, 0)  36.6 us
    unnamed x66, local copies, waits for them, and re-layouts  27.2 us
    pallas_call x8, Pallas kernels, call(): pl.pallas_call(kernel, name=name, out_shape=outs, in_specs=[HBM if i in h...  17.3 us
    all_to_all x1, blocking collectives, on_device(): sums = lax.all_to_all(sums, 'heads', 0, 0)  15.2 us
    all_to_all x2, starting transfers between devices, exchange(): got = lax.all_to_all(messages.reshape(count, 1, rows * HALF), CHUNKS, 0, 0)  9.99 us
    all_to_all x2, waiting for transfers between devices, exchange(): got = lax.all_to_all(messages.reshape(count, 1, rows * HALF), CHUNKS, 0, 0)  4.28 us
  transfers between devices with their start and end apart: 2, of which 1 were waited for; matrix products, arithmetic and copies ran while one was open for 0% of the time, Pallas kernels for 7%

profile of v2, /device:TPU:1, one launch (start us, length us, event | category | flops | bytes accessed | tf_op | source)
XLA Modules:
  0.0 111.5 jit_solution(9648106587243803464)
XLA Ops:
  3.2 2.2 %start.1 = (f32[1056,128]{1,0:T(8,128)S(1)}, f32[16,256]{1,0:T(8,128)S(1)}, f32[256,1024]{1,0:T(8,128)S(1)}) custom-call(f32[16,256]{1,0:T(8,128)S(1)} %bitcast.24, bf16[256,1024]{1,0:T(8,128)(2,1)S(1)} %copy-done.2, bf16[256,128]{1,0:T(8,128)(2,1)S(1)} %copy-done.15), custom_call_target="tpu_custom_call" | custom-call | flops 1000000000 | bytes 2211840 | tf_op jit(solution)/shard_map/start/pallas_call | solution.py:331
  5.4 19.6 %all_to_all.25 = f32[32,1,4224]{2,1,0:T(1,128)S(1)} all-to-all(f32[32,1,4224]{2,1,0:T(1,128)S(1)} %bitcast.17), channel_id=1, replica_groups=mesh['outer'=8,'inner'=4,'heads'=8] {'outer','inner'}, dimensions={0} | all-to-all | bytes 1081344 | tf_op jit(solution)/shard_map/all_to_all | solution.py:345
  25.8 4.7 %all-to-all-start.1 = ((f32[32,1,4096]{2,1,0:T(1,128)}), f32[32,1,4096]{2,1,0:T(1,128)S(1)}, u32[]{:S(2)}, u32[]{:S(2)}) async-start(f32[32,1,4096]{2,1,0:T(1,128)} %bitcast.3), calls=%async_computation.1 | async-start | bytes 1048576 | tf_op jit(solution)/shard_map/all_to_all | solution.py:345
  31.2 1.0 copy-done.13
  32.3 2.2 %local.1 = (f32[256,1024]{1,0:T(8,128)S(1)}, f32[256,1024]{1,0:T(8,128)S(1)}, f32[256,1024]{1,0:T(8,128)S(1)}, f32[256,1024]{1,0:T(8,128)S(1)}, f32[256,1024]{1,0:T(8,128)S(1)}) custom-call(f32[16,256]{1,0:T(8,128)S(1)} %get-tuple-element.34.cum_ref, bf16[256,1024]{1,0:T(8,128)(2,1)S(1)} %copy-done.3, bf16[256,128]{1,0:T(8,128)(2,1)S(1)} %copy-done.16, ...), custom_call_target="tpu_custom_call" | custom-call | flops 8000000000 | bytes 6438976 | tf_op jit(solution)/shard_map/local/pallas_call | solution.py:331
  37.4 4.3 %all-to-all-done.1 = f32[32,1,4096]{2,1,0:T(1,128)S(1)} async-done(((f32[32,1,4096]{2,1,0:T(1,128)}), f32[32,1,4096]{2,1,0:T(1,128)S(1)}, u32[]{:S(2)}, u32[]{:S(2)}) %all-to-all-start.1) | async-done | bytes 524320 | tf_op jit(solution)/shard_map/all_to_all | solution.py:345
  42.5 1.0 copy-done
  43.5 1.0 copy-done.8
  44.6 1.2 %copy-done.22 = f32[256,1024]{1,0:T(8,128)S(1)} copy-done((f32[256,1024]{1,0:T(8,128)S(1)}, f32[256,1024]{1,0:T(8,128)}, u32[]{:S(2)}) %copy-start.22) | copy-done | bytes 1048600
  45.8 1.2 %copy-done.24 = f32[256,1024]{1,0:T(8,128)S(1)} copy-done((f32[256,1024]{1,0:T(8,128)S(1)}, f32[256,1024]{1,0:T(8,128)}, u32[]{:S(2)}) %copy-start.24) | copy-done | bytes 1048600
  48.6 15.2 %all_to_all.26.refs_0_ = f32[8,8,256]{2,1,0:T(8,128)S(1)} all-to-all(f32[8,8,256]{2,1,0:T(8,128)S(1)} %get-tuple-element.37), channel_id=1, replica_groups=mesh['outer'=8,'inner'=4,'heads'=8] {'heads'}, dimensions={0} | all-to-all | bytes 131072 | tf_op jit(solution)/shard_map/all_to_all | solution.py:378
  64.8 17.1 %all_to_all.27 = f32[32,1,4352]{2,1,0:T(1,128)S(1)} all-to-all(f32[32,1,4352]{2,1,0:T(1,128)S(1)} %bitcast.16), channel_id=1, replica_groups=mesh['outer'=8,'inner'=4,'heads'=8] {'outer','inner'}, dimensions={0} | all-to-all | bytes 1114112 | tf_op jit(solution)/shard_map/all_to_all | solution.py:345
  82.7 5.3 %all-to-all-start.4 = ((f32[32,1,4352]{2,1,0:T(1,128)}), f32[32,1,4352]{2,1,0:T(1,128)}, u32[]{:S(2)}, u32[]{:S(2)}) async-start(f32[32,1,4352]{2,1,0:T(1,128)} %bitcast.9), calls=%async_computation.4 | async-start | bytes 1114112 | tf_op jit(solution)/shard_map/all_to_all | solution.py:345
  89.0 1.0 copy-done.5
  90.1 1.0 copy-done.9
  91.1 1.0 copy-done.14
  92.2 1.2 %copy-done.20 = f32[256,1024]{1,0:T(8,128)S(1)} copy-done((f32[256,1024]{1,0:T(8,128)S(1)}, f32[256,1024]{1,0:T(8,128)}, u32[]{:S(2)}) %copy-start.20) | copy-done | bytes 1048600
  93.4 1.2 %copy-done.32 = f32[256,1024]{1,0:T(8,128)S(1)} copy-done((f32[256,1024]{1,0:T(8,128)S(1)}, f32[256,1024]{1,0:T(8,128)}, u32[]{:S(2)}) %copy-start.32) | copy-done | bytes 1048600
  94.6 5.8 %grads.1 = (f32[256,1024]{1,0:T(8,128)S(1)}, bf16[256,1024]{1,0:T(8,128)(2,1)}, f32[256,128]{1,0:T(8,128)S(1)}, f32[256,128]{1,0:T(8,128)}, f32[16,256]{1,0:T(8,128)S(1)}) custom-call(f32[16,256]{1,0:T(8,128)S(1)} %get-tuple-element.34.cum_ref, f32[256,128]{1,0:T(8,128)S(1)} %get-tuple-element.44.scal_ref, ...), custom_call_target="tpu_custom_call" | custom-call | flops 16000000000 | bytes 9474112 | tf_op jit(solution)/shard_map/grads/pallas_call | solution.py:331
  102.0 1.0 copy-done.6
  103.1 1.0 copy-done.10
  104.1 1.2 %copy-done.26 = f32[256,1024]{1,0:T(8,128)S(1)} copy-done((f32[256,1024]{1,0:T(8,128)S(1)}, f32[256,1024]{1,0:T(8,128)}, u32[]{:S(2)}) %copy-start.26) | copy-done | bytes 1048600
  105.3 1.2 %copy-done.28 = f32[256,1024]{1,0:T(8,128)S(1)} copy-done((f32[256,1024]{1,0:T(8,128)S(1)}, f32[256,1024]{1,0:T(8,128)}, u32[]{:S(2)}) %copy-start.28) | copy-done | bytes 1048600
  107.5 3.9 %final.1 = (bf16[256,1024]{1,0:T(8,128)(2,1)}, f32[256,128]{1,0:T(8,128)}, f32[16,256]{1,0:T(8,128)}, f32[1,16]{1,0:T(1,128)}, f32[8,128]{1,0:T(8,128)}) custom-call(f32[1088,128]{1,0:T(8,128)} %bitcast.10.a_ref, f32[1024,128]{1,0:T(8,128)S(1)} %bitcast.20, f32[16,256]{1,0:T(8,128)S(1)} %get-tuple-element.34.cum_ref, f32[256,1024]{1,0:T(8,128)S(1)} %copy-done.26, ...), custom_call_target="tpu_custom_call" | custom-call | flops 2000000000 | bytes 4608064 | tf_op jit(solution)/shard_map/final/pallas_call | solution.py:331
  (57 shorter events, 14.9 us)
Async XLA Ops:
  0.6 1.0 copy-start.2
  5.4 20.4 %copy-start.25 = (f32[256,1024]{1,0:T(8,128)}, f32[256,1024]{1,0:T(8,128)S(1)}, u32[]{:S(2)}) copy-start(f32[256,1024]{1,0:T(8,128)S(1)} %get-tuple-element.43.tail_ref) | copy-start | bytes 3145732
  25.8 4.8 %copy-start.3 = (bf16[256,1024]{1,0:T(8,128)(2,1)S(1)}, bf16[256,1024]{1,0:T(8,128)(2,1)}, u32[]{:S(2)}) copy-start(bf16[256,1024]{1,0:T(8,128)(2,1)} %x_ref.5) | copy-start | bytes 1572868
  25.8 4.8 %copy-start.11 = (bf16[256,128]{1,0:T(8,128)(2,1)S(1)}, bf16[256,128]{1,0:T(8,128)(2,1)}, u32[]{:S(2)}) copy-start(bf16[256,128]{1,0:T(8,128)(2,1)} %c_ref.5) | copy-start | bytes 196612
  25.8 4.8 %copy-start.16 = (bf16[256,128]{1,0:T(8,128)(2,1)S(1)}, bf16[256,128]{1,0:T(8,128)(2,1)}, u32[]{:S(2)}) copy-start(bf16[256,128]{1,0:T(8,128)(2,1)} %b_ref.7) | copy-start | bytes 196612
  25.8 15.9 %all-to-all-start.1 = ((f32[32,1,4096]{2,1,0:T(1,128)}), f32[32,1,4096]{2,1,0:T(1,128)S(1)}, u32[]{:S(2)}, u32[]{:S(2)}) async-start(f32[32,1,4096]{2,1,0:T(1,128)} %bitcast.3), calls=%async_computation.1 | async-start | bytes 1048576 | tf_op jit(solution)/shard_map/all_to_all | solution.py:345
  31.2 1.0 copy-start.13
  37.4 5.1 %copy-start.12 = (f32[1024]{0:T(1024)S(1)}, f32[1024]{0:T(1024)}, u32[]{:S(2)}) copy-start(f32[1024]{0:T(1024)} %param.14) | copy-start | bytes 12292
  42.5 1.0 copy-start
  43.5 1.0 copy-start.8
  44.6 1.2 %copy-start.22 = (f32[256,1024]{1,0:T(8,128)S(1)}, f32[256,1024]{1,0:T(8,128)}, u32[]{:S(2)}) copy-start(f32[256,1024]{1,0:T(8,128)} %copy-done.21) | copy-start | bytes 3145732
  45.8 1.2 %copy-start.24 = (f32[256,1024]{1,0:T(8,128)S(1)}, f32[256,1024]{1,0:T(8,128)}, u32[]{:S(2)}) copy-start(f32[256,1024]{1,0:T(8,128)} %copy-done.23) | copy-start | bytes 3145732
  47.0 16.8 %copy-start.4 = (bf16[256,1024]{1,0:T(8,128)(2,1)S(1)}, bf16[256,1024]{1,0:T(8,128)(2,1)}, u32[]{:S(2)}) copy-start(bf16[256,1024]{1,0:T(8,128)(2,1)} %x_ref.5) | copy-start | bytes 1572868
  82.7 19.3 %all-to-all-start.4 = ((f32[32,1,4352]{2,1,0:T(1,128)}), f32[32,1,4352]{2,1,0:T(1,128)}, u32[]{:S(2)}, u32[]{:S(2)}) async-start(f32[32,1,4352]{2,1,0:T(1,128)} %bitcast.9), calls=%async_computation.4 | async-start | bytes 1114112 | tf_op jit(solution)/shard_map/all_to_all | solution.py:345
  88.0 1.0 copy-start.1
  89.0 1.0 copy-start.5
  90.1 1.0 copy-start.9
  91.1 1.0 copy-start.14
  92.2 1.2 %copy-start.20 = (f32[256,1024]{1,0:T(8,128)S(1)}, f32[256,1024]{1,0:T(8,128)}, u32[]{:S(2)}) copy-start(f32[256,1024]{1,0:T(8,128)} %copy-done.19) | copy-start | bytes 3145732
  93.4 1.2 %copy-start.32 = (f32[256,1024]{1,0:T(8,128)S(1)}, f32[256,1024]{1,0:T(8,128)}, u32[]{:S(2)}) copy-start(f32[256,1024]{1,0:T(8,128)} %copy-done.31) | copy-start | bytes 3145732
  102.0 1.0 copy-start.6
  103.1 1.0 copy-start.10
  104.1 1.2 %copy-start.26 = (f32[256,1024]{1,0:T(8,128)S(1)}, f32[256,1024]{1,0:T(8,128)}, u32[]{:S(2)}) copy-start(f32[256,1024]{1,0:T(8,128)} %copy-done.25) | copy-start | bytes 3145732
  105.3 1.2 %copy-start.28 = (f32[256,1024]{1,0:T(8,128)S(1)}, f32[256,1024]{1,0:T(8,128)}, u32[]{:S(2)}) copy-start(f32[256,1024]{1,0:T(8,128)} %copy-done.27) | copy-start | bytes 3145732
  (11 other events, 9.5 us)

commit v3 on v2

--- a/solution.py
+++ b/solution.py
@@ -10,8 +10,6 @@
 F32 = jnp.float32
 BF16 = jnp.bfloat16
 CHUNKS = ("outer", "inner")
-VMEM = pl.BlockSpec(memory_space=pltpu.VMEM)
-HBM = pl.BlockSpec(memory_space=pltpu.HBM)
 HALF = 128
 
 
@@ -63,29 +61,35 @@
     return mm(hi, tri) + mm(mid, tri) + mm(lo, tri)
 
 
-def store_state(out_ref, state, rows):
-    for q in range(state.shape[1] // HALF):
-        for r in range(4):
-            at = rows * (4 * q + r)
-            out_ref[at : at + 32, :] = state[32 * r : 32 * r + 32, HALF * q : HALF * (q + 1)]
-
-
-def load_state(ref, rows):
+def load_block(ref, rows, k):
     cols = []
-    for q in range(8):
+    for q in (2 * k, 2 * k + 1):
         at = [rows * (4 * q + r) for r in range(4)]
         cols.append(jnp.concatenate([ref[i : i + 32, :] for i in at], axis=0))
     return jnp.concatenate(cols, axis=1)
 
 
-def start_kernel(lt_ref, x_hbm, b_ref, pay_ref, cum_ref, tail_ref, x_ref, sems):
-    heads, length = lt_ref.shape
+def load_state(ref, rows):
+    return jnp.concatenate([load_block(ref, rows, k) for k in range(4)], axis=1)
+
+
+def fetch(pairs, sems):
+    copies = [pltpu.make_async_copy(src, dst, sems.at[i]) for i, (src, dst) in enumerate(pairs)]
+    for copy in copies:
+        copy.start()
+    return copies
+
+
+def quarters(ref):
+    return [ref.at[:, pl.ds(256 * k, 256)] for k in range(4)]
+
+
+def start_kernel(lt_hbm, x_hbm, b_hbm, pay_ref, cum_ref, tail_ref, x_ref, b_ref, lt_ref, sems):
+    heads, length = lt_hbm.shape
     width = x_hbm.shape[1]
-    copies = []
-    for k in range(4):
-        cols = pl.ds(256 * k, 256)
-        copies.append(pltpu.make_async_copy(x_hbm.at[:, cols], x_ref.at[:, cols], sems.at[k]))
-        copies[-1].start()
+    pairs = [(lt_hbm, lt_ref), (b_hbm, b_ref)] + list(zip(quarters(x_hbm), quarters(x_ref)))
+    first, second, *copies = fetch(pairs, sems)
+    first.wait()
     spread = head_map(heads, width)
     cum = mm_by(lt_ref[...], triangle(length, lambda i, j: i <= j))
     cum_ref[...] = cum
@@ -93,6 +97,7 @@
     tail = expand(jnp.exp(last - cum), spread, 0)
     tail_ref[...] = tail
     whole = expand(jnp.broadcast_to(jnp.exp(last), (heads, HALF)), spread, 0)[0:1, :]
+    second.wait()
     b_val = b_ref[...]
     for k in range(4):
         copies[k].wait()
@@ -107,7 +112,13 @@
                 pay_ref[at + 32 : at + 33, :] = whole[:, HALF * q : HALF * (q + 1)]
 
 
-def local_kernel(cum_ref, x_ref, b_ref, c_ref, z_ref, d_ref, yn_ref, base_ref, silu_ref, esilu_ref, ecum_ref):
+def local_kernel(
+    cum_ref, x_ref, b_ref, c_hbm, z_hbm, d_hbm, w_hbm, dout_hbm,
+    yn_ref, base_ref, silu_ref, esilu_ref, ecum_ref, c_ref, z_ref, d_ref, w_ref, dout_ref, sems,
+):
+    copies = fetch([(c_hbm, c_ref), (z_hbm, z_ref), (d_hbm, d_ref), (w_hbm, w_ref), (dout_hbm, dout_ref)], sems)
+    for copy in copies:
+        copy.wait()
     heads, length = cum_ref.shape
     width = x_ref.shape[1]
     spread = head_map(heads, width)
@@ -165,14 +176,14 @@
 
 
 def gate_kernel(s_ref, c_ref, base_ref, esilu_ref, dout_ref, w_ref, gated_ref, cs_ref, sums_ref):
-    hi, lo = split2(load_state(s_ref, 32))
     c_val = c_ref[...]
     length, width = base_ref.shape
     squares = jnp.zeros((length, HALF), F32)
     products = jnp.zeros((length, HALF), F32)
     for q in range(width // 256):
         big = slice(256 * q, 256 * (q + 1))
-        c_state = mm(c_val, hi[:, big]) + mm(c_val, lo[:, big])
+        hi, lo = split2(load_block(s_ref, 32, q))
+        c_state = mm(c_val, hi) + mm(c_val, lo)
         cs_ref[:, big] = c_state
         gated = base_ref[:, big] + esilu_ref[:, big] * c_state
         gated_ref[:, big] = gated
@@ -219,7 +230,7 @@
 
 def grads_kernel(
     cum_ref, scal_ref, gated_ref, silu_ref, ecum_ref, dout_ref, w_ref, x_ref, z_ref, b_ref, c_ref, d_ref, yn_ref, cs_ref, s_ref,
-    gx_ref, gz_ref, gb_ref, gc_ref, gl_ref, dy_ref, dot_ref,
+    gx_ref, gz_hbm, gb_ref, gc_hbm, gl_ref, dy_ref, dot_ref, gz_ref, gc_ref, sems,
 ):
     heads, length = cum_ref.shape
     width = x_ref.shape[1]
@@ -282,62 +293,71 @@
     gb_ref[HALF:, :] = mm2(w_low, c_val[HALF:])
     low_part = mm2(w_right.T, b_val[:HALF]) + mm2(w_low.T, b_val[HALF:])
     gc_ref[...] = far + jnp.concatenate([mm2(w_left.T, b_val[:HALF]), low_part], axis=0)
+    for copy in fetch([(gc_ref, gc_hbm), (gz_ref, gz_hbm)], sems):
+        copy.wait()
 
 
 def final_kernel(
     a_ref, s_ref, cum_ref, tail_ref, x_ref, b_ref, gx_ref, gb_ref, gl_ref,
-    ox_hbm, ob_ref, ol_ref, skip_ref, weight_ref, ox_ref, sems,
+    ox_hbm, ob_hbm, ol_hbm, skip_hbm, weight_hbm, ox_ref, ob_ref, ol_ref, skip_ref, weight_ref, sems,
 ):
     heads, length = cum_ref.shape
     width = x_ref.shape[1]
     spread = head_map(heads, width)
-    after = load_state(a_ref, 34)
-    a_hi, a_lo = split2(after)
-    b_val = b_ref[...]
-    copies = []
-    late = jnp.zeros((heads, length), F32)
-    far = jnp.zeros(ob_ref.shape, F32)
-    for k in range(width // 256):
-        big = slice(256 * k, 256 * (k + 1))
-        tail, x_val = tail_ref[:, big], x_ref[:, big].astype(F32)
-        one_hi, one_lo = a_hi[:, big], a_lo[:, big]
-        b_after = (mm(b_val, one_hi) + mm(b_val, one_lo)) * tail
-        ox_ref[:, big] = (gx_ref[:, big] + b_after).astype(BF16)
-        cols = pl.ds(256 * k, 256)
-        copies.append(pltpu.make_async_copy(ox_ref.at[:, cols], ox_hbm.at[:, cols], sems.at[k]))
-        copies[-1].start()
-        late = late + segment(x_val * b_after, spread[:, big])
-        x_hi, x_lo = split2(x_val * tail)
-        far = far + (mm(x_hi, one_hi, 1, 1) + mm(x_hi, one_lo, 1, 1) + mm(x_lo, one_hi, 1, 1))
-    ob_ref[...] = gb_ref[...] + far
-    start = jnp.broadcast_to(jnp.sum(load_state(s_ref, 32) * after, axis=0, keepdims=True), (HALF, width))
-    hi, mid, lo = split3(start)
-    start = (mm(spread, hi, 1, 1) + mm(spread, mid, 1, 1) + mm(spread, lo, 1, 1))[:, 0:1]
-    whole = jnp.exp(cum_ref[:, length - 1 : length])
-    ol_ref[...] = gl_ref[...] + mm_by(late, triangle(length, lambda i, j: i < j)) + whole * start
+    outs = [(weight_ref, weight_hbm), (skip_ref, skip_hbm), (ol_ref, ol_hbm), (ob_ref, ob_hbm)]
+    outs += zip(quarters(ox_ref), quarters(ox_hbm))
+    copies = [pltpu.make_async_copy(src, dst, sems.at[i]) for i, (src, dst) in enumerate(outs)]
     sums = [a_ref[34 * 4 * q + 32 : 34 * 4 * q + 34, :] for q in range(8)]
     weight_ref[...] = jnp.concatenate([one[0:1, :] for one in sums], axis=0)
+    copies[0].start()
     skip = jnp.concatenate([one[1:2, :] for one in sums], axis=0)
     halves = jnp.where(iota((HALF, heads), 0) // P_SIZE == iota((HALF, heads), 1) % 2, 1.0, 0.0).astype(BF16)
     skip = mm_by(skip, halves)
     skip = jnp.where(iota((8, heads), 1) // 2 == iota((8, heads), 0), skip, 0.0)
     skip_ref[...] = jnp.sum(skip, axis=0, keepdims=True)
+    copies[1].start()
+    b_val = b_ref[...]
+    late = jnp.zeros((heads, length), F32)
+    far = jnp.zeros(ob_ref.shape, F32)
+    starts = []
+    for k in range(width // 256):
+        big = slice(256 * k, 256 * (k + 1))
+        after = load_block(a_ref, 34, k)
+        starts.append(jnp.sum(load_block(s_ref, 32, k) * after, axis=0, keepdims=True))
+        tail, x_val = tail_ref[:, big], x_ref[:, big].astype(F32)
+        a_hi, a_lo = split2(after)
+        b_after = (mm(b_val, a_hi) + mm(b_val, a_lo)) * tail
+        ox_ref[:, big] = (gx_ref[:, big] + b_after).astype(BF16)
+        copies[4 + k].start()
+        late = late + segment(x_val * b_after, spread[:, big])
+        x_hi, x_lo = split2(x_val * tail)
+        far = far + (mm(x_hi, a_hi, 1, 1) + mm(x_hi, a_lo, 1, 1) + mm(x_lo, a_hi, 1, 1))
+    ob_ref[...] = gb_ref[...] + far
+    copies[3].start()
+    start = jnp.broadcast_to(jnp.concatenate(starts, axis=1), (HALF, width))
+    hi, mid, lo = split3(start)
+    start = (mm(spread, hi, 1, 1) + mm(spread, mid, 1, 1) + mm(spread, lo, 1, 1))[:, 0:1]
+    whole = jnp.exp(cum_ref[:, length - 1 : length])
+    ol_ref[...] = gl_ref[...] + mm_by(late, triangle(length, lambda i, j: i < j)) + whole * start
+    copies[2].start()
     for copy in copies:
         copy.wait()
 
 
 def call(kernel, name, outs, *args, flops=0, scratch=(), hbm_in=(), hbm_out=(), mib=16):
     nbytes = sum(a.size * a.dtype.itemsize for a in (*args, *outs))
+    spaces = [pltpu.HBM if i in hbm_in else pltpu.VMEM for i in range(len(args))]
+    out_spaces = [pltpu.HBM if i in hbm_out else pltpu.VMEM for i in range(len(outs))]
     return pl.pallas_call(
         kernel,
         name=name,
-        out_shape=outs,
-        in_specs=[HBM if i in hbm_in else VMEM for i in range(len(args))],
-        out_specs=[HBM if i in hbm_out else VMEM for i in range(len(outs))],
+        out_shape=[space(o.shape, o.dtype) for space, o in zip(out_spaces, outs)],
+        in_specs=[pl.BlockSpec(memory_space=space) for space in spaces],
+        out_specs=[pl.BlockSpec(memory_space=space) for space in out_spaces],
         scratch_shapes=list(scratch),
         compiler_params=pltpu.CompilerParams(vmem_limit_bytes=mib * 1024 * 1024),
         cost_estimate=pl.CostEstimate(flops=flops, bytes_accessed=nbytes, transcendentals=0),
-    )(*args)
+    )(*[pltpu.with_memory_space_constraint(a, space) for a, space in zip(args, spaces)])
 
 
 def exchange(messages, rows):
@@ -357,15 +377,21 @@
     small = shape((heads, length), F32)
     weight = norm_weight.reshape(1, width)
     d_row = d_skip.reshape(1, heads)
-    pieces = [pltpu.VMEM((length, width), BF16), pltpu.SemaphoreType.DMA((4,))]
-
-    pay, cum, tail = call(
-        start_kernel, "start", [shape((chunks * 33, HALF), F32), small, wide], decay_log.T, x_in, b_in,
-        flops=10**9, scratch=pieces, hbm_in=(1,),
+    sem = pltpu.SemaphoreType.DMA
+    narrow = shape(b_in.shape, F32)
+    half_narrow = shape(b_in.shape, BF16)
+
+    pay, cum, tail, x_val, b_val = call(
+        start_kernel, "start", [shape((chunks * 33, HALF), F32), small, wide, half_wide, half_narrow],
+        decay_log.T, x_in, b_in,
+        flops=10**9, scratch=[pltpu.VMEM((heads, length), F32), sem((6,))], hbm_in=(0, 1, 2),
     )
     got = exchange(pay, 33)
-    y_near, base, silu, esilu, ecum = call(
-        local_kernel, "local", [wide] * 5, cum, x_in, b_in, c_in, gate, d_row, flops=8 * 10**9, mib=24
+    y_near, base, silu, esilu, ecum, c_val, z_val, d_val, w_val, dout_val = call(
+        local_kernel, "local",
+        [wide] * 5 + [half_narrow, half_wide, shape(d_row.shape, F32), shape(weight.shape, F32), half_wide],
+        cum, x_val, b_val, c_in, gate, d_row, weight, d_out,
+        flops=8 * 10**9, scratch=[sem((5,))], hbm_in=(3, 4, 5, 6, 7), mib=24,
     )
     spread, decays = call(
         prefix_kernel, "prefix", [shape((chunks * 32, HALF), F32), shape((chunks, HALF), F32)], got
@@ -373,7 +399,7 @@
     before = exchange(spread, 32)
     gated, c_state, sums = call(
         gate_kernel, "gated", [wide, wide, shape((groups, 8, length), F32)],
-        before, c_in, base, esilu, d_out, weight, flops=10**9,
+        before, c_val, base, esilu, dout_val, w_val, flops=10**9,
     )
     sums = lax.all_to_all(sums, "heads", 0, 0)
 
@@ -382,21 +408,23 @@
 
     pay, scalars = call(
         back, "back", [shape((chunks * 34, HALF), F32), shape((length, HALF), F32)],
-        sums, gated, silu, ecum, d_out, weight, x_in, c_in, flops=10**9,
+        sums, gated, silu, ecum, dout_val, w_val, x_val, c_val, flops=10**9,
     )
     got = exchange(pay, 34)
     gx, grad_gate, gb, grad_c, gl = call(
-        grads_kernel, "grads",
-        [wide, half_wide, shape(b_in.shape, F32), shape(c_in.shape, F32), small],
-        cum, scalars, gated, silu, ecum, d_out, weight, x_in, gate, b_in, c_in, d_row, y_near, c_state, before,
-        flops=16 * 10**9, scratch=[pltpu.VMEM((length, width), F32)] * 2, mib=28,
+        grads_kernel, "grads", [wide, half_wide, narrow, narrow, small],
+        cum, scalars, gated, silu, ecum, dout_val, w_val, x_val, z_val, b_val, c_val, d_val, y_near, c_state, before,
+        flops=16 * 10**9, hbm_out=(1, 3), mib=28,
+        scratch=[pltpu.VMEM((length, width), F32)] * 2
+        + [pltpu.VMEM((length, width), BF16), pltpu.VMEM(b_in.shape, F32), sem((2,))],
     )
     (spread,) = call(suffix_kernel, "suffix", [shape((chunks * 34, HALF), F32)], got, decays)
     after = exchange(spread, 34)
+    outs = [half_wide, narrow, small, shape((1, heads), F32), shape((8, HALF), F32)]
     grad_x, grad_b, grad_decay, grad_skip, grad_weight = call(
-        final_kernel, "final",
-        [half_wide, shape(b_in.shape, F32), small, shape((1, heads), F32), shape((8, HALF), F32)],
-        after, before, cum, tail, x_in, b_in, gx, gb, gl, flops=2 * 10**9, scratch=pieces, hbm_out=(0,),
+        final_kernel, "final", outs,
+        after, before, cum, tail, x_val, b_val, gx, gb, gl,
+        flops=2 * 10**9, scratch=[pltpu.VMEM(o.shape, o.dtype) for o in outs] + [sem((8,))], hbm_out=range(5),
     )
     return (
         grad_x,

time: 113 us -> 112 us (level)
  Pallas kernels: 17.3 us -> 19.3 us
  local copies, waits for them, and re-layouts: 27.2 us -> 25.6 us
  waiting for transfers between devices: 4.28 us -> 2.97 us
    pallas_call x8, Pallas kernels: 17.3 us -> 19.3 us  [call(): pl.pallas_call(kernel, name=name, out_shape=[space(o.shape, o.dtype) for...]
    unnamed x66 -> x58, local copies, waits for them, and re-layouts: 27.2 us -> 25.6 us
    all_to_all x2, waiting for transfers between devices: 4.28 us -> 2.97 us  [exchange(): got = lax.all_to_all(messages.reshape(count, 1, rows * HALF), CHUNKS, 0, 0)]
  transfers between devices with their start and end apart: 2 -> 2, of which waited for: 1 -> 1; matrix products, arithmetic and copies ran while one was open for 0% -> 0% of each run, Pallas kernels for 7% -> 9%
where the time goes in v3:
time: 112 us; the launch traced here: 110 us
  blocking collectives  51.8 us (46%)
  local copies, waits for them, and re-layouts  25.6 us (23%)
  Pallas kernels  19.3 us (17%)
  starting transfers between devices  9.84 us (9%)
  waiting for transfers between devices  2.97 us (3%)
    all_to_all x2, blocking collectives, exchange(): got = lax.all_to_all(messages.reshape(count, 1, rows * HALF), CHUNKS, 0, 0)  36.6 us
    unnamed x58, local copies, waits for them, and re-layouts  25.6 us
    pallas_call x8, Pallas kernels, call(): pl.pallas_call(kernel, name=name, out_shape=[space(o.shape, o.dtype) for...  19.3 us
    all_to_all x1, blocking collectives, on_device(): sums = lax.all_to_all(sums, 'heads', 0, 0)  15.2 us
    all_to_all x2, starting transfers between devices, exchange(): got = lax.all_to_all(messages.reshape(count, 1, rows * HALF), CHUNKS, 0, 0)  9.84 us
    all_to_all x2, waiting for transfers between devices, exchange(): got = lax.all_to_all(messages.reshape(count, 1, rows * HALF), CHUNKS, 0, 0)  2.97 us
  transfers between devices with their start and end apart: 2, of which 1 were waited for; matrix products, arithmetic and copies ran while one was open for 0% of the time, Pallas kernels for 9%

profile of v3, /device:TPU:1, one launch (start us, length us, event | category | flops | bytes accessed | tf_op | source)
XLA Modules:
  0.0 110.4 jit_solution(16496011287725150755)
XLA Ops:
  0.6 2.8 %start.1 = (f32[1056,128]{1,0:T(8,128)S(1)}, f32[16,256]{1,0:T(8,128)S(1)}, f32[256,1024]{1,0:T(8,128)S(1)}, bf16[256,1024]{1,0:T(8,128)(2,1)S(1)}, bf16[256,128]{1,0:T(8,128)(2,1)S(1)}) custom-call(f32[16,256]{1,0:T(8,128)} %bitcast.21, bf16[256,1024]{1,0:T(8,128)(2,1)} %x_hbm.1, bf16[256,128]{1,0:T(8,128)(2,1)} %b_hbm.1), custom_call_target="tpu_custom_call" | custom-call | flops 1000000000 | bytes 2801664 | tf_op jit(solution)/shard_map/start/pallas_call | solution.py:351
  4.5 19.5 %all_to_all.25 = f32[32,1,4224]{2,1,0:T(1,128)S(1)} all-to-all(f32[32,1,4224]{2,1,0:T(1,128)S(1)} %bitcast.17), channel_id=1, replica_groups=mesh['outer'=8,'inner'=4,'heads'=8] {'outer','inner'}, dimensions={0} | all-to-all | bytes 1081344 | tf_op jit(solution)/shard_map/all_to_all | solution.py:365
  24.9 4.6 %all-to-all-start.1 = ((f32[32,1,4096]{2,1,0:T(1,128)}), f32[32,1,4096]{2,1,0:T(1,128)S(1)}, u32[]{:S(2)}, u32[]{:S(2)}) async-start(f32[32,1,4096]{2,1,0:T(1,128)} %bitcast.3), calls=%async_computation.1 | async-start | bytes 1048576 | tf_op jit(solution)/shard_map/all_to_all | solution.py:365
  29.5 3.6 %local.1 = (f32[256,1024]{1,0:T(8,128)S(1)}, f32[256,1024]{1,0:T(8,128)S(1)}, f32[256,1024]{1,0:T(8,128)S(1)}, f32[256,1024]{1,0:T(8,128)S(1)}, f32[256,1024]{1,...) custom-call(f32[16,256]{1,0:T(8,128)S(1)} %get-tuple-element.41.cum_, ...), custom_call_target="tpu_custom_call" | custom-call | flops 8000000000 | bytes 8085632 | tf_op jit(solution)/shard_map/local/pallas_call | solution.py:351
  37.6 3.0 %all-to-all-done.1 = f32[32,1,4096]{2,1,0:T(1,128)S(1)} async-done(((f32[32,1,4096]{2,1,0:T(1,128)}), f32[32,1,4096]{2,1,0:T(1,128)S(1)}, u32[]{:S(2)}, u32[]{:S(2)}) %all-to-all-start.1) | async-done | bytes 524320 | tf_op jit(solution)/shard_map/all_to_all | solution.py:365
  41.4 1.0 copy-done.5
  42.4 1.0 copy-done.9
  43.5 1.2 %copy-done.15 = f32[256,1024]{1,0:T(8,128)S(1)} copy-done((f32[256,1024]{1,0:T(8,128)S(1)}, f32[256,1024]{1,0:T(8,128)}, u32[]{:S(2)}) %copy-start.15) | copy-done | bytes 1048600
  44.7 1.2 %copy-done.17 = f32[256,1024]{1,0:T(8,128)S(1)} copy-done((f32[256,1024]{1,0:T(8,128)S(1)}, f32[256,1024]{1,0:T(8,128)}, u32[]{:S(2)}) %copy-start.17) | copy-done | bytes 1048600
  47.5 15.2 %all_to_all.26.refs_0_ = f32[8,8,256]{2,1,0:T(8,128)S(1)} all-to-all(f32[8,8,256]{2,1,0:T(8,128)S(1)} %get-tuple-element.49), channel_id=1, replica_groups=mesh['outer'=8,'inner'=4,'heads'=8] {'heads'}, dimensions={0} | all-to-all | bytes 131072 | tf_op jit(solution)/shard_map/all_to_all | solution.py:404
  63.7 17.1 %all_to_all.27 = f32[32,1,4352]{2,1,0:T(1,128)S(1)} all-to-all(f32[32,1,4352]{2,1,0:T(1,128)S(1)} %bitcast.16), channel_id=1, replica_groups=mesh['outer'=8,'inner'=4,'heads'=8] {'outer','inner'}, dimensions={0} | all-to-all | bytes 1114112 | tf_op jit(solution)/shard_map/all_to_all | solution.py:365
  81.6 5.3 %all-to-all-start.4 = ((f32[32,1,4352]{2,1,0:T(1,128)}), f32[32,1,4352]{2,1,0:T(1,128)}, u32[]{:S(2)}, u32[]{:S(2)}) async-start(f32[32,1,4352]{2,1,0:T(1,128)} %bitcast.9), calls=%async_computation.4 | async-start | bytes 1114112 | tf_op jit(solution)/shard_map/all_to_all | solution.py:365
  86.9 1.0 copy-done.2
  87.9 1.0 copy-done.7
  89.0 1.0 copy-done.10
  90.0 1.2 %copy-done.13 = f32[256,1024]{1,0:T(8,128)S(1)} copy-done((f32[256,1024]{1,0:T(8,128)S(1)}, f32[256,1024]{1,0:T(8,128)}, u32[]{:S(2)}) %copy-start.13) | copy-done | bytes 1048600
  92.1 1.2 %copy-done.26 = f32[256,1024]{1,0:T(8,128)S(1)} copy-done((f32[256,1024]{1,0:T(8,128)S(1)}, f32[256,1024]{1,0:T(8,128)}, u32[]{:S(2)}) %copy-start.26) | copy-done | bytes 1048600
  93.3 1.0 copy-done.28
  94.3 5.9 %grads.1 = (f32[256,1024]{1,0:T(8,128)S(1)}, bf16[256,1024]{1,0:T(8,128)(2,1)}, f32[256,128]{1,0:T(8,128)S(1)}, f32[256,128]{1,0:T(8,128)}, f32[16,256]{1,0:T(8,128)S(1)}) custom-call(f32[16,256]{1,0:T(8,128)S(1)} %get-tuple-element.41.cum_ref, f32[256,128]{1,0:T(8,128)S(1)} %get-tuple-element.56.scal_ref, ...), custom_call_target="tpu_custom_call" | custom-call | flops 16000000000 | bytes 9474112 | tf_op jit(solution)/shard_map/grads/pallas_call | solution.py:351
  101.2 1.0 copy-done.3
  102.3 1.0 copy-done.11
  103.3 1.2 %copy-done.19 = f32[256,1024]{1,0:T(8,128)S(1)} copy-done((f32[256,1024]{1,0:T(8,128)S(1)}, f32[256,1024]{1,0:T(8,128)}, u32[]{:S(2)}) %copy-start.19) | copy-done | bytes 1048600
  104.5 1.2 %copy-done.21 = f32[256,1024]{1,0:T(8,128)S(1)} copy-done((f32[256,1024]{1,0:T(8,128)S(1)}, f32[256,1024]{1,0:T(8,128)}, u32[]{:S(2)}) %copy-start.21) | copy-done | bytes 1048600
  106.6 3.7 %final.1 = (bf16[256,1024]{1,0:T(8,128)(2,1)}, f32[256,128]{1,0:T(8,128)}, f32[16,256]{1,0:T(8,128)}, f32[1,16]{1,0:T(1,128)}, f32[8,128]{1,0:T(8,128)}) custom-call(f32[1088,128]{1,0:T(8,128)} %bitcast.10.a_ref, f32[1024,128]{1,0:T(8,128)S(1)} %bitcast.20, f32[16,256]{1,0:T(8,128)S(1)} %get-tuple-element.41.cum_ref, f32[256,1024]{1,0:T(8,128)S(1)} %copy-done.19, ...), custom_call_target="tpu_custom_call" | custom-call | flops 2000000000 | bytes 4608064 | tf_op jit(solution)/shard_map/final/pallas_call | solution.py:351
  (49 shorter events, 13.3 us)
Async XLA Ops:
  3.5 1.0 copy-start.18
  4.5 25.0 %copy-start = (bf16[256,1024]{1,0:T(8,128)(2,1)}, bf16[256,1024]{1,0:T(8,128)(2,1)S(1)}, u32[]{:S(2)}) copy-start(bf16[256,1024]{1,0:T(8,128)(2,1)S(1)} %get-tuple-element.42.x_ref.refs_6_) | copy-start | bytes 1572868
  4.5 25.0 %copy-start.22 = (bf16[256,128]{1,0:T(8,128)(2,1)}, bf16[256,128]{1,0:T(8,128)(2,1)S(1)}, u32[]{:S(2)}) copy-start(bf16[256,128]{1,0:T(8,128)(2,1)S(1)} %get-tuple-element.43.b_ref) | copy-start | bytes 196612
  24.9 15.7 %all-to-all-start.1 = ((f32[32,1,4096]{2,1,0:T(1,128)}), f32[32,1,4096]{2,1,0:T(1,128)S(1)}, u32[]{:S(2)}, u32[]{:S(2)}) async-start(f32[32,1,4096]{2,1,0:T(1,128)} %bitcast.3), calls=%async_computation.1 | async-start | bytes 1048576 | tf_op jit(solution)/shard_map/all_to_all | solution.py:365
  33.8 1.0 copy-start.14
  34.8 1.0 copy-start.16
  41.4 1.0 copy-start.5
  42.4 1.0 copy-start.9
  43.5 1.2 %copy-start.15 = (f32[256,1024]{1,0:T(8,128)S(1)}, f32[256,1024]{1,0:T(8,128)}, u32[]{:S(2)}) copy-start(f32[256,1024]{1,0:T(8,128)} %copy-done.14) | copy-start | bytes 3145732
  44.7 1.2 %copy-start.17 = (f32[256,1024]{1,0:T(8,128)S(1)}, f32[256,1024]{1,0:T(8,128)}, u32[]{:S(2)}) copy-start(f32[256,1024]{1,0:T(8,128)} %copy-done.16) | copy-start | bytes 3145732
  45.9 16.8 %copy-start.1 = (bf16[256,1024]{1,0:T(8,128)(2,1)S(1)}, bf16[256,1024]{1,0:T(8,128)(2,1)}, u32[]{:S(2)}) copy-start(bf16[256,1024]{1,0:T(8,128)(2,1)} %copy-done) | copy-start | bytes 1572868
  45.9 16.8 %copy-start.6 = (bf16[256,1024]{1,0:T(8,128)(2,1)S(1)}, bf16[256,1024]{1,0:T(8,128)(2,1)}, u32[]{:S(2)}) copy-start(bf16[256,1024]{1,0:T(8,128)(2,1)} %copy-done.4) | copy-start | bytes 1572868
  46.5 1.0 copy-start.12
  81.6 19.6 %all-to-all-start.4 = ((f32[32,1,4352]{2,1,0:T(1,128)}), f32[32,1,4352]{2,1,0:T(1,128)}, u32[]{:S(2)}, u32[]{:S(2)}) async-start(f32[32,1,4352]{2,1,0:T(1,128)} %bitcast.9), calls=%async_computation.4 | async-start | bytes 1114112 | tf_op jit(solution)/shard_map/all_to_all | solution.py:365
  86.9 1.0 copy-start.2
  87.9 1.0 copy-start.7
  89.0 1.0 copy-start.10
  90.0 1.2 %copy-start.13 = (f32[256,1024]{1,0:T(8,128)S(1)}, f32[256,1024]{1,0:T(8,128)}, u32[]{:S(2)}) copy-start(f32[256,1024]{1,0:T(8,128)} %copy-done.12) | copy-start | bytes 3145732
  92.1 1.2 %copy-start.26 = (f32[256,1024]{1,0:T(8,128)S(1)}, f32[256,1024]{1,0:T(8,128)}, u32[]{:S(2)}) copy-start(f32[256,1024]{1,0:T(8,128)} %copy-done.25) | copy-start | bytes 3145732
  93.3 1.0 copy-start.28
  101.2 1.0 copy-start.3
  102.3 1.0 copy-start.11
  103.3 1.2 %copy-start.19 = (f32[256,1024]{1,0:T(8,128)S(1)}, f32[256,1024]{1,0:T(8,128)}, u32[]{:S(2)}) copy-start(f32[256,1024]{1,0:T(8,128)} %copy-done.18) | copy-start | bytes 3145732
  104.5 1.2 %copy-start.21 = (f32[256,1024]{1,0:T(8,128)S(1)}, f32[256,1024]{1,0:T(8,128)}, u32[]{:S(2)}) copy-start(f32[256,1024]{1,0:T(8,128)} %copy-done.20) | copy-start | bytes 3145732
  (7 other events, 6.0 us)

commit v4 on v3

v4 whole, which is shorter than its diff:
```python
import jax
import jax.numpy as jnp
from jax import lax
from jax.experimental import pallas as pl
from jax.experimental.pallas import tpu as pltpu
from jax.sharding import PartitionSpec as P

P_SIZE = 64
EPS = 1e-05
F32 = jnp.float32
BF16 = jnp.bfloat16
CHUNKS = ("outer", "inner")
HALF = 128


def mm(a, b, ca=1, cb=0):
    return lax.dot_general(a, b, (((ca,), (cb,)), ((), ())), preferred_element_type=F32)


def split2(a):
    hi = a.astype(BF16)
    return hi, (a - hi.astype(F32)).astype(BF16)


def split3(a):
    hi = a.astype(BF16)
    rest = a - hi.astype(F32)
    mid = rest.astype(BF16)
    return hi, mid, (rest - mid.astype(F32)).astype(BF16)


def mm2(a, b, ca=1, cb=0):
    hi, lo = split2(a)
    return mm(hi, b, ca, cb) + mm(lo, b, ca, cb)


def iota(shape, dim):
    return lax.broadcasted_iota(jnp.int32, shape, dim)


def head_map(heads, width):
    return jnp.where(iota((heads, width), 1) // P_SIZE == iota((heads, width), 0), 1.0, 0.0).astype(BF16)


def expand(a, spread, ca=1):
    hi, lo = split2(a)
    return mm(hi, spread, ca) + mm(lo, spread, ca)


def segment(a, spread):
    hi, lo = split2(a)
    return mm(spread, hi, 1, 1) + mm(spread, lo, 1, 1)


def triangle(n, keep):
    return jnp.where(keep(iota((n, n), 0), iota((n, n), 1)), 1.0, 0.0).astype(BF16)


def mm_by(a, tri):
    hi, mid, lo = split3(a)
    return mm(hi, tri) + mm(mid, tri) + mm(lo, tri)


def load_block(ref, rows, k):
    cols = []
    for q in (2 * k, 2 * k + 1):
        at = [rows * (4 * q + r) for r in range(4)]
        cols.append(jnp.concatenate([ref[i : i + 32, :] for i in at], axis=0))
    return jnp.concatenate(cols, axis=1)


def copies_of(pairs, sems):
    return [pltpu.make_async_copy(src, dst, sems.at[i]) for i, (src, dst) in enumerate(pairs)]


def fetch(pairs, sems):
    copies = copies_of(pairs, sems)
    for copy in copies:
        copy.start()
    return copies


def quarters(ref):
    return [ref.at[:, pl.ds(256 * k, 256)] for k in range(4)]


def block_sums(lt):
    return mm_by(lt, triangle(lt.shape[1], lambda i, j: i <= j))


def skip_row(d_ref, spread):
    heads, width = spread.shape
    hi, mid, lo = split3(jnp.broadcast_to(d_ref[...], (8, heads)))
    return (mm(hi, spread) + mm(mid, spread) + mm(lo, spread))[0:1, :]


def start_kernel(lt_hbm, x_hbm, b_hbm, pay_ref, lt_ref, b_ref, x_ref, sems):
    heads, length = lt_hbm.shape
    width = x_hbm.shape[1]
    pairs = [(lt_hbm, lt_ref), (b_hbm, b_ref)] + list(zip(quarters(x_hbm), quarters(x_ref)))
    first, second, *copies = fetch(pairs, sems)
    spread = head_map(heads, width)
    first.wait()
    cum = block_sums(lt_ref[...])
    last = cum[:, length - 1 : length]
    tail = expand(jnp.exp(last - cum), spread, 0)
    whole = expand(jnp.broadcast_to(jnp.exp(last), (heads, HALF)), spread, 0)[0:1, :]
    second.wait()
    b_val = b_ref[...]
    for k in range(4):
        copies[k].wait()
        big = slice(256 * k, 256 * (k + 1))
        hi, lo = split2(x_ref[:, big].astype(F32) * tail[:, big])
        state = mm(b_val, hi, 0, 0) + mm(b_val, lo, 0, 0)
        for q in (2 * k, 2 * k + 1):
            for r in range(4):
                at = 33 * (4 * q + r)
                off = HALF * (q - 2 * k)
                pay_ref[at : at + 32, :] = state[32 * r : 32 * r + 32, off : off + HALF]
                pay_ref[at + 32 : at + 33, :] = whole[:, HALF * q : HALF * (q + 1)]


def local_kernel(
    lt_hbm, x_hbm, b_hbm, c_hbm, z_hbm, d_hbm, w_hbm, dout_hbm,
    base_ref, esilu_ref, c_ref, w_ref, dout_ref, yn_hbm,
    lt_ref, x_ref, b_ref, z_ref, d_ref, yn_ref, sems,
):
    heads, length = lt_hbm.shape
    width = x_hbm.shape[1]
    copies = fetch(
        [(lt_hbm, lt_ref), (b_hbm, b_ref), (c_hbm, c_ref), (x_hbm, x_ref), (z_hbm, z_ref), (d_hbm, d_ref),
         (w_hbm, w_ref), (dout_hbm, dout_ref)],
        sems,
    )
    outs = [
        pltpu.make_async_copy(src, dst, sems.at[8 + k])
        for k, (src, dst) in enumerate(zip(quarters(yn_ref), quarters(yn_hbm)))
    ]
    spread = head_map(heads, width)
    for copy in copies[:3]:
        copy.wait()
    cum_t = block_sums(lt_ref[...])
    cum = cum_t.T
    ecum = expand(jnp.exp(cum_t), spread, 0)
    inner = mm(c_ref[...], b_ref[...], 1, 1)
    top, left, right = inner[:HALF, :HALF], inner[HALF:, :HALF], inner[HALF:, HALF:]
    lower = iota((HALF, HALF), 0) >= iota((HALF, HALF), 1)
    first = iota((length, HALF), 1) < P_SIZE
    for copy in copies[3:6]:
        copy.wait()
    skip = skip_row(d_ref, spread)
    for q in range(width // HALF):
        cols = slice(HALF * q, HALF * (q + 1))
        x_pair = x_ref[:, cols]
        parts = []
        for h in (2 * q, 2 * q + 1):
            col, row = cum[:, h : h + 1], cum_t[h : h + 1, :]
            up = jnp.where(lower, jnp.exp(col[:HALF] - row[:, :HALF]), 0.0) * top
            dl = jnp.exp(col[HALF:] - row[:, :HALF]) * left
            dr = jnp.where(lower, jnp.exp(col[HALF:] - row[:, HALF:]), 0.0) * right
            down = jnp.concatenate([dl, dr], axis=1)
            parts.append(jnp.concatenate([mm2(up, x_pair[:HALF]), mm2(down, x_pair)], axis=0))
        yn = jnp.where(first, parts[0], parts[1])
        yn_ref[:, cols] = yn
        if q % 2 == 1:
            outs[q // 2].start()
        z_val = z_ref[:, cols].astype(F32)
        silu = z_val * (1.0 / (1.0 + jnp.exp(-z_val)))
        esilu_ref[:, cols] = ecum[:, cols] * silu
        base_ref[:, cols] = (yn + skip[:, cols] * x_pair.astype(F32)) * silu
    for copy in copies[6:] + outs:
        copy.wait()


def prefix_kernel(in_ref, out_ref, dec_ref):
    count = dec_ref.shape[0]
    state = jnp.zeros((32, HALF), F32)
    for p in range(count):
        out_ref[32 * p : 32 * p + 32, :] = state
        decay = in_ref[33 * p + 32 : 33 * p + 33, :]
        dec_ref[p : p + 1, :] = decay
        if p < count - 1:
            state = decay * state + in_ref[33 * p : 33 * p + 32, :]


def gate_kernel(s_ref, c_ref, base_ref, esilu_ref, dout_ref, w_ref, gated_ref, sums_ref):
    c_val = c_ref[...]
    length, width = base_ref.shape
    squares = jnp.zeros((length, HALF), F32)
    products = jnp.zeros((length, HALF), F32)
    for q in range(width // 256):
        big = slice(256 * q, 256 * (q + 1))
        hi, lo = split2(load_block(s_ref, 32, q))
        c_state = mm(c_val, hi) + mm(c_val, lo)
        gated = base_ref[:, big] + esilu_ref[:, big] * c_state
        gated_ref[:, big] = gated
        sq = gated * gated
        pr = dout_ref[:, big].astype(F32) * w_ref[:, big] * gated
        squares = squares + sq[:, :HALF] + sq[:, HALF:]
        products = products + pr[:, :HALF] + pr[:, HALF:]
    sq_row = jnp.sum(squares.T, axis=0, keepdims=True)
    pr_row = jnp.sum(products.T, axis=0, keepdims=True)
    tile = jnp.concatenate([sq_row, pr_row, jnp.zeros((6, length), F32)], axis=0)
    for i in range(sums_ref.shape[0]):
        sums_ref[i] = tile


def back_kernel(
    channels, sums_ref, gated_ref, esilu_ref, dout_ref, w_ref, c_ref, s_ref,
    pay_ref, scal_hbm, s_hbm, scal_ref, sems,
):
    length, width = gated_ref.shape
    scal_copy, s_copy = copies_of([(scal_ref, scal_hbm), (s_ref, s_hbm)], sems)
    s_copy.start()
    total = sums_ref[0]
    for i in range(1, sums_ref.shape[0]):
        total = total + sums_ref[i]
    squares, products = total[0:1, :], total[1:2, :]
    inv = lax.rsqrt(squares / channels + EPS)
    fall = inv * inv * inv * products / channels
    rows = jnp.concatenate([inv, fall, jnp.zeros((6, length), F32)], axis=0)
    scal_ref[...] = rows
    scal_copy.start()
    both = jnp.concatenate([rows, jnp.zeros((HALF - 8, length), F32)], axis=0).T
    inv_col, fall_col = both[:, 0:1], both[:, 1:2]
    c_val = c_ref[...]
    for k in range(width // 256):
        big = slice(256 * k, 256 * (k + 1))
        gated = gated_ref[:, big]
        d_inv = dout_ref[:, big].astype(F32) * inv_col
        weight = jnp.sum(d_inv * gated, axis=0, keepdims=True)
        hi, lo = split2((d_inv * w_ref[:, big] - gated * fall_col) * esilu_ref[:, big])
        back = mm(c_val, hi, 0, 0) + mm(c_val, lo, 0, 0)
        for q in (2 * k, 2 * k + 1):
            off = HALF * (q - 2 * k)
            for r in range(4):
                at = 33 * (4 * q + r)
                pay_ref[at : at + 32, :] = back[32 * r : 32 * r + 32, off : off + HALF]
                pay_ref[at + 32 : at + 33, :] = weight[:, off : off + HALF]
    scal_copy.wait()
    s_copy.wait()


def grads_kernel(
    lt_hbm, scal_hbm, dout_hbm, w_hbm, x_hbm, z_hbm, b_hbm, c_hbm, d_hbm, yn_hbm, s_hbm,
    gx_ref, gb_ref, gl_ref, tail_ref, x_ref, s_ref, b_ref, skip_ref, gz_hbm, gc_hbm,
    lt_ref, scal_ref, dout_ref, w_ref, z_ref, c_ref, d_ref, yn_ref, dye_ref, dot_ref, gz_ref, gc_ref, sems,
):
    heads, length = lt_hbm.shape
    width = x_hbm.shape[1]
    copies = fetch(
        [(lt_hbm, lt_ref), (scal_hbm, scal_ref), (b_hbm, b_ref), (c_hbm, c_ref), (d_hbm, d_ref), (w_hbm, w_ref),
         (x_hbm, x_ref), (s_hbm, s_ref), (yn_hbm, yn_ref), (z_hbm, z_ref), (dout_hbm, dout_ref)],
        sems,
    )
    outs = [
        pltpu.make_async_copy(src, dst, sems.at[11 + k])
        for k, (src, dst) in enumerate([(gc_ref, gc_hbm), *zip(quarters(gz_ref), quarters(gz_hbm))])
    ]
    spread = head_map(heads, width)
    for copy in copies[:6]:
        copy.wait()
    cum_t = block_sums(lt_ref[...])
    cum = cum_t.T
    last = cum_t[:, length - 1 : length]
    ecum = expand(jnp.exp(cum_t), spread, 0)
    tail_ref[...] = expand(jnp.exp(last - cum_t), spread, 0)
    both = jnp.concatenate([scal_ref[...], jnp.zeros((HALF - 8, length), F32)], axis=0).T
    inv_col, fall_col = both[:, 0:1], both[:, 1:2]
    skip = skip_row(d_ref, spread)
    b_val, c_val = b_ref[...], c_ref[...]
    inner_t = mm(b_val, c_val, 1, 1)
    left, right, low = inner_t[:HALF, :HALF], inner_t[:HALF, HALF:], inner_t[HALF:, HALF:]
    upper = iota((HALF, HALF), 0) <= iota((HALF, HALF), 1)
    first = iota((length, HALF), 1) < P_SIZE
    w_left = jnp.zeros((HALF, HALF), F32)
    w_right = jnp.zeros((HALF, HALF), F32)
    w_low = jnp.zeros((HALF, HALF), F32)
    skips = []
    far = jnp.zeros((length, HALF), F32)
    for copy in copies[6:]:
        copy.wait()
    for q in range(width // HALF):
        cols = slice(HALF * q, HALF * (q + 1))
        x_pair = x_ref[:, cols]
        x_val = x_pair.astype(F32)
        z_val = z_ref[:, cols].astype(F32)
        sig = 1.0 / (1.0 + jnp.exp(-z_val))
        silu = z_val * sig
        if q % 2 == 0:
            s_hi, s_lo = split2(load_block(s_ref, 32, q // 2))
            c_state = mm(c_val, s_hi) + mm(c_val, s_lo)
        off = slice(HALF * (q % 2), HALF * (q % 2 + 1))
        y_near = yn_ref[:, cols] + ecum[:, cols] * c_state[:, off]
        y_val = y_near + skip[:, cols] * x_val
        d_gated = inv_col * (dout_ref[:, cols].astype(F32) * w_ref[:, cols]) - y_val * silu * fall_col
        dy = d_gated * silu
        dye_ref[:, cols] = dy * ecum[:, cols]
        gz_ref[:, cols] = (d_gated * y_val * sig * (1.0 + z_val * (1.0 - sig))).astype(BF16)
        if q % 2 == 1:
            outs[1 + q // 2].start()
            e_hi, e_lo = split2(dye_ref[:, 128 * q - 128 : 128 * q + 128])
            far = far + (mm(e_hi, s_hi, 1, 1) + mm(e_hi, s_lo, 1, 1) + mm(e_lo, s_hi, 1, 1))
        skips.append(jnp.sum(dy * x_val, axis=0, keepdims=True))
        hi, lo = split2(dy)
        parts = []
        for k in range(2):
            h = 2 * q + k
            col, row = cum[:, h : h + 1], cum_t[h : h + 1, :]
            x_one = jnp.where(first if k == 0 else ~first, x_val, 0.0).astype(BF16)
            dec_left = jnp.where(upper, jnp.exp(row[:, :HALF] - col[:HALF]), 0.0)
            dec_right = jnp.exp(row[:, HALF:] - col[:HALF])
            dec_low = jnp.where(upper, jnp.exp(row[:, HALF:] - col[HALF:]), 0.0)
            dot_up = mm(x_one[:HALF], hi, 1, 1) + mm(x_one[:HALF], lo, 1, 1)
            dot_low = mm(x_one[HALF:], hi[HALF:], 1, 1) + mm(x_one[HALF:], lo[HALF:], 1, 1)
            w_left = w_left + dec_left * dot_up[:, :HALF]
            w_right = w_right + dec_right * dot_up[:, HALF:]
            w_low = w_low + dec_low * dot_low
            mix_up = jnp.concatenate([dec_left * left, dec_right * right], axis=1)
            mix_low = dec_low * low
            up_hi, up_lo = split2(mix_up)
            low_hi, low_lo = split2(mix_low)
            g_up = mm(up_hi, hi) + mm(up_hi, lo) + mm(up_lo, hi)
            g_low = mm(low_hi, hi[HALF:]) + mm(low_hi, lo[HALF:]) + mm(low_lo, hi[HALF:])
            parts.append(jnp.concatenate([g_up, g_low], axis=0))
        g_near = jnp.where(first, parts[0], parts[1])
        gx_ref[:, cols] = g_near + skip[:, cols] * dy
        dot_ref[:, cols] = dy * y_near - x_val * g_near
    w_up = jnp.concatenate([w_left, w_right], axis=1)
    low_part = mm2(w_right.T, b_val[:HALF]) + mm2(w_low.T, b_val[HALF:])
    gc_ref[...] = far + jnp.concatenate([mm2(w_left.T, b_val[:HALF]), low_part], axis=0)
    outs[0].start()
    gl_ref[...] = mm_by(segment(dot_ref[...], spread), triangle(length, lambda i, j: i >= j))
    gb_ref[:HALF, :] = mm2(w_up, c_val)
    gb_ref[HALF:, :] = mm2(w_low, c_val[HALF:])
    hi, mid, lo = split3(jnp.broadcast_to(jnp.concatenate(skips, axis=1), (8, width)))
    wide = head_map(HALF, width)
    skip_ref[...] = mm(hi, wide, 1, 1) + mm(mid, wide, 1, 1) + mm(lo, wide, 1, 1)
    for copy in outs:
        copy.wait()


def suffix_kernel(in_ref, dec_ref, skip_ref, out_ref):
    count = dec_ref.shape[0]
    state = jnp.zeros((32, HALF), F32)
    sums = in_ref[32:33, :]
    for p in range(1, count):
        sums = sums + in_ref[33 * p + 32 : 33 * p + 33, :]
    rows = jnp.concatenate([sums, skip_ref[0:1, :]], axis=0)
    for p in range(count - 1, -1, -1):
        out_ref[34 * p : 34 * p + 32, :] = state
        out_ref[34 * p + 32 : 34 * p + 34, :] = rows
        if p > 0:
            state = dec_ref[p : p + 1, :] * state + in_ref[33 * p : 33 * p + 32, :]


def final_kernel(
    a_ref, s_ref, lt_hbm, tail_ref, x_ref, b_ref, gx_ref, gb_ref, gl_ref,
    ox_hbm, ob_hbm, ol_hbm, skip_hbm, weight_hbm, ox_ref, ob_ref, ol_ref, skip_ref, weight_ref, lt_ref, sems,
):
    heads, length = lt_hbm.shape
    width = x_ref.shape[1]
    spread = head_map(heads, width)
    outs = [(weight_ref, weight_hbm), (skip_ref, skip_hbm), (ol_ref, ol_hbm), (ob_ref, ob_hbm)]
    outs += zip(quarters(ox_ref), quarters(ox_hbm))
    copies = copies_of(outs + [(lt_hbm, lt_ref)], sems)
    copies[8].start()
    weight_ref[...] = jnp.concatenate([a_ref[136 * q + 32 : 136 * q + 33, :] for q in range(8)], axis=0)
    copies[0].start()
    skip = a_ref[33:34, :]
    for p in range(1, a_ref.shape[0] // 34):
        skip = skip + a_ref[34 * p + 33 : 34 * p + 34, :]
    skip_ref[...] = skip[:, :heads]
    copies[1].start()
    b_val = b_ref[...]
    late = jnp.zeros((heads, length), F32)
    far = jnp.zeros(ob_ref.shape, F32)
    starts = []
    for k in range(width // 256):
        big = slice(256 * k, 256 * (k + 1))
        after = load_block(a_ref, 34, k)
        starts.append(jnp.sum(load_block(s_ref, 32, k) * after, axis=0, keepdims=True))
        tail, x_val = tail_ref[:, big], x_ref[:, big].astype(F32)
        a_hi, a_lo = split2(after)
        b_after = (mm(b_val, a_hi) + mm(b_val, a_lo)) * tail
        ox_ref[:, big] = (gx_ref[:, big] + b_after).astype(BF16)
        copies[4 + k].start()
        late = late + segment(x_val * b_after, spread[:, big])
        x_hi, x_lo = split2(x_val * tail)
        far = far + (mm(x_hi, a_hi, 1, 1) + mm(x_hi, a_lo, 1, 1) + mm(x_lo, a_hi, 1, 1))
    ob_ref[...] = gb_ref[...] + far
    copies[3].start()
    start = jnp.broadcast_to(jnp.concatenate(starts, axis=1), (HALF, width))
    hi, mid, lo = split3(start)
    start = (mm(spread, hi, 1, 1) + mm(spread, mid, 1, 1) + mm(spread, lo, 1, 1))[:, 0:1]
    copies[8].wait()
    whole = jnp.exp(jnp.sum(lt_ref[...], axis=1, keepdims=True))
    ol_ref[...] = gl_ref[...] + mm_by(late, triangle(length, lambda i, j: i < j)) + whole * start
    copies[2].start()
    for copy in copies[:8]:
        copy.wait()


def call(kernel, name, outs, *args, flops=0, scratch=(), hbm_in=(), hbm_out=(), mib=16):
    nbytes = sum(a.size * a.dtype.itemsize for a in (*args, *outs))
    spaces = [pltpu.HBM if i in hbm_in else pltpu.VMEM for i in range(len(args))]
    out_spaces = [pltpu.HBM if i in hbm_out else pltpu.VMEM for i in range(len(outs))]
    return pl.pallas_call(
        kernel,
        name=name,
        out_shape=[space(o.shape, o.dtype) for space, o in zip(out_spaces, outs)],
        in_specs=[pl.BlockSpec(memory_space=space) for space in spaces],
        out_specs=[pl.BlockSpec(memory_space=space) for space in out_spaces],
        scratch_shapes=list(scratch),
        compiler_params=pltpu.CompilerParams(vmem_limit_bytes=mib * 1024 * 1024),
        cost_estimate=pl.CostEstimate(flops=flops, bytes_accessed=nbytes, transcendentals=0),
    )(*[pltpu.with_memory_space_constraint(a, space) for a, space in zip(args, spaces)])


def exchange(messages, rows):
    count = lax.axis_size(CHUNKS)
    got = lax.all_to_all(messages.reshape(count, 1, rows * HALF), CHUNKS, 0, 0)
    return got.reshape(count * rows, HALF)


def on_device(x_in, b_in, c_in, decay_log, d_skip, gate, norm_weight, d_out):
    length, heads = decay_log.shape
    width = x_in.shape[1]
    chunks = lax.axis_size(CHUNKS)
    groups = lax.axis_size("heads")
    shape = jax.ShapeDtypeStruct
    wide = shape((length, width), F32)
    half_wide = shape((length, width), BF16)
    small = shape((heads, length), F32)
    narrow = shape(b_in.shape, F32)
    half_narrow = shape(b_in.shape, BF16)
    state = shape((chunks * 32, HALF), F32)
    weight = norm_weight.reshape(1, width)
    d_row = d_skip.reshape(1, heads)
    w_row, one_row = shape(weight.shape, F32), shape(d_row.shape, F32)
    decay_t = decay_log.T
    sem = pltpu.SemaphoreType.DMA

    def vmem(*shapes):
        return [pltpu.VMEM(s.shape, s.dtype) for s in shapes]

    (pay,) = call(
        start_kernel, "start", [shape((chunks * 33, HALF), F32)], decay_t, x_in, b_in,
        flops=10**9, scratch=vmem(small, half_narrow, half_wide) + [sem((6,))], hbm_in=(0, 1, 2),
    )
    got = exchange(pay, 33)
    base, esilu, c_val, w_val, dout_val, y_near = call(
        local_kernel, "local", [wide, wide, half_narrow, w_row, half_wide, wide],
        decay_t, x_in, b_in, c_in, gate, d_row, weight, d_out,
        flops=8 * 10**9, hbm_in=range(8), hbm_out=(5,), mib=24,
        scratch=vmem(small, half_wide, half_narrow, half_wide, one_row, wide) + [sem((12,))],
    )
    spread, decays = call(prefix_kernel, "prefix", [state, shape((chunks, HALF), F32)], got)
    before = exchange(spread, 32)
    gated, sums = call(
        gate_kernel, "gated", [wide, shape((groups, 8, length), F32)],
        before, c_val, base, esilu, dout_val, w_val, flops=10**9,
    )
    sums = lax.all_to_all(sums, "heads", 0, 0)

    def back(*refs):
        back_kernel(float(width * groups), *refs)

    rows = shape((8, length), F32)
    pay, scalars, before = call(
        back, "back", [shape((chunks * 33, HALF), F32), rows, state],
        sums, gated, esilu, dout_val, w_val, c_val, before,
        flops=10**9, hbm_out=(1, 2), scratch=vmem(rows) + [sem((2,))],
    )
    got = exchange(pay, 33)
    gx, gb, gl, tail, x_val, before, b_val, skip, grad_gate, grad_c = call(
        grads_kernel, "grads",
        [wide, narrow, small, wide, half_wide, state, half_narrow, shape((8, HALF), F32), half_wide, narrow],
        decay_t, scalars, d_out, weight, x_in, gate, b_in, c_in, d_row, y_near, before,
        flops=16 * 10**9, hbm_in=range(11), hbm_out=(8, 9), mib=32,
        scratch=vmem(small, rows, half_wide, w_row, half_wide, half_narrow, one_row, wide, wide, wide, half_wide, narrow)
        + [sem((16,))],
    )
    (spread,) = call(suffix_kernel, "suffix", [shape((chunks * 34, HALF), F32)], got, decays, skip)
    after = exchange(spread, 34)
    outs = [half_wide, narrow, small, one_row, shape((8, HALF), F32)]
    grad_x, grad_b, grad_decay, grad_skip, grad_weight = call(
        final_kernel, "final", outs,
        after, before, decay_t, tail, x_val, b_val, gx, gb, gl,
        flops=2 * 10**9, scratch=vmem(*outs, small) + [sem((9,))], hbm_in=(2,), hbm_out=range(5),
    )
    return (
        grad_x,
        grad_b,
        grad_c,
        grad_decay.T,
        grad_skip.reshape(heads),
        grad_gate,
        grad_weight.reshape(width),
    )


def solution(mesh):
    tokens = P(CHUNKS, "heads")
    in_specs = (tokens, tokens, tokens, tokens, P("heads"), tokens, P("heads"), tokens)
    out_specs = (tokens, tokens, tokens, tokens, P("heads"), tokens, P("heads"))
    return jax.shard_map(on_device, mesh=mesh, in_specs=in_specs, out_specs=out_specs, check_vma=False)
```

time: 112 us -> 94.1 us (0.84)
  local copies, waits for them, and re-layouts: 25.6 us -> 0.79 us
  waiting for transfers between devices: 2.97 us -> 9.02 us
  Pallas kernels: 19.3 us -> 21 us
    unnamed x58 -> x4, local copies, waits for them, and re-layouts: 25.6 us -> 0.79 us
    all_to_all x2, waiting for transfers between devices: 2.97 us -> 9.02 us  [exchange(): got = lax.all_to_all(messages.reshape(count, 1, rows * HALF), CHUNKS, 0, 0)]
    pallas_call x8, Pallas kernels: 19.3 us -> 21 us  [call(): pl.pallas_call(kernel, name=name, out_shape=[space(o.shape, o.dtype) for...]
  transfers between devices with their start and end apart: 2 -> 2, of which waited for: 1 -> 2; matrix products, arithmetic and copies ran while one was open for 0% -> 0% of each run, Pallas kernels for 9% -> 13%
where the time goes in v4:
time: 94.1 us; the launch traced here: 93.4 us
  blocking collectives  51.3 us (55%)
  Pallas kernels  21 us (22%)
  starting transfers between devices  10.6 us (11%)
  waiting for transfers between devices  9.02 us (10%)
    all_to_all x2, blocking collectives, exchange(): got = lax.all_to_all(messages.reshape(count, 1, rows * HALF), CHUNKS, 0, 0)  36.1 us
    pallas_call x8, Pallas kernels, call(): pl.pallas_call(kernel, name=name, out_shape=[space(o.shape, o.dtype) for...  21 us
    all_to_all x1, blocking collectives, on_device(): sums = lax.all_to_all(sums, 'heads', 0, 0)  15.2 us
    all_to_all x2, starting transfers between devices, exchange(): got = lax.all_to_all(messages.reshape(count, 1, rows * HALF), CHUNKS, 0, 0)  10.6 us
    all_to_all x2, waiting for transfers between devices, exchange(): got = lax.all_to_all(messages.reshape(count, 1, rows * HALF), CHUNKS, 0, 0)  9.02 us
  transfers between devices with their start and end apart: 2, of which 2 were waited for; matrix products, arithmetic and copies ran while one was open for 0% of the time, Pallas kernels for 13%

profile of v4, /device:TPU:1, one launch (start us, length us, event | category | flops | bytes accessed | tf_op | source)
XLA Modules:
  0.0 93.4 jit_solution(11728316421009202331)
XLA Ops:
  0.6 2.6 %start.1 = f32[1056,128]{1,0:T(8,128)S(1)} custom-call(f32[16,256]{1,0:T(8,128)} %bitcast.21, bf16[256,1024]{1,0:T(8,128)(2,1)} %x_hbm.5, bf16[256,128]{1,0:T(8,128)(2,1)} %b_hbm.5), custom_call_target="tpu_custom_call" | custom-call | flops 1000000000 | bytes 1146880 | tf_op jit(solution)/shard_map/start/pallas_call | solution.py:408
  3.3 19.6 %all_to_all.25 = f32[32,1,4224]{2,1,0:T(1,128)S(1)} all-to-all(f32[32,1,4224]{2,1,0:T(1,128)S(1)} %bitcast.18), channel_id=1, replica_groups=mesh['outer'=8,'inner'=4,'heads'=8] {'outer','inner'}, dimensions={0} | all-to-all | bytes 1081344 | tf_op jit(solution)/shard_map/all_to_all | solution.py:422
  22.8 0.9 prefix.1
  23.7 4.6 %all-to-all-start.1 = ((f32[32,1,4096]{2,1,0:T(1,128)}), f32[32,1,4096]{2,1,0:T(1,128)S(1)}, u32[]{:S(2)}, u32[]{:S(2)}) async-start(f32[32,1,4096]{2,1,0:T(1,128)} %bitcast.3), calls=%async_computation.1 | async-start | bytes 1048576 | tf_op jit(solution)/shard_map/all_to_all | solution.py:422
  28.3 4.2 %local.1 = (f32[256,1024]{1,0:T(8,128)S(1)}, f32[256,1024]{1,0:T(8,128)S(1)}, bf16[256,128]{1,0:T(8,128)(2,1)S(1)}, f32[1,1024]{1,0:T(1,128)S(1)}, bf16[256,1024]{1,0:T(8,128)(2,1)S(1)}, /*index=5*/f32[256,1024]{1,0:T(8,128)}) custom-call(f32[16,256]{1,0:T(8,128)} %bitcast.22, bf16[256,1024]{1,0:T(8,128)(2,1)} %x_hbm.5, bf16[256,128]{1,0:T(8,128)(2,1)} %b_hbm.5, ...), custom_call_target="tpu_custom_call" | custom-call | flops 8000000000 | bytes 5464128 | tf_op jit(solution)/shard_map/local/pallas_call | solution.py:408
  32.5 6.9 %all-to-all-done.1 = f32[32,1,4096]{2,1,0:T(1,128)S(1)} async-done(((f32[32,1,4096]{2,1,0:T(1,128)}), f32[32,1,4096]{2,1,0:T(1,128)S(1)}, u32[]{:S(2)}, u32[]{:S(2)}) %all-to-all-start.1) | async-done | bytes 524320 | tf_op jit(solution)/shard_map/all_to_all | solution.py:422
  39.4 0.6 gated.1
  40.0 15.2 %all_to_all.26.refs_0_ = f32[8,8,256]{2,1,0:T(8,128)S(1)} all-to-all(f32[8,8,256]{2,1,0:T(8,128)S(1)} %get-tuple-element.41), channel_id=1, replica_groups=mesh['outer'=8,'inner'=4,'heads'=8] {'heads'}, dimensions={0} | all-to-all | bytes 131072 | tf_op jit(solution)/shard_map/all_to_all | solution.py:464
  55.2 1.6 %back.1 = (f32[1056,128]{1,0:T(8,128)}, f32[8,256]{1,0:T(8,128)}, f32[1024,128]{1,0:T(8,128)}) custom-call(f32[8,8,256]{2,1,0:T(8,128)S(1)} %all_to_all.26.refs_0_, f32[256,1024]{1,0:T(8,128)S(1)} %get-tuple-element.42.refs_1_, f32[256,1024]{1,0:T(8,128)S(1)} %get-tuple-element.38.esilu_ref.refs_2_, ...), custom_call_target="tpu_custom_call" | custom-call | flops 1000000000 | bytes 4354048 | tf_op jit(solution)/shard_map/back/pallas_call | solution.py:408
  56.9 6.0 %all-to-all-start.3 = ((f32[32,1,4224]{2,1,0:T(1,128)}), f32[32,1,4224]{2,1,0:T(1,128)S(1)}, u32[]{:S(2)}, u32[]{:S(2)}) async-start(f32[32,1,4224]{2,1,0:T(1,128)} %bitcast.7), calls=%async_computation.3 | async-start | bytes 1081344 | tf_op jit(solution)/shard_map/all_to_all | solution.py:422
  62.9 8.3 %grads.1 = (f32[256,1024]{1,0:T(8,128)S(1)}, f32[256,128]{1,0:T(8,128)S(1)}, f32[16,256]{1,0:T(8,128)S(1)}, f32[256,1024]{1,0:T(8,128)S(1)}, bf16[256,1024]{1,0:...) custom-call(f32[16,256]{1,0:T(8,128)} %bitcast.23, ...), custom_call_target="tpu_custom_call" | custom-call | flops 16000000000 | bytes 7323712 | tf_op jit(solution)/shard_map/grads/pallas_call | solution.py:408
  71.2 0.0 copy-start
  71.2 0.8 copy-done
  72.0 2.1 %all-to-all-done.3 = f32[32,1,4224]{2,1,0:T(1,128)S(1)} async-done(((f32[32,1,4224]{2,1,0:T(1,128)}), f32[32,1,4224]{2,1,0:T(1,128)S(1)}, u32[]{:S(2)}, u32[]{:S(2)}) %all-to-all-start.3) | async-done | bytes 540704 | tf_op jit(solution)/shard_map/all_to_all | solution.py:422
  74.1 0.1 suffix.1
  74.2 0.0 copy-start.1
  74.2 16.6 %all_to_all.27 = f32[32,1,4352]{2,1,0:T(1,128)S(1)} all-to-all(f32[32,1,4352]{2,1,0:T(1,128)S(1)} %bitcast.14), channel_id=1, replica_groups=mesh['outer'=8,'inner'=4,'heads'=8] {'outer','inner'}, dimensions={0} | all-to-all | bytes 1114112 | tf_op jit(solution)/shard_map/all_to_all | solution.py:422
  90.8 0.0 copy-done.1
  90.8 2.7 %final.1 = (bf16[256,1024]{1,0:T(8,128)(2,1)}, f32[256,128]{1,0:T(8,128)}, f32[16,256]{1,0:T(8,128)}, f32[1,16]{1,0:T(1,128)}, f32[8,128]{1,0:T(8,128)}) custom-call(f32[1088,128]{1,0:T(8,128)S(1)} %bitcast.17, f32[1024,128]{1,0:T(8,128)S(1)} %copy-done.1, f32[16,256]{1,0:T(8,128)} %bitcast.24, f32[256,1024]{1,0:T(8,128)S(1)} %get-tuple-element.50.tail_ref, ...), custom_call_target="tpu_custom_call" | custom-call | flops 2000000000 | bytes 4608064 | tf_op jit(solution)/shard_map/final/pallas_call | solution.py:408
Async XLA Ops:
  23.7 15.7 %all-to-all-start.1 = ((f32[32,1,4096]{2,1,0:T(1,128)}), f32[32,1,4096]{2,1,0:T(1,128)S(1)}, u32[]{:S(2)}, u32[]{:S(2)}) async-start(f32[32,1,4096]{2,1,0:T(1,128)} %bitcast.3), calls=%async_computation.1 | async-start | bytes 1048576 | tf_op jit(solution)/shard_map/all_to_all | solution.py:422
  56.9 17.3 %all-to-all-start.3 = ((f32[32,1,4224]{2,1,0:T(1,128)}), f32[32,1,4224]{2,1,0:T(1,128)S(1)}, u32[]{:S(2)}, u32[]{:S(2)}) async-start(f32[32,1,4224]{2,1,0:T(1,128)} %bitcast.7), calls=%async_computation.3 | async-start | bytes 1081344 | tf_op jit(solution)/shard_map/all_to_all | solution.py:422
  71.2 0.8 copy-start
  74.2 16.6 %copy-start.1 = (f32[1024,128]{1,0:T(8,128)S(1)}, f32[1024,128]{1,0:T(8,128)}, u32[]{:S(2)}) copy-start(f32[1024,128]{1,0:T(8,128)} %copy-done) | copy-start | bytes 1572868

commit v5 on v4

--- a/solution.py
+++ b/solution.py
@@ -34,6 +34,10 @@
     return mm(hi, b, ca, cb) + mm(lo, b, ca, cb)
 
 
+def mm_split(a, b):
+    return mm(jnp.concatenate([a, a], axis=1), jnp.concatenate(split2(b), axis=0))
+
+
 def iota(shape, dim):
     return lax.broadcasted_iota(jnp.int32, shape, dim)
 
@@ -42,14 +46,16 @@
     return jnp.where(iota((heads, width), 1) // P_SIZE == iota((heads, width), 0), 1.0, 0.0).astype(BF16)
 
 
-def expand(a, spread, ca=1):
+def expand(a, spread):
     hi, lo = split2(a)
-    return mm(hi, spread, ca) + mm(lo, spread, ca)
+    both = jnp.concatenate([hi.astype(F32), lo.astype(F32)], axis=0).T.astype(BF16)
+    return mm(both, jnp.concatenate([spread, spread], axis=0))
 
 
 def segment(a, spread):
+    turned_map = turned(spread)
     hi, lo = split2(a)
-    return mm(spread, hi, 1, 1) + mm(spread, lo, 1, 1)
+    return (mm(hi, turned_map) + mm(lo, turned_map)).T
 
 
 def triangle(n, keep):
@@ -57,8 +63,13 @@
 
 
 def mm_by(a, tri):
-    hi, mid, lo = split3(a)
-    return mm(hi, tri) + mm(mid, tri) + mm(lo, tri)
+    rows = a.shape[0]
+    got = mm(jnp.concatenate(split3(a), axis=0), tri)
+    return got[:rows] + got[rows : 2 * rows] + got[2 * rows :]
+
+
+def load_state(ref, rows):
+    return jnp.concatenate([load_block(ref, rows, k) for k in range(4)], axis=1)
 
 
 def load_block(ref, rows, k):
@@ -84,8 +95,18 @@
     return [ref.at[:, pl.ds(256 * k, 256)] for k in range(4)]
 
 
+def turned(a):
+    return a.astype(F32).T.astype(BF16)
+
+
 def block_sums(lt):
     return mm_by(lt, triangle(lt.shape[1], lambda i, j: i <= j))
+
+
+def below(up, zeros, left, right, i):
+    return jnp.concatenate(
+        [jnp.concatenate([up[i], zeros], axis=1), jnp.concatenate([left[i], right[i]], axis=1)], axis=0
+    )
 
 
 def skip_row(d_ref, spread):
@@ -97,32 +118,27 @@
 def start_kernel(lt_hbm, x_hbm, b_hbm, pay_ref, lt_ref, b_ref, x_ref, sems):
     heads, length = lt_hbm.shape
     width = x_hbm.shape[1]
-    pairs = [(lt_hbm, lt_ref), (b_hbm, b_ref)] + list(zip(quarters(x_hbm), quarters(x_ref)))
-    first, second, *copies = fetch(pairs, sems)
-    spread = head_map(heads, width)
+    first, second, third = fetch([(lt_hbm, lt_ref), (b_hbm, b_ref), (x_hbm, x_ref)], sems)
+    second.wait()
+    b_turned = b_ref[...].astype(F32).T
     first.wait()
     cum = block_sums(lt_ref[...])
     last = cum[:, length - 1 : length]
-    tail = expand(jnp.exp(last - cum), spread, 0)
-    whole = expand(jnp.broadcast_to(jnp.exp(last), (heads, HALF)), spread, 0)[0:1, :]
-    second.wait()
-    b_val = b_ref[...]
-    for k in range(4):
-        copies[k].wait()
-        big = slice(256 * k, 256 * (k + 1))
-        hi, lo = split2(x_ref[:, big].astype(F32) * tail[:, big])
-        state = mm(b_val, hi, 0, 0) + mm(b_val, lo, 0, 0)
-        for q in (2 * k, 2 * k + 1):
-            for r in range(4):
-                at = 33 * (4 * q + r)
-                off = HALF * (q - 2 * k)
-                pay_ref[at : at + 32, :] = state[32 * r : 32 * r + 32, off : off + HALF]
-                pay_ref[at + 32 : at + 33, :] = whole[:, HALF * q : HALF * (q + 1)]
+    ends = jnp.concatenate([last - cum, jnp.broadcast_to(last, (heads, HALF))], axis=1)
+    tail = expand(jnp.exp(ends), head_map(heads, width))
+    whole = tail[length : length + 1, :]
+    third.wait()
+    state = mm_split(b_turned.astype(BF16), x_ref[...].astype(F32) * tail[:length])
+    for q in range(width // HALF):
+        for r in range(4):
+            at = 33 * (4 * q + r)
+            pay_ref[at : at + 32, :] = state[32 * r : 32 * r + 32, HALF * q : HALF * (q + 1)]
+            pay_ref[at + 32 : at + 33, :] = whole[:, HALF * q : HALF * (q + 1)]
 
 
 def local_kernel(
     lt_hbm, x_hbm, b_hbm, c_hbm, z_hbm, d_hbm, w_hbm, dout_hbm,
-    base_ref, esilu_ref, c_ref, w_ref, dout_ref, yn_hbm,
+    base_ref, esilu_ref, c_ref, ct_ref, w_ref, dout_ref, yn_hbm,
     lt_ref, x_ref, b_ref, z_ref, d_ref, yn_ref, sems,
 ):
     heads, length = lt_hbm.shape
@@ -132,44 +148,45 @@
          (w_hbm, w_ref), (dout_hbm, dout_ref)],
         sems,
     )
-    outs = [
-        pltpu.make_async_copy(src, dst, sems.at[8 + k])
-        for k, (src, dst) in enumerate(zip(quarters(yn_ref), quarters(yn_hbm)))
-    ]
     spread = head_map(heads, width)
     for copy in copies[:3]:
         copy.wait()
     cum_t = block_sums(lt_ref[...])
     cum = cum_t.T
-    ecum = expand(jnp.exp(cum_t), spread, 0)
+    ecum = expand(jnp.exp(cum_t), spread)
+    ct_ref[...] = turned(c_ref[...])
     inner = mm(c_ref[...], b_ref[...], 1, 1)
     top, left, right = inner[:HALF, :HALF], inner[HALF:, :HALF], inner[HALF:, HALF:]
     lower = iota((HALF, HALF), 0) >= iota((HALF, HALF), 1)
     first = iota((length, HALF), 1) < P_SIZE
+    zeros = jnp.zeros((HALF, HALF), BF16)
     for copy in copies[3:6]:
         copy.wait()
     skip = skip_row(d_ref, spread)
     for q in range(width // HALF):
         cols = slice(HALF * q, HALF * (q + 1))
         x_pair = x_ref[:, cols]
-        parts = []
+        mixes = []
         for h in (2 * q, 2 * q + 1):
             col, row = cum[:, h : h + 1], cum_t[h : h + 1, :]
             up = jnp.where(lower, jnp.exp(col[:HALF] - row[:, :HALF]), 0.0) * top
             dl = jnp.exp(col[HALF:] - row[:, :HALF]) * left
             dr = jnp.where(lower, jnp.exp(col[HALF:] - row[:, HALF:]), 0.0) * right
-            down = jnp.concatenate([dl, dr], axis=1)
-            parts.append(jnp.concatenate([mm2(up, x_pair[:HALF]), mm2(down, x_pair)], axis=0))
-        yn = jnp.where(first, parts[0], parts[1])
+            mixes += [below(split2(up), zeros, split2(dl), split2(dr), i) for i in range(2)]
+        got = mm(jnp.concatenate(mixes, axis=0), x_pair)
+        yn = jnp.where(
+            first, got[:length] + got[length : 2 * length], got[2 * length : 3 * length] + got[3 * length :]
+        )
         yn_ref[:, cols] = yn
-        if q % 2 == 1:
-            outs[q // 2].start()
         z_val = z_ref[:, cols].astype(F32)
         silu = z_val * (1.0 / (1.0 + jnp.exp(-z_val)))
         esilu_ref[:, cols] = ecum[:, cols] * silu
         base_ref[:, cols] = (yn + skip[:, cols] * x_pair.astype(F32)) * silu
-    for copy in copies[6:] + outs:
-        copy.wait()
+    for copy in copies[6:]:
+        copy.wait()
+    yn_copy = pltpu.make_async_copy(yn_ref, yn_hbm, sems.at[8])
+    yn_copy.start()
+    yn_copy.wait()
 
 
 def prefix_kernel(in_ref, out_ref, dec_ref):
@@ -190,8 +207,7 @@
     products = jnp.zeros((length, HALF), F32)
     for q in range(width // 256):
         big = slice(256 * q, 256 * (q + 1))
-        hi, lo = split2(load_block(s_ref, 32, q))
-        c_state = mm(c_val, hi) + mm(c_val, lo)
+        c_state = mm_split(c_val, load_block(s_ref, 32, q))
         gated = base_ref[:, big] + esilu_ref[:, big] * c_state
         gated_ref[:, big] = gated
         sq = gated * gated
@@ -206,7 +222,7 @@
 
 
 def back_kernel(
-    channels, sums_ref, gated_ref, esilu_ref, dout_ref, w_ref, c_ref, s_ref,
+    channels, sums_ref, gated_ref, esilu_ref, dout_ref, w_ref, ct_ref, s_ref,
     pay_ref, scal_hbm, s_hbm, scal_ref, sems,
 ):
     length, width = gated_ref.shape
@@ -223,14 +239,13 @@
     scal_copy.start()
     both = jnp.concatenate([rows, jnp.zeros((HALF - 8, length), F32)], axis=0).T
     inv_col, fall_col = both[:, 0:1], both[:, 1:2]
-    c_val = c_ref[...]
+    c_turned = ct_ref[...]
     for k in range(width // 256):
         big = slice(256 * k, 256 * (k + 1))
         gated = gated_ref[:, big]
         d_inv = dout_ref[:, big].astype(F32) * inv_col
         weight = jnp.sum(d_inv * gated, axis=0, keepdims=True)
-        hi, lo = split2((d_inv * w_ref[:, big] - gated * fall_col) * esilu_ref[:, big])
-        back = mm(c_val, hi, 0, 0) + mm(c_val, lo, 0, 0)
+        back = mm_split(c_turned, (d_inv * w_ref[:, big] - gated * fall_col) * esilu_ref[:, big])
         for q in (2 * k, 2 * k + 1):
             off = HALF * (q - 2 * k)
             for r in range(4):
@@ -243,8 +258,8 @@
 
 def grads_kernel(
     lt_hbm, scal_hbm, dout_hbm, w_hbm, x_hbm, z_hbm, b_hbm, c_hbm, d_hbm, yn_hbm, s_hbm,
-    gx_ref, gb_ref, gl_ref, tail_ref, x_ref, s_ref, b_ref, skip_ref, gz_hbm, gc_hbm,
-    lt_ref, scal_ref, dout_ref, w_ref, z_ref, c_ref, d_ref, yn_ref, dye_ref, dot_ref, gz_ref, gc_ref, sems,
+    gx_ref, gb_ref, gl_ref, tail_ref, x_ref, b_ref, skip_ref, gz_hbm, gc_hbm,
+    s_ref, lt_ref, scal_ref, dout_ref, w_ref, z_ref, c_ref, d_ref, yn_ref, dye_ref, dot_ref, gz_ref, gc_ref, sems,
 ):
     heads, length = lt_hbm.shape
     width = x_hbm.shape[1]
@@ -253,18 +268,14 @@
          (x_hbm, x_ref), (s_hbm, s_ref), (yn_hbm, yn_ref), (z_hbm, z_ref), (dout_hbm, dout_ref)],
         sems,
     )
-    outs = [
-        pltpu.make_async_copy(src, dst, sems.at[11 + k])
-        for k, (src, dst) in enumerate([(gc_ref, gc_hbm), *zip(quarters(gz_ref), quarters(gz_hbm))])
-    ]
     spread = head_map(heads, width)
     for copy in copies[:6]:
         copy.wait()
     cum_t = block_sums(lt_ref[...])
     cum = cum_t.T
     last = cum_t[:, length - 1 : length]
-    ecum = expand(jnp.exp(cum_t), spread, 0)
-    tail_ref[...] = expand(jnp.exp(last - cum_t), spread, 0)
+    ecum = expand(jnp.exp(cum_t), spread)
+    tail_ref[...] = expand(jnp.exp(last - cum_t), spread)
     both = jnp.concatenate([scal_ref[...], jnp.zeros((HALF - 8, length), F32)], axis=0).T
     inv_col, fall_col = both[:, 0:1], both[:, 1:2]
     skip = skip_row(d_ref, spread)
@@ -273,6 +284,7 @@
     left, right, low = inner_t[:HALF, :HALF], inner_t[:HALF, HALF:], inner_t[HALF:, HALF:]
     upper = iota((HALF, HALF), 0) <= iota((HALF, HALF), 1)
     first = iota((length, HALF), 1) < P_SIZE
+    zeros = jnp.zeros((HALF, HALF), BF16)
     w_left = jnp.zeros((HALF, HALF), F32)
     w_right = jnp.zeros((HALF, HALF), F32)
     w_low = jnp.zeros((HALF, HALF), F32)
@@ -288,8 +300,8 @@
         sig = 1.0 / (1.0 + jnp.exp(-z_val))
         silu = z_val * sig
         if q % 2 == 0:
-            s_hi, s_lo = split2(load_block(s_ref, 32, q // 2))
-            c_state = mm(c_val, s_hi) + mm(c_val, s_lo)
+            state = load_block(s_ref, 32, q // 2)
+            c_state = mm_split(c_val, state)
         off = slice(HALF * (q % 2), HALF * (q % 2 + 1))
         y_near = yn_ref[:, cols] + ecum[:, cols] * c_state[:, off]
         y_val = y_near + skip[:, cols] * x_val
@@ -298,38 +310,38 @@
         dye_ref[:, cols] = dy * ecum[:, cols]
         gz_ref[:, cols] = (d_gated * y_val * sig * (1.0 + z_val * (1.0 - sig))).astype(BF16)
         if q % 2 == 1:
-            outs[1 + q // 2].start()
             e_hi, e_lo = split2(dye_ref[:, 128 * q - 128 : 128 * q + 128])
-            far = far + (mm(e_hi, s_hi, 1, 1) + mm(e_hi, s_lo, 1, 1) + mm(e_lo, s_hi, 1, 1))
+            both = mm(jnp.concatenate([e_hi, e_lo], axis=0), jnp.concatenate(split2(state.T), axis=1))
+            far = far + both[:length, :HALF] + both[:length, HALF:] + both[length:, :HALF]
         skips.append(jnp.sum(dy * x_val, axis=0, keepdims=True))
         hi, lo = split2(dy)
-        parts = []
+        ones = jnp.concatenate([jnp.where(first, x_val, 0.0), jnp.where(first, 0.0, x_val)], axis=0).astype(BF16)
+        both = jnp.concatenate([hi, lo], axis=1)
+        dots = mm(jnp.concatenate([ones, ones], axis=1), both, 1, 1)
+        mix_hi, mix_lo = [], []
         for k in range(2):
             h = 2 * q + k
             col, row = cum[:, h : h + 1], cum_t[h : h + 1, :]
-            x_one = jnp.where(first if k == 0 else ~first, x_val, 0.0).astype(BF16)
+            dot = dots[length * k : length * (k + 1)]
             dec_left = jnp.where(upper, jnp.exp(row[:, :HALF] - col[:HALF]), 0.0)
             dec_right = jnp.exp(row[:, HALF:] - col[:HALF])
             dec_low = jnp.where(upper, jnp.exp(row[:, HALF:] - col[HALF:]), 0.0)
-            dot_up = mm(x_one[:HALF], hi, 1, 1) + mm(x_one[:HALF], lo, 1, 1)
-            dot_low = mm(x_one[HALF:], hi[HALF:], 1, 1) + mm(x_one[HALF:], lo[HALF:], 1, 1)
-            w_left = w_left + dec_left * dot_up[:, :HALF]
-            w_right = w_right + dec_right * dot_up[:, HALF:]
-            w_low = w_low + dec_low * dot_low
-            mix_up = jnp.concatenate([dec_left * left, dec_right * right], axis=1)
-            mix_low = dec_low * low
-            up_hi, up_lo = split2(mix_up)
-            low_hi, low_lo = split2(mix_low)
-            g_up = mm(up_hi, hi) + mm(up_hi, lo) + mm(up_lo, hi)
-            g_low = mm(low_hi, hi[HALF:]) + mm(low_hi, lo[HALF:]) + mm(low_lo, hi[HALF:])
-            parts.append(jnp.concatenate([g_up, g_low], axis=0))
-        g_near = jnp.where(first, parts[0], parts[1])
+            w_left = w_left + dec_left * dot[:HALF, :HALF]
+            w_right = w_right + dec_right * dot[:HALF, HALF:]
+            w_low = w_low + dec_low * dot[HALF:, HALF:]
+            blocks = [split2(m) for m in (dec_left * left, dec_right * right, dec_low * low)]
+            for i, mix in enumerate((mix_hi, mix_lo)):
+                up = jnp.concatenate([blocks[0][i], blocks[1][i]], axis=1)
+                mix.append(jnp.concatenate([up, jnp.concatenate([zeros, blocks[2][i]], axis=1)], axis=0))
+        got = mm(jnp.concatenate(mix_hi + mix_lo, axis=0), both)
+        got = got[: 2 * length, :HALF] + got[: 2 * length, HALF:] + got[2 * length :, :HALF]
+        g_near = jnp.where(first, got[:length], got[length:])
         gx_ref[:, cols] = g_near + skip[:, cols] * dy
         dot_ref[:, cols] = dy * y_near - x_val * g_near
     w_up = jnp.concatenate([w_left, w_right], axis=1)
     low_part = mm2(w_right.T, b_val[:HALF]) + mm2(w_low.T, b_val[HALF:])
     gc_ref[...] = far + jnp.concatenate([mm2(w_left.T, b_val[:HALF]), low_part], axis=0)
-    outs[0].start()
+    outs = fetch([(gc_ref, gc_hbm), (gz_ref, gz_hbm)], sems)
     gl_ref[...] = mm_by(segment(dot_ref[...], spread), triangle(length, lambda i, j: i >= j))
     gb_ref[:HALF, :] = mm2(w_up, c_val)
     gb_ref[HALF:, :] = mm2(w_low, c_val[HALF:])
@@ -355,49 +367,43 @@
 
 
 def final_kernel(
-    a_ref, s_ref, lt_hbm, tail_ref, x_ref, b_ref, gx_ref, gb_ref, gl_ref,
-    ox_hbm, ob_hbm, ol_hbm, skip_hbm, weight_hbm, ox_ref, ob_ref, ol_ref, skip_ref, weight_ref, lt_ref, sems,
+    a_ref, s_hbm, lt_hbm, tail_ref, x_ref, b_ref, gx_ref, gb_ref, gl_ref,
+    ox_hbm, ob_hbm, ol_hbm, skip_hbm, weight_hbm, ox_ref, ob_ref, ol_ref, skip_ref, weight_ref, lt_ref, s_ref, sems,
 ):
     heads, length = lt_hbm.shape
     width = x_ref.shape[1]
     spread = head_map(heads, width)
-    outs = [(weight_ref, weight_hbm), (skip_ref, skip_hbm), (ol_ref, ol_hbm), (ob_ref, ob_hbm)]
-    outs += zip(quarters(ox_ref), quarters(ox_hbm))
-    copies = copies_of(outs + [(lt_hbm, lt_ref)], sems)
-    copies[8].start()
+    outs = [(weight_ref, weight_hbm), (skip_ref, skip_hbm), (ol_ref, ol_hbm), (ob_ref, ob_hbm), (ox_ref, ox_hbm)]
+    copies = copies_of(outs + [(lt_hbm, lt_ref), (s_hbm, s_ref)], sems)
+    copies[6].start()
+    copies[5].start()
+    after = load_state(a_ref, 34)
+    tail, x_val = tail_ref[...], x_ref[...].astype(F32)
+    b_after = mm_split(b_ref[...], after) * tail
+    ox_ref[...] = (gx_ref[...] + b_after).astype(BF16)
+    copies[4].start()
+    late = segment(x_val * b_after, spread)
+    x_hi, x_lo = split2(x_val * tail)
+    a_hi, a_lo = split2(after.T)
+    both = mm(x_hi, jnp.concatenate([a_hi, a_lo], axis=1))
+    ob_ref[...] = gb_ref[...] + both[:, :HALF] + both[:, HALF:] + mm(x_lo, a_hi)
+    copies[3].start()
     weight_ref[...] = jnp.concatenate([a_ref[136 * q + 32 : 136 * q + 33, :] for q in range(8)], axis=0)
-    copies[0].start()
     skip = a_ref[33:34, :]
     for p in range(1, a_ref.shape[0] // 34):
         skip = skip + a_ref[34 * p + 33 : 34 * p + 34, :]
     skip_ref[...] = skip[:, :heads]
+    copies[0].start()
     copies[1].start()
-    b_val = b_ref[...]
-    late = jnp.zeros((heads, length), F32)
-    far = jnp.zeros(ob_ref.shape, F32)
-    starts = []
-    for k in range(width // 256):
-        big = slice(256 * k, 256 * (k + 1))
-        after = load_block(a_ref, 34, k)
-        starts.append(jnp.sum(load_block(s_ref, 32, k) * after, axis=0, keepdims=True))
-        tail, x_val = tail_ref[:, big], x_ref[:, big].astype(F32)
-        a_hi, a_lo = split2(after)
-        b_after = (mm(b_val, a_hi) + mm(b_val, a_lo)) * tail
-        ox_ref[:, big] = (gx_ref[:, big] + b_after).astype(BF16)
-        copies[4 + k].start()
-        late = late + segment(x_val * b_after, spread[:, big])
-        x_hi, x_lo = split2(x_val * tail)
-        far = far + (mm(x_hi, a_hi, 1, 1) + mm(x_hi, a_lo, 1, 1) + mm(x_lo, a_hi, 1, 1))
-    ob_ref[...] = gb_ref[...] + far
-    copies[3].start()
-    start = jnp.broadcast_to(jnp.concatenate(starts, axis=1), (HALF, width))
-    hi, mid, lo = split3(start)
-    start = (mm(spread, hi, 1, 1) + mm(spread, mid, 1, 1) + mm(spread, lo, 1, 1))[:, 0:1]
-    copies[8].wait()
+    copies[5].wait()
+    copies[6].wait()
+    start = jnp.sum(load_state(s_ref, 32) * after, axis=0, keepdims=True)
+    mine = iota((heads, width), 1) // P_SIZE == iota((heads, width), 0)
+    start = jnp.sum(jnp.where(mine, start, 0.0), axis=1, keepdims=True)
     whole = jnp.exp(jnp.sum(lt_ref[...], axis=1, keepdims=True))
     ol_ref[...] = gl_ref[...] + mm_by(late, triangle(length, lambda i, j: i < j)) + whole * start
     copies[2].start()
-    for copy in copies[:8]:
+    for copy in copies[:5]:
         copy.wait()
 
 
@@ -446,14 +452,14 @@
 
     (pay,) = call(
         start_kernel, "start", [shape((chunks * 33, HALF), F32)], decay_t, x_in, b_in,
-        flops=10**9, scratch=vmem(small, half_narrow, half_wide) + [sem((6,))], hbm_in=(0, 1, 2),
+        flops=10**9, scratch=vmem(small, half_narrow, half_wide) + [sem((3,))], hbm_in=(0, 1, 2),
     )
     got = exchange(pay, 33)
-    base, esilu, c_val, w_val, dout_val, y_near = call(
-        local_kernel, "local", [wide, wide, half_narrow, w_row, half_wide, wide],
+    base, esilu, c_val, c_turned, w_val, dout_val, y_near = call(
+        local_kernel, "local", [wide, wide, half_narrow, shape(c_in.shape[::-1], BF16), w_row, half_wide, wide],
         decay_t, x_in, b_in, c_in, gate, d_row, weight, d_out,
-        flops=8 * 10**9, hbm_in=range(8), hbm_out=(5,), mib=24,
-        scratch=vmem(small, half_wide, half_narrow, half_wide, one_row, wide) + [sem((12,))],
+        flops=8 * 10**9, hbm_in=range(8), hbm_out=(6,), mib=24,
+        scratch=vmem(small, half_wide, half_narrow, half_wide, one_row, wide) + [sem((9,))],
     )
     spread, decays = call(prefix_kernel, "prefix", [state, shape((chunks, HALF), F32)], got)
     before = exchange(spread, 32)
@@ -469,16 +475,16 @@
     rows = shape((8, length), F32)
     pay, scalars, before = call(
         back, "back", [shape((chunks * 33, HALF), F32), rows, state],
-        sums, gated, esilu, dout_val, w_val, c_val, before,
+        sums, gated, esilu, dout_val, w_val, c_turned, before,
         flops=10**9, hbm_out=(1, 2), scratch=vmem(rows) + [sem((2,))],
     )
     got = exchange(pay, 33)
-    gx, gb, gl, tail, x_val, before, b_val, skip, grad_gate, grad_c = call(
+    gx, gb, gl, tail, x_val, b_val, skip, grad_gate, grad_c = call(
         grads_kernel, "grads",
-        [wide, narrow, small, wide, half_wide, state, half_narrow, shape((8, HALF), F32), half_wide, narrow],
+        [wide, narrow, small, wide, half_wide, half_narrow, shape((8, HALF), F32), half_wide, narrow],
         decay_t, scalars, d_out, weight, x_in, gate, b_in, c_in, d_row, y_near, before,
-        flops=16 * 10**9, hbm_in=range(11), hbm_out=(8, 9), mib=32,
-        scratch=vmem(small, rows, half_wide, w_row, half_wide, half_narrow, one_row, wide, wide, wide, half_wide, narrow)
+        flops=16 * 10**9, hbm_in=range(11), hbm_out=(7, 8), mib=32,
+        scratch=vmem(state, small, rows, half_wide, w_row, half_wide, half_narrow, one_row, wide, wide, wide, half_wide, narrow)
         + [sem((16,))],
     )
     (spread,) = call(suffix_kernel, "suffix", [shape((chunks * 34, HALF), F32)], got, decays, skip)
@@ -487,7 +493,7 @@
     grad_x, grad_b, grad_decay, grad_skip, grad_weight = call(
         final_kernel, "final", outs,
         after, before, decay_t, tail, x_val, b_val, gx, gb, gl,
-        flops=2 * 10**9, scratch=vmem(*outs, small) + [sem((9,))], hbm_in=(2,), hbm_out=range(5),
+        flops=2 * 10**9, scratch=vmem(*outs, small, state) + [sem((7,))], hbm_in=(1, 2), hbm_out=range(5),
     )
     return (
         grad_x,

time: 94.1 us -> 91.8 us (0.976)
  Pallas kernels: 21 us -> 18.3 us
  waiting for transfers between devices: 9.02 us -> 11.2 us
    pallas_call x8, Pallas kernels: 21 us -> 18.3 us  [call(): pl.pallas_call(kernel, name=name, out_shape=[space(o.shape, o.dtype) for...]
    all_to_all x2, waiting for transfers between devices: 9.02 us -> 11.2 us  [exchange(): got = lax.all_to_all(messages.reshape(count, 1, rows * HALF), CHUNKS, 0, 0)]
  transfers between devices with their start and end apart: 2 -> 2, of which waited for: 2 -> 2; matrix products, arithmetic and copies ran while one was open for 0% -> 0% of each run, Pallas kernels for 13% -> 12%
where the time goes in v5:
time: 91.8 us; the launch traced here: 91.2 us
  blocking collectives  50.4 us (55%)
  Pallas kernels  18.3 us (20%)
  waiting for transfers between devices  11.2 us (12%)
  starting transfers between devices  10.6 us (12%)
    all_to_all x2, blocking collectives, exchange(): got = lax.all_to_all(messages.reshape(count, 1, rows * HALF), CHUNKS, 0, 0)  35.2 us
    pallas_call x8, Pallas kernels, call(): pl.pallas_call(kernel, name=name, out_shape=[space(o.shape, o.dtype) for...  18.3 us
    all_to_all x1, blocking collectives, on_device(): sums = lax.all_to_all(sums, 'heads', 0, 0)  15.2 us
    all_to_all x2, waiting for transfers between devices, exchange(): got = lax.all_to_all(messages.reshape(count, 1, rows * HALF), CHUNKS, 0, 0)  11.2 us
    all_to_all x2, starting transfers between devices, exchange(): got = lax.all_to_all(messages.reshape(count, 1, rows * HALF), CHUNKS, 0, 0)  10.6 us
  transfers between devices with their start and end apart: 2, of which 2 were waited for; matrix products, arithmetic and copies ran while one was open for 0% of the time, Pallas kernels for 12%

profile of v5, /device:TPU:1, one launch (start us, length us, event | category | flops | bytes accessed | tf_op | source)
XLA Modules:
  0.0 91.2 jit_solution(7381802598534644896)
XLA Ops:
  0.6 2.0 %start.1 = f32[1056,128]{1,0:T(8,128)S(1)} custom-call(f32[16,256]{1,0:T(8,128)} %bitcast.21, bf16[256,1024]{1,0:T(8,128)(2,1)} %x_hbm.5, bf16[256,128]{1,0:T(8,128)(2,1)} %b_hbm.5), custom_call_target="tpu_custom_call" | custom-call | flops 1000000000 | bytes 1146880 | tf_op jit(solution)/shard_map/start/pallas_call | solution.py:414
  2.7 19.6 %all_to_all.25 = f32[32,1,4224]{2,1,0:T(1,128)S(1)} all-to-all(f32[32,1,4224]{2,1,0:T(1,128)S(1)} %bitcast.18), channel_id=1, replica_groups=mesh['outer'=8,'inner'=4,'heads'=8] {'outer','inner'}, dimensions={0} | all-to-all | bytes 1081344 | tf_op jit(solution)/shard_map/all_to_all | solution.py:428
  22.2 0.9 prefix.1
  23.1 4.6 %all-to-all-start.1 = ((f32[32,1,4096]{2,1,0:T(1,128)}), f32[32,1,4096]{2,1,0:T(1,128)S(1)}, u32[]{:S(2)}, u32[]{:S(2)}) async-start(f32[32,1,4096]{2,1,0:T(1,128)} %bitcast.3), calls=%async_computation.1 | async-start | bytes 1048576 | tf_op jit(solution)/shard_map/all_to_all | solution.py:428
  27.7 4.0 %local.1 = (f32[256,1024]{1,0:T(8,128)S(1)}, f32[256,1024]{1,0:T(8,128)S(1)}, bf16[256,128]{1,0:T(8,128)(2,1)S(1)}, bf16[128,256]{1,0:T(8,128)(2,1)S(1)}, f32[1,...) custom-call(f32[16,256]{1,0:T(8,128)} %bitcast.22, bf16[256,1024]{1,0:T(8,128)(2,1)} %x_hbm.5, ...), custom_call_target="tpu_custom_call" | custom-call | flops 8000000000 | bytes 5529664 | tf_op jit(solution)/shard_map/local/pallas_call | solution.py:414
  31.7 7.1 %all-to-all-done.1 = f32[32,1,4096]{2,1,0:T(1,128)S(1)} async-done(((f32[32,1,4096]{2,1,0:T(1,128)}), f32[32,1,4096]{2,1,0:T(1,128)S(1)}, u32[]{:S(2)}, u32[]{:S(2)}) %all-to-all-start.1) | async-done | bytes 524320 | tf_op jit(solution)/shard_map/all_to_all | solution.py:428
  38.8 0.5 gated.1
  39.3 15.2 %all_to_all.26.refs_0_ = f32[8,8,256]{2,1,0:T(8,128)S(1)} all-to-all(f32[8,8,256]{2,1,0:T(8,128)S(1)} %get-tuple-element.41), channel_id=1, replica_groups=mesh['outer'=8,'inner'=4,'heads'=8] {'heads'}, dimensions={0} | all-to-all | bytes 131072 | tf_op jit(solution)/shard_map/all_to_all | solution.py:470
  54.5 1.7 %back.1 = (f32[1056,128]{1,0:T(8,128)}, f32[8,256]{1,0:T(8,128)}, f32[1024,128]{1,0:T(8,128)}) custom-call(f32[8,8,256]{2,1,0:T(8,128)S(1)} %all_to_all.26.refs_0_, f32[256,1024]{1,0:T(8,128)S(1)} %get-tuple-element.42.refs_1_, f32[256,1024]{1,0:T(8,128)S(1)} %get-tuple-element.38.esilu_ref.refs_2_, ...), custom_call_target="tpu_custom_call" | custom-call | flops 1000000000 | bytes 4354048 | tf_op jit(solution)/shard_map/back/pallas_call | solution.py:414
  56.2 6.0 %all-to-all-start.3 = ((f32[32,1,4224]{2,1,0:T(1,128)}), f32[32,1,4224]{2,1,0:T(1,128)S(1)}, u32[]{:S(2)}, u32[]{:S(2)}) async-start(f32[32,1,4224]{2,1,0:T(1,128)} %bitcast.7), calls=%async_computation.3 | async-start | bytes 1081344 | tf_op jit(solution)/shard_map/all_to_all | solution.py:428
  62.2 7.1 %grads.1 = (f32[256,1024]{1,0:T(8,128)S(1)}, f32[256,128]{1,0:T(8,128)S(1)}, f32[16,256]{1,0:T(8,128)S(1)}, f32[256,1024]{1,0:T(8,128)S(1)}, bf16[256,1024]{1,0:...) custom-call(f32[16,256]{1,0:T(8,128)} %bitcast.23, ...), custom_call_target="tpu_custom_call" | custom-call | flops 16000000000 | bytes 6799424 | tf_op jit(solution)/shard_map/grads/pallas_call | solution.py:414
  69.3 4.1 %all-to-all-done.3 = f32[32,1,4224]{2,1,0:T(1,128)S(1)} async-done(((f32[32,1,4224]{2,1,0:T(1,128)}), f32[32,1,4224]{2,1,0:T(1,128)S(1)}, u32[]{:S(2)}, u32[]{:S(2)}) %all-to-all-start.3) | async-done | bytes 540704 | tf_op jit(solution)/shard_map/all_to_all | solution.py:428
  73.5 0.1 suffix.1
  73.5 15.7 %all_to_all.27 = f32[32,1,4352]{2,1,0:T(1,128)S(1)} all-to-all(f32[32,1,4352]{2,1,0:T(1,128)S(1)} %bitcast.14), channel_id=1, replica_groups=mesh['outer'=8,'inner'=4,'heads'=8] {'outer','inner'}, dimensions={0} | all-to-all | bytes 1114112 | tf_op jit(solution)/shard_map/all_to_all | solution.py:428
  89.2 2.0 %final.1 = (bf16[256,1024]{1,0:T(8,128)(2,1)}, f32[256,128]{1,0:T(8,128)}, f32[16,256]{1,0:T(8,128)}, f32[1,16]{1,0:T(1,128)}, f32[8,128]{1,0:T(8,128)}) custom-call(f32[1088,128]{1,0:T(8,128)S(1)} %bitcast.17, f32[1024,128]{1,0:T(8,128)} %get-tuple-element.48.s_hbm, f32[16,256]{1,0:T(8,128)} %bitcast.24, f32[256,1024]{1,0:T(8,128)S(1)} %get-tuple-element.50.tail_ref, ...), custom_call_target="tpu_custom_call" | custom-call | flops 2000000000 | bytes 4608064 | tf_op jit(solution)/shard_map/final/pallas_call | solution.py:414
Async XLA Ops:
  23.1 15.7 %all-to-all-start.1 = ((f32[32,1,4096]{2,1,0:T(1,128)}), f32[32,1,4096]{2,1,0:T(1,128)S(1)}, u32[]{:S(2)}, u32[]{:S(2)}) async-start(f32[32,1,4096]{2,1,0:T(1,128)} %bitcast.3), calls=%async_computation.1 | async-start | bytes 1048576 | tf_op jit(solution)/shard_map/all_to_all | solution.py:428
  56.2 17.2 %all-to-all-start.3 = ((f32[32,1,4224]{2,1,0:T(1,128)}), f32[32,1,4224]{2,1,0:T(1,128)S(1)}, u32[]{:S(2)}, u32[]{:S(2)}) async-start(f32[32,1,4224]{2,1,0:T(1,128)} %bitcast.7), calls=%async_computation.3 | async-start | bytes 1081344 | tf_op jit(solution)/shard_map/all_to_all | solution.py:428

commit v6 on v5

--- a/solution.py
+++ b/solution.py
@@ -46,10 +46,10 @@
     return jnp.where(iota((heads, width), 1) // P_SIZE == iota((heads, width), 0), 1.0, 0.0).astype(BF16)
 
 
-def expand(a, spread):
+def expand(a, spread, rows=None):
     hi, lo = split2(a)
     both = jnp.concatenate([hi.astype(F32), lo.astype(F32)], axis=0).T.astype(BF16)
-    return mm(both, jnp.concatenate([spread, spread], axis=0))
+    return mm(both[:rows], jnp.concatenate([spread, spread], axis=0))
 
 
 def segment(a, spread):
@@ -125,7 +125,7 @@
     cum = block_sums(lt_ref[...])
     last = cum[:, length - 1 : length]
     ends = jnp.concatenate([last - cum, jnp.broadcast_to(last, (heads, HALF))], axis=1)
-    tail = expand(jnp.exp(ends), head_map(heads, width))
+    tail = expand(jnp.exp(ends), head_map(heads, width), length + 16)
     whole = tail[length : length + 1, :]
     third.wait()
     state = mm_split(b_turned.astype(BF16), x_ref[...].astype(F32) * tail[:length])
@@ -214,31 +214,33 @@
         pr = dout_ref[:, big].astype(F32) * w_ref[:, big] * gated
         squares = squares + sq[:, :HALF] + sq[:, HALF:]
         products = products + pr[:, :HALF] + pr[:, HALF:]
-    sq_row = jnp.sum(squares.T, axis=0, keepdims=True)
-    pr_row = jnp.sum(products.T, axis=0, keepdims=True)
-    tile = jnp.concatenate([sq_row, pr_row, jnp.zeros((6, length), F32)], axis=0)
-    for i in range(sums_ref.shape[0]):
-        sums_ref[i] = tile
+    rows = [jnp.sum(total.T, axis=0, keepdims=True) for total in (squares, products)]
+    tile = jnp.concatenate([row[:, HALF * i : HALF * (i + 1)] for row in rows for i in range(2)], axis=0)
+    sums_ref[...] = jnp.concatenate([tile] * (sums_ref.shape[0] // 4), axis=0)
+
+
+def columns(rows):
+    turned_rows = jnp.concatenate([rows, jnp.zeros((HALF - 8, HALF), F32)], axis=0).T
+    return [jnp.concatenate([turned_rows[:, i : i + 1], turned_rows[:, i + 1 : i + 2]], axis=0) for i in (0, 2)]
 
 
 def back_kernel(
     channels, sums_ref, gated_ref, esilu_ref, dout_ref, w_ref, ct_ref, s_ref,
-    pay_ref, scal_hbm, s_hbm, scal_ref, sems,
+    pay_hbm, scal_hbm, s_hbm, scal_ref, pay_ref, sems,
 ):
     length, width = gated_ref.shape
     scal_copy, s_copy = copies_of([(scal_ref, scal_hbm), (s_ref, s_hbm)], sems)
     s_copy.start()
-    total = sums_ref[0]
-    for i in range(1, sums_ref.shape[0]):
-        total = total + sums_ref[i]
-    squares, products = total[0:1, :], total[1:2, :]
-    inv = lax.rsqrt(squares / channels + EPS)
-    fall = inv * inv * inv * products / channels
-    rows = jnp.concatenate([inv, fall, jnp.zeros((6, length), F32)], axis=0)
+    total = sums_ref[0:4, :]
+    for i in range(1, sums_ref.shape[0] // 4):
+        total = total + sums_ref[4 * i : 4 * i + 4, :]
+    inv = lax.rsqrt(total[0:2] / channels + EPS)
+    fall = inv * inv * inv * total[2:4] / channels
+    rows = jnp.concatenate([inv, fall, jnp.zeros((4, HALF), F32)], axis=0)
     scal_ref[...] = rows
     scal_copy.start()
-    both = jnp.concatenate([rows, jnp.zeros((HALF - 8, length), F32)], axis=0).T
-    inv_col, fall_col = both[:, 0:1], both[:, 1:2]
+    inv_col, fall_col = columns(rows)
+    outs = []
     c_turned = ct_ref[...]
     for k in range(width // 256):
         big = slice(256 * k, 256 * (k + 1))
@@ -252,6 +254,12 @@
                 at = 33 * (4 * q + r)
                 pay_ref[at : at + 32, :] = back[32 * r : 32 * r + 32, off : off + HALF]
                 pay_ref[at + 32 : at + 33, :] = weight[:, off : off + HALF]
+        if k % 2 == 1:
+            rows = pl.ds(528 * (k // 2), 528)
+            outs.append(pltpu.make_async_copy(pay_ref.at[rows], pay_hbm.at[rows], sems.at[2 + k]))
+            outs[-1].start()
+    for copy in outs:
+        copy.wait()
     scal_copy.wait()
     s_copy.wait()
 
@@ -276,8 +284,7 @@
     last = cum_t[:, length - 1 : length]
     ecum = expand(jnp.exp(cum_t), spread)
     tail_ref[...] = expand(jnp.exp(last - cum_t), spread)
-    both = jnp.concatenate([scal_ref[...], jnp.zeros((HALF - 8, length), F32)], axis=0).T
-    inv_col, fall_col = both[:, 0:1], both[:, 1:2]
+    inv_col, fall_col = columns(scal_ref[...])
     skip = skip_row(d_ref, spread)
     b_val, c_val = b_ref[...], c_ref[...]
     inner_t = mm(b_val, c_val, 1, 1)
@@ -423,9 +430,9 @@
     )(*[pltpu.with_memory_space_constraint(a, space) for a, space in zip(args, spaces)])
 
 
-def exchange(messages, rows):
-    count = lax.axis_size(CHUNKS)
-    got = lax.all_to_all(messages.reshape(count, 1, rows * HALF), CHUNKS, 0, 0)
+def exchange(messages, rows, axes=CHUNKS):
+    count = lax.axis_size(axes)
+    got = lax.all_to_all(messages.reshape(count, 1, rows * HALF), axes, 0, 0)
     return got.reshape(count * rows, HALF)
 
 
@@ -464,19 +471,19 @@
     spread, decays = call(prefix_kernel, "prefix", [state, shape((chunks, HALF), F32)], got)
     before = exchange(spread, 32)
     gated, sums = call(
-        gate_kernel, "gated", [wide, shape((groups, 8, length), F32)],
+        gate_kernel, "gated", [wide, shape((groups * 4, HALF), F32)],
         before, c_val, base, esilu, dout_val, w_val, flops=10**9,
     )
-    sums = lax.all_to_all(sums, "heads", 0, 0)
+    sums = exchange(sums, 4, "heads")
 
     def back(*refs):
         back_kernel(float(width * groups), *refs)
 
-    rows = shape((8, length), F32)
+    rows = shape((8, HALF), F32)
     pay, scalars, before = call(
         back, "back", [shape((chunks * 33, HALF), F32), rows, state],
         sums, gated, esilu, dout_val, w_val, c_turned, before,
-        flops=10**9, hbm_out=(1, 2), scratch=vmem(rows) + [sem((2,))],
+        flops=10**9, hbm_out=(0, 1, 2), scratch=vmem(rows, shape((chunks * 33, HALF), F32)) + [sem((6,))],
     )
     got = exchange(pay, 33)
     gx, gb, gl, tail, x_val, b_val, skip, grad_gate, grad_c = call(

time: 91.8 us -> 90.9 us (level)
  no operation moved by 1% of the time
where the time goes in v6:
time: 90.9 us; the launch traced here: 90.4 us
  blocking collectives  49.8 us (55%)
  Pallas kernels  18.1 us (20%)
  waiting for transfers between devices  11.2 us (12%)
  starting transfers between devices  10.6 us (12%)
    all_to_all x3, blocking collectives, exchange(): got = lax.all_to_all(messages.reshape(count, 1, rows * HALF), axes, 0, 0)  49.8 us
    pallas_call x8, Pallas kernels, call(): pl.pallas_call(kernel, name=name, out_shape=[space(o.shape, o.dtype) for...  18.1 us
    all_to_all x2, waiting for transfers between devices, exchange(): got = lax.all_to_all(messages.reshape(count, 1, rows * HALF), axes, 0, 0)  11.2 us
    all_to_all x2, starting transfers between devices, exchange(): got = lax.all_to_all(messages.reshape(count, 1, rows * HALF), axes, 0, 0)  10.6 us
  transfers between devices with their start and end apart: 2, of which 2 were waited for; matrix products, arithmetic and copies ran while one was open for 0% of the time, Pallas kernels for 12%

profile of v6, /device:TPU:1, one launch (start us, length us, event | category | flops | bytes accessed | tf_op | source)
XLA Modules:
  0.0 90.4 jit_solution(2421572553523614875)
XLA Ops:
  0.6 2.0 %start.1 = f32[1056,128]{1,0:T(8,128)S(1)} custom-call(f32[16,256]{1,0:T(8,128)} %bitcast.26, bf16[256,1024]{1,0:T(8,128)(2,1)} %x_hbm.5, bf16[256,128]{1,0:T(8,128)(2,1)} %b_hbm.5), custom_call_target="tpu_custom_call" | custom-call | flops 1000000000 | bytes 1146880 | tf_op jit(solution)/shard_map/start/pallas_call | solution.py:421
  2.6 19.6 %all_to_all.25 = f32[32,1,4224]{2,1,0:T(1,128)S(1)} all-to-all(f32[32,1,4224]{2,1,0:T(1,128)S(1)} %bitcast.20), channel_id=1, replica_groups=mesh['outer'=8,'inner'=4,'heads'=8] {'outer','inner'}, dimensions={0} | all-to-all | bytes 1081344 | tf_op jit(solution)/shard_map/all_to_all | solution.py:435
  22.2 0.9 prefix.1
  23.0 4.6 %all-to-all-start.1 = ((f32[32,1,4096]{2,1,0:T(1,128)}), f32[32,1,4096]{2,1,0:T(1,128)S(1)}, u32[]{:S(2)}, u32[]{:S(2)}) async-start(f32[32,1,4096]{2,1,0:T(1,128)} %bitcast.3), calls=%async_computation.1 | async-start | bytes 1048576 | tf_op jit(solution)/shard_map/all_to_all | solution.py:435
  27.6 4.0 %local.1 = (f32[256,1024]{1,0:T(8,128)S(1)}, f32[256,1024]{1,0:T(8,128)S(1)}, bf16[256,128]{1,0:T(8,128)(2,1)S(1)}, bf16[128,256]{1,0:T(8,128)(2,1)S(1)}, f32[1,...) custom-call(f32[16,256]{1,0:T(8,128)} %bitcast.27, bf16[256,1024]{1,0:T(8,128)(2,1)} %x_hbm.5, ...), custom_call_target="tpu_custom_call" | custom-call | flops 8000000000 | bytes 5529664 | tf_op jit(solution)/shard_map/local/pallas_call | solution.py:421
  31.7 7.1 %all-to-all-done.1 = f32[32,1,4096]{2,1,0:T(1,128)S(1)} async-done(((f32[32,1,4096]{2,1,0:T(1,128)}), f32[32,1,4096]{2,1,0:T(1,128)S(1)}, u32[]{:S(2)}, u32[]{:S(2)}) %all-to-all-start.1) | async-done | bytes 524320 | tf_op jit(solution)/shard_map/all_to_all | solution.py:435
  38.7 0.6 gated.1
  39.3 14.6 %all_to_all.26 = f32[8,1,512]{2,1,0:T(1,128)S(1)} all-to-all(f32[8,1,512]{2,1,0:T(1,128)S(1)} %bitcast.24), channel_id=1, replica_groups=mesh['outer'=8,'inner'=4,'heads'=8] {'heads'}, dimensions={0} | all-to-all | bytes 32768 | tf_op jit(solution)/shard_map/all_to_all | solution.py:435
  53.9 1.5 %back.1 = (f32[1056,128]{1,0:T(8,128)}, f32[8,128]{1,0:T(8,128)}, f32[1024,128]{1,0:T(8,128)}) custom-call(f32[32,128]{1,0:T(8,128)S(1)} %bitcast.23, f32[256,1024]{1,0:T(8,128)S(1)} %get-tuple-element.42.refs_1_, f32[256,1024]{1,0:T(8,128)S(1)} %get-tuple-element.38.esilu_ref.refs_2_, bf16[256,1024]{1,0:T(8,128)(2,1)S(1)} %get-tuple-element.39.dout_ref.refs_3_, ...), custom_call_target="tpu_custom_call" | custom-call | flops 1000000000 | bytes 4300800 | tf_op jit(solution)/shard_map/back/pallas_call | solution.py:421
  55.5 6.0 %all-to-all-start.3 = ((f32[32,1,4224]{2,1,0:T(1,128)}), f32[32,1,4224]{2,1,0:T(1,128)S(1)}, u32[]{:S(2)}, u32[]{:S(2)}) async-start(f32[32,1,4224]{2,1,0:T(1,128)} %bitcast.25), calls=%async_computation.3 | async-start | bytes 1081344 | tf_op jit(solution)/shard_map/all_to_all | solution.py:435
  61.5 7.1 %grads.1 = (f32[256,1024]{1,0:T(8,128)S(1)}, f32[256,128]{1,0:T(8,128)S(1)}, f32[16,256]{1,0:T(8,128)S(1)}, f32[256,1024]{1,0:T(8,128)S(1)}, bf16[256,1024]{1,0:...) custom-call(f32[16,256]{1,0:T(8,128)} %bitcast.28, ...), custom_call_target="tpu_custom_call" | custom-call | flops 16000000000 | bytes 6795328 | tf_op jit(solution)/shard_map/grads/pallas_call | solution.py:421
  68.5 4.2 %all-to-all-done.3 = f32[32,1,4224]{2,1,0:T(1,128)S(1)} async-done(((f32[32,1,4224]{2,1,0:T(1,128)}), f32[32,1,4224]{2,1,0:T(1,128)S(1)}, u32[]{:S(2)}, u32[]{:S(2)}) %all-to-all-start.3) | async-done | bytes 540704 | tf_op jit(solution)/shard_map/all_to_all | solution.py:435
  72.7 0.1 suffix.1
  72.8 15.7 %all_to_all.27 = f32[32,1,4352]{2,1,0:T(1,128)S(1)} all-to-all(f32[32,1,4352]{2,1,0:T(1,128)S(1)} %bitcast.16), channel_id=1, replica_groups=mesh['outer'=8,'inner'=4,'heads'=8] {'outer','inner'}, dimensions={0} | all-to-all | bytes 1114112 | tf_op jit(solution)/shard_map/all_to_all | solution.py:435
  88.4 1.9 %final.1 = (bf16[256,1024]{1,0:T(8,128)(2,1)}, f32[256,128]{1,0:T(8,128)}, f32[16,256]{1,0:T(8,128)}, f32[1,16]{1,0:T(1,128)}, f32[8,128]{1,0:T(8,128)}) custom-call(f32[1088,128]{1,0:T(8,128)S(1)} %bitcast.19, f32[1024,128]{1,0:T(8,128)} %get-tuple-element.48.s_hbm, f32[16,256]{1,0:T(8,128)} %bitcast.29, f32[256,1024]{1,0:T(8,128)S(1)} %get-tuple-element.50.tail_ref, ...), custom_call_target="tpu_custom_call" | custom-call | flops 2000000000 | bytes 4608064 | tf_op jit(solution)/shard_map/final/pallas_call | solution.py:421
Async XLA Ops:
  23.0 15.7 %all-to-all-start.1 = ((f32[32,1,4096]{2,1,0:T(1,128)}), f32[32,1,4096]{2,1,0:T(1,128)S(1)}, u32[]{:S(2)}, u32[]{:S(2)}) async-start(f32[32,1,4096]{2,1,0:T(1,128)} %bitcast.3), calls=%async_computation.1 | async-start | bytes 1048576 | tf_op jit(solution)/shard_map/all_to_all | solution.py:435
  55.5 17.3 %all-to-all-start.3 = ((f32[32,1,4224]{2,1,0:T(1,128)}), f32[32,1,4224]{2,1,0:T(1,128)S(1)}, u32[]{:S(2)}, u32[]{:S(2)}) async-start(f32[32,1,4224]{2,1,0:T(1,128)} %bitcast.25), calls=%async_computation.3 | async-start | bytes 1081344 | tf_op jit(solution)/shard_map/all_to_all | solution.py:435

commit v7 on v6

--- a/solution.py
+++ b/solution.py
@@ -120,20 +120,26 @@
     width = x_hbm.shape[1]
     first, second, third = fetch([(lt_hbm, lt_ref), (b_hbm, b_ref), (x_hbm, x_ref)], sems)
     second.wait()
-    b_turned = b_ref[...].astype(F32).T
+    b_turned = turned(b_ref[...])
     first.wait()
-    cum = block_sums(lt_ref[...])
-    last = cum[:, length - 1 : length]
-    ends = jnp.concatenate([last - cum, jnp.broadcast_to(last, (heads, HALF))], axis=1)
-    tail = expand(jnp.exp(ends), head_map(heads, width), length + 16)
-    whole = tail[length : length + 1, :]
+    later = triangle(length, lambda i, j: i > j)
+    ends = mm_by(lt_ref[...], jnp.concatenate([later, jnp.ones((length, HALF), BF16)], axis=1))
+    hi, lo = split2(jnp.exp(ends))
+    both = jnp.concatenate([hi.astype(F32), lo.astype(F32)], axis=0).T.astype(BF16)[: length + 16]
+    spread = head_map(heads, width)
+    spread = jnp.concatenate([spread, spread], axis=0)
     third.wait()
-    state = mm_split(b_turned.astype(BF16), x_ref[...].astype(F32) * tail[:length])
-    for q in range(width // HALF):
-        for r in range(4):
-            at = 33 * (4 * q + r)
-            pay_ref[at : at + 32, :] = state[32 * r : 32 * r + 32, HALF * q : HALF * (q + 1)]
-            pay_ref[at + 32 : at + 33, :] = whole[:, HALF * q : HALF * (q + 1)]
+    for k in range(1):
+        big = slice(1024 * k, 1024 * (k + 1))
+        tail = mm(both, spread[:, big])
+        state = mm_split(b_turned, x_ref[:, big].astype(F32) * tail[:length])
+        whole = tail[length : length + 1, :]
+        for q in range(8):
+            cols = slice(HALF * q, HALF * (q + 1))
+            for r in range(4):
+                at = 33 * (4 * (q + 8 * k) + r)
+                pay_ref[at : at + 32, :] = state[32 * r : 32 * r + 32, cols]
+                pay_ref[at + 32 : at + 33, :] = whole[:, cols]
 
 
 def local_kernel(

time: 90.9 us -> 90.7 us (level)
  no operation moved by 1% of the time
where the time goes in v7:
time: 90.7 us; the launch traced here: 90.2 us
  blocking collectives  49.8 us (55%)
  Pallas kernels  17.8 us (20%)
  waiting for transfers between devices  11.2 us (12%)
  starting transfers between devices  10.6 us (12%)
    all_to_all x3, blocking collectives, exchange(): got = lax.all_to_all(messages.reshape(count, 1, rows * HALF), axes, 0, 0)  49.8 us
    pallas_call x8, Pallas kernels, call(): pl.pallas_call(kernel, name=name, out_shape=[space(o.shape, o.dtype) for...  17.8 us
    all_to_all x2, waiting for transfers between devices, exchange(): got = lax.all_to_all(messages.reshape(count, 1, rows * HALF), axes, 0, 0)  11.2 us
    all_to_all x2, starting transfers between devices, exchange(): got = lax.all_to_all(messages.reshape(count, 1, rows * HALF), axes, 0, 0)  10.6 us
  transfers between devices with their start and end apart: 2, of which 2 were waited for; matrix products, arithmetic and copies ran while one was open for 0% of the time, Pallas kernels for 12%

profile of v7, /device:TPU:1, one launch (start us, length us, event | category | flops | bytes accessed | tf_op | source)
XLA Modules:
  0.0 90.2 jit_solution(14211909920812290001)
XLA Ops:
  0.6 1.7 %start.1 = f32[1056,128]{1,0:T(8,128)S(1)} custom-call(f32[16,256]{1,0:T(8,128)} %bitcast.26, bf16[256,1024]{1,0:T(8,128)(2,1)} %x_hbm.5, bf16[256,128]{1,0:T(8,128)(2,1)} %b_hbm.5), custom_call_target="tpu_custom_call" | custom-call | flops 1000000000 | bytes 1146880 | tf_op jit(solution)/shard_map/start/pallas_call | solution.py:427
  2.4 19.6 %all_to_all.25 = f32[32,1,4224]{2,1,0:T(1,128)S(1)} all-to-all(f32[32,1,4224]{2,1,0:T(1,128)S(1)} %bitcast.20), channel_id=1, replica_groups=mesh['outer'=8,'inner'=4,'heads'=8] {'outer','inner'}, dimensions={0} | all-to-all | bytes 1081344 | tf_op jit(solution)/shard_map/all_to_all | solution.py:441
  21.9 0.9 prefix.1
  22.8 4.6 %all-to-all-start.1 = ((f32[32,1,4096]{2,1,0:T(1,128)}), f32[32,1,4096]{2,1,0:T(1,128)S(1)}, u32[]{:S(2)}, u32[]{:S(2)}) async-start(f32[32,1,4096]{2,1,0:T(1,128)} %bitcast.3), calls=%async_computation.1 | async-start | bytes 1048576 | tf_op jit(solution)/shard_map/all_to_all | solution.py:441
  27.4 4.0 %local.1 = (f32[256,1024]{1,0:T(8,128)S(1)}, f32[256,1024]{1,0:T(8,128)S(1)}, bf16[256,128]{1,0:T(8,128)(2,1)S(1)}, bf16[128,256]{1,0:T(8,128)(2,1)S(1)}, f32[1,...) custom-call(f32[16,256]{1,0:T(8,128)} %bitcast.27, bf16[256,1024]{1,0:T(8,128)(2,1)} %x_hbm.5, ...), custom_call_target="tpu_custom_call" | custom-call | flops 8000000000 | bytes 5529664 | tf_op jit(solution)/shard_map/local/pallas_call | solution.py:427
  31.4 7.1 %all-to-all-done.1 = f32[32,1,4096]{2,1,0:T(1,128)S(1)} async-done(((f32[32,1,4096]{2,1,0:T(1,128)}), f32[32,1,4096]{2,1,0:T(1,128)S(1)}, u32[]{:S(2)}, u32[]{:S(2)}) %all-to-all-start.1) | async-done | bytes 524320 | tf_op jit(solution)/shard_map/all_to_all | solution.py:441
  38.5 0.6 gated.1
  39.1 14.6 %all_to_all.26 = f32[8,1,512]{2,1,0:T(1,128)S(1)} all-to-all(f32[8,1,512]{2,1,0:T(1,128)S(1)} %bitcast.24), channel_id=1, replica_groups=mesh['outer'=8,'inner'=4,'heads'=8] {'heads'}, dimensions={0} | all-to-all | bytes 32768 | tf_op jit(solution)/shard_map/all_to_all | solution.py:441
  53.7 1.5 %back.1 = (f32[1056,128]{1,0:T(8,128)}, f32[8,128]{1,0:T(8,128)}, f32[1024,128]{1,0:T(8,128)}) custom-call(f32[32,128]{1,0:T(8,128)S(1)} %bitcast.23, f32[256,1024]{1,0:T(8,128)S(1)} %get-tuple-element.42.refs_1_, f32[256,1024]{1,0:T(8,128)S(1)} %get-tuple-element.38.esilu_ref.refs_2_, bf16[256,1024]{1,0:T(8,128)(2,1)S(1)} %get-tuple-element.39.dout_ref.refs_3_, ...), custom_call_target="tpu_custom_call" | custom-call | flops 1000000000 | bytes 4300800 | tf_op jit(solution)/shard_map/back/pallas_call | solution.py:427
  55.2 6.0 %all-to-all-start.3 = ((f32[32,1,4224]{2,1,0:T(1,128)}), f32[32,1,4224]{2,1,0:T(1,128)S(1)}, u32[]{:S(2)}, u32[]{:S(2)}) async-start(f32[32,1,4224]{2,1,0:T(1,128)} %bitcast.25), calls=%async_computation.3 | async-start | bytes 1081344 | tf_op jit(solution)/shard_map/all_to_all | solution.py:441
  61.2 7.1 %grads.1 = (f32[256,1024]{1,0:T(8,128)S(1)}, f32[256,128]{1,0:T(8,128)S(1)}, f32[16,256]{1,0:T(8,128)S(1)}, f32[256,1024]{1,0:T(8,128)S(1)}, bf16[256,1024]{1,0:...) custom-call(f32[16,256]{1,0:T(8,128)} %bitcast.28, ...), custom_call_target="tpu_custom_call" | custom-call | flops 16000000000 | bytes 6795328 | tf_op jit(solution)/shard_map/grads/pallas_call | solution.py:427
  68.3 4.2 %all-to-all-done.3 = f32[32,1,4224]{2,1,0:T(1,128)S(1)} async-done(((f32[32,1,4224]{2,1,0:T(1,128)}), f32[32,1,4224]{2,1,0:T(1,128)S(1)}, u32[]{:S(2)}, u32[]{:S(2)}) %all-to-all-start.3) | async-done | bytes 540704 | tf_op jit(solution)/shard_map/all_to_all | solution.py:441
  72.5 0.1 suffix.1
  72.6 15.7 %all_to_all.27 = f32[32,1,4352]{2,1,0:T(1,128)S(1)} all-to-all(f32[32,1,4352]{2,1,0:T(1,128)S(1)} %bitcast.16), channel_id=1, replica_groups=mesh['outer'=8,'inner'=4,'heads'=8] {'outer','inner'}, dimensions={0} | all-to-all | bytes 1114112 | tf_op jit(solution)/shard_map/all_to_all | solution.py:441
  88.2 1.9 %final.1 = (bf16[256,1024]{1,0:T(8,128)(2,1)}, f32[256,128]{1,0:T(8,128)}, f32[16,256]{1,0:T(8,128)}, f32[1,16]{1,0:T(1,128)}, f32[8,128]{1,0:T(8,128)}) custom-call(f32[1088,128]{1,0:T(8,128)S(1)} %bitcast.19, f32[1024,128]{1,0:T(8,128)} %get-tuple-element.48.s_hbm, f32[16,256]{1,0:T(8,128)} %bitcast.29, f32[256,1024]{1,0:T(8,128)S(1)} %get-tuple-element.50.tail_ref, ...), custom_call_target="tpu_custom_call" | custom-call | flops 2000000000 | bytes 4608064 | tf_op jit(solution)/shard_map/final/pallas_call | solution.py:427
Async XLA Ops:
  22.8 15.7 %all-to-all-start.1 = ((f32[32,1,4096]{2,1,0:T(1,128)}), f32[32,1,4096]{2,1,0:T(1,128)S(1)}, u32[]{:S(2)}, u32[]{:S(2)}) async-start(f32[32,1,4096]{2,1,0:T(1,128)} %bitcast.3), calls=%async_computation.1 | async-start | bytes 1048576 | tf_op jit(solution)/shard_map/all_to_all | solution.py:441
  55.2 17.3 %all-to-all-start.3 = ((f32[32,1,4224]{2,1,0:T(1,128)}), f32[32,1,4224]{2,1,0:T(1,128)S(1)}, u32[]{:S(2)}, u32[]{:S(2)}) async-start(f32[32,1,4224]{2,1,0:T(1,128)} %bitcast.25), calls=%async_computation.3 | async-start | bytes 1081344 | tf_op jit(solution)/shard_map/all_to_all | solution.py:441

commit v8 on v7

--- a/solution.py
+++ b/solution.py
@@ -119,27 +119,24 @@
     heads, length = lt_hbm.shape
     width = x_hbm.shape[1]
     first, second, third = fetch([(lt_hbm, lt_ref), (b_hbm, b_ref), (x_hbm, x_ref)], sems)
-    second.wait()
-    b_turned = turned(b_ref[...])
     first.wait()
     later = triangle(length, lambda i, j: i > j)
     ends = mm_by(lt_ref[...], jnp.concatenate([later, jnp.ones((length, HALF), BF16)], axis=1))
+    second.wait()
+    b_turned = turned(b_ref[...])
     hi, lo = split2(jnp.exp(ends))
     both = jnp.concatenate([hi.astype(F32), lo.astype(F32)], axis=0).T.astype(BF16)[: length + 16]
     spread = head_map(heads, width)
     spread = jnp.concatenate([spread, spread], axis=0)
     third.wait()
-    for k in range(1):
-        big = slice(1024 * k, 1024 * (k + 1))
-        tail = mm(both, spread[:, big])
-        state = mm_split(b_turned, x_ref[:, big].astype(F32) * tail[:length])
-        whole = tail[length : length + 1, :]
-        for q in range(8):
-            cols = slice(HALF * q, HALF * (q + 1))
-            for r in range(4):
-                at = 33 * (4 * (q + 8 * k) + r)
-                pay_ref[at : at + 32, :] = state[32 * r : 32 * r + 32, cols]
-                pay_ref[at + 32 : at + 33, :] = whole[:, cols]
+    tail = mm(both, spread)
+    state = mm_split(b_turned, x_ref[...].astype(F32) * tail[:length])
+    for q in range(width // HALF):
+        cols = slice(HALF * q, HALF * (q + 1))
+        for r in range(4):
+            at = 33 * (4 * q + r)
+            pay_ref[at : at + 32, :] = state[32 * r : 32 * r + 32, cols]
+            pay_ref[at + 32 : at + 33, :] = tail[length : length + 1, cols]
 
 
 def local_kernel(

time: 90.7 us -> 90.7 us (level)
  no operation moved by 1% of the time
where the time goes in v8:
time: 90.7 us; the launch traced here: 90.1 us
  blocking collectives  49.8 us (55%)
  Pallas kernels  17.7 us (20%)
  waiting for transfers between devices  11.2 us (12%)
  starting transfers between devices  10.6 us (12%)
    all_to_all x3, blocking collectives, exchange(): got = lax.all_to_all(messages.reshape(count, 1, rows * HALF), axes, 0, 0)  49.8 us
    pallas_call x8, Pallas kernels, call(): pl.pallas_call(kernel, name=name, out_shape=[space(o.shape, o.dtype) for...  17.7 us
    all_to_all x2, waiting for transfers between devices, exchange(): got = lax.all_to_all(messages.reshape(count, 1, rows * HALF), axes, 0, 0)  11.2 us
    all_to_all x2, starting transfers between devices, exchange(): got = lax.all_to_all(messages.reshape(count, 1, rows * HALF), axes, 0, 0)  10.6 us
  transfers between devices with their start and end apart: 2, of which 2 were waited for; matrix products, arithmetic and copies ran while one was open for 0% of the time, Pallas kernels for 12%

profile of v8, /device:TPU:1, one launch (start us, length us, event | category | flops | bytes accessed | tf_op | source)
XLA Modules:
  0.0 90.1 jit_solution(14097590072023441944)
XLA Ops:
  0.6 1.6 %start.1 = f32[1056,128]{1,0:T(8,128)S(1)} custom-call(f32[16,256]{1,0:T(8,128)} %bitcast.26, bf16[256,1024]{1,0:T(8,128)(2,1)} %x_hbm.5, bf16[256,128]{1,0:T(8,128)(2,1)} %b_hbm.5), custom_call_target="tpu_custom_call" | custom-call | flops 1000000000 | bytes 1146880 | tf_op jit(solution)/shard_map/start/pallas_call | solution.py:424
  2.3 19.6 %all_to_all.25 = f32[32,1,4224]{2,1,0:T(1,128)S(1)} all-to-all(f32[32,1,4224]{2,1,0:T(1,128)S(1)} %bitcast.20), channel_id=1, replica_groups=mesh['outer'=8,'inner'=4,'heads'=8] {'outer','inner'}, dimensions={0} | all-to-all | bytes 1081344 | tf_op jit(solution)/shard_map/all_to_all | solution.py:438
  21.8 0.9 prefix.1
  22.7 4.6 %all-to-all-start.1 = ((f32[32,1,4096]{2,1,0:T(1,128)}), f32[32,1,4096]{2,1,0:T(1,128)S(1)}, u32[]{:S(2)}, u32[]{:S(2)}) async-start(f32[32,1,4096]{2,1,0:T(1,128)} %bitcast.3), calls=%async_computation.1 | async-start | bytes 1048576 | tf_op jit(solution)/shard_map/all_to_all | solution.py:438
  27.3 4.0 %local.1 = (f32[256,1024]{1,0:T(8,128)S(1)}, f32[256,1024]{1,0:T(8,128)S(1)}, bf16[256,128]{1,0:T(8,128)(2,1)S(1)}, bf16[128,256]{1,0:T(8,128)(2,1)S(1)}, f32[1,...) custom-call(f32[16,256]{1,0:T(8,128)} %bitcast.27, bf16[256,1024]{1,0:T(8,128)(2,1)} %x_hbm.5, ...), custom_call_target="tpu_custom_call" | custom-call | flops 8000000000 | bytes 5529664 | tf_op jit(solution)/shard_map/local/pallas_call | solution.py:424
  31.3 7.1 %all-to-all-done.1 = f32[32,1,4096]{2,1,0:T(1,128)S(1)} async-done(((f32[32,1,4096]{2,1,0:T(1,128)}), f32[32,1,4096]{2,1,0:T(1,128)S(1)}, u32[]{:S(2)}, u32[]{:S(2)}) %all-to-all-start.1) | async-done | bytes 524320 | tf_op jit(solution)/shard_map/all_to_all | solution.py:438
  38.4 0.6 gated.1
  39.0 14.6 %all_to_all.26 = f32[8,1,512]{2,1,0:T(1,128)S(1)} all-to-all(f32[8,1,512]{2,1,0:T(1,128)S(1)} %bitcast.24), channel_id=1, replica_groups=mesh['outer'=8,'inner'=4,'heads'=8] {'heads'}, dimensions={0} | all-to-all | bytes 32768 | tf_op jit(solution)/shard_map/all_to_all | solution.py:438
  53.6 1.5 %back.1 = (f32[1056,128]{1,0:T(8,128)}, f32[8,128]{1,0:T(8,128)}, f32[1024,128]{1,0:T(8,128)}) custom-call(f32[32,128]{1,0:T(8,128)S(1)} %bitcast.23, f32[256,1024]{1,0:T(8,128)S(1)} %get-tuple-element.42.refs_1_, f32[256,1024]{1,0:T(8,128)S(1)} %get-tuple-element.38.esilu_ref.refs_2_, bf16[256,1024]{1,0:T(8,128)(2,1)S(1)} %get-tuple-element.39.dout_ref.refs_3_, ...), custom_call_target="tpu_custom_call" | custom-call | flops 1000000000 | bytes 4300800 | tf_op jit(solution)/shard_map/back/pallas_call | solution.py:424
  55.1 6.0 %all-to-all-start.3 = ((f32[32,1,4224]{2,1,0:T(1,128)}), f32[32,1,4224]{2,1,0:T(1,128)S(1)}, u32[]{:S(2)}, u32[]{:S(2)}) async-start(f32[32,1,4224]{2,1,0:T(1,128)} %bitcast.25), calls=%async_computation.3 | async-start | bytes 1081344 | tf_op jit(solution)/shard_map/all_to_all | solution.py:438
  61.1 7.1 %grads.1 = (f32[256,1024]{1,0:T(8,128)S(1)}, f32[256,128]{1,0:T(8,128)S(1)}, f32[16,256]{1,0:T(8,128)S(1)}, f32[256,1024]{1,0:T(8,128)S(1)}, bf16[256,1024]{1,0:...) custom-call(f32[16,256]{1,0:T(8,128)} %bitcast.28, ...), custom_call_target="tpu_custom_call" | custom-call | flops 16000000000 | bytes 6795328 | tf_op jit(solution)/shard_map/grads/pallas_call | solution.py:424
  68.2 4.2 %all-to-all-done.3 = f32[32,1,4224]{2,1,0:T(1,128)S(1)} async-done(((f32[32,1,4224]{2,1,0:T(1,128)}), f32[32,1,4224]{2,1,0:T(1,128)S(1)}, u32[]{:S(2)}, u32[]{:S(2)}) %all-to-all-start.3) | async-done | bytes 540704 | tf_op jit(solution)/shard_map/all_to_all | solution.py:438
  72.4 0.1 suffix.1
  72.4 15.7 %all_to_all.27 = f32[32,1,4352]{2,1,0:T(1,128)S(1)} all-to-all(f32[32,1,4352]{2,1,0:T(1,128)S(1)} %bitcast.16), channel_id=1, replica_groups=mesh['outer'=8,'inner'=4,'heads'=8] {'outer','inner'}, dimensions={0} | all-to-all | bytes 1114112 | tf_op jit(solution)/shard_map/all_to_all | solution.py:438
  88.1 1.9 %final.1 = (bf16[256,1024]{1,0:T(8,128)(2,1)}, f32[256,128]{1,0:T(8,128)}, f32[16,256]{1,0:T(8,128)}, f32[1,16]{1,0:T(1,128)}, f32[8,128]{1,0:T(8,128)}) custom-call(f32[1088,128]{1,0:T(8,128)S(1)} %bitcast.19, f32[1024,128]{1,0:T(8,128)} %get-tuple-element.48.s_hbm, f32[16,256]{1,0:T(8,128)} %bitcast.29, f32[256,1024]{1,0:T(8,128)S(1)} %get-tuple-element.50.tail_ref, ...), custom_call_target="tpu_custom_call" | custom-call | flops 2000000000 | bytes 4608064 | tf_op jit(solution)/shard_map/final/pallas_call | solution.py:424
Async XLA Ops:
  22.7 15.7 %all-to-all-start.1 = ((f32[32,1,4096]{2,1,0:T(1,128)}), f32[32,1,4096]{2,1,0:T(1,128)S(1)}, u32[]{:S(2)}, u32[]{:S(2)}) async-start(f32[32,1,4096]{2,1,0:T(1,128)} %bitcast.3), calls=%async_computation.1 | async-start | bytes 1048576 | tf_op jit(solution)/shard_map/all_to_all | solution.py:438
  55.1 17.3 %all-to-all-start.3 = ((f32[32,1,4224]{2,1,0:T(1,128)}), f32[32,1,4224]{2,1,0:T(1,128)S(1)}, u32[]{:S(2)}, u32[]{:S(2)}) async-start(f32[32,1,4224]{2,1,0:T(1,128)} %bitcast.25), calls=%async_computation.3 | async-start | bytes 1081344 | tf_op jit(solution)/shard_map/all_to_all | solution.py:438

commit v9 on v8

--- a/solution.py
+++ b/solution.py
@@ -62,6 +62,12 @@
     return jnp.where(keep(iota((n, n), 0), iota((n, n), 1)), 1.0, 0.0).astype(BF16)
 
 
+def mm_by_two(a, tri):
+    rows = a.shape[0]
+    got = mm(jnp.concatenate(split2(a), axis=0), tri)
+    return got[:rows] + got[rows:]
+
+
 def mm_by(a, tri):
     rows = a.shape[0]
     got = mm(jnp.concatenate(split3(a), axis=0), tri)
@@ -121,7 +127,7 @@
     first, second, third = fetch([(lt_hbm, lt_ref), (b_hbm, b_ref), (x_hbm, x_ref)], sems)
     first.wait()
     later = triangle(length, lambda i, j: i > j)
-    ends = mm_by(lt_ref[...], jnp.concatenate([later, jnp.ones((length, HALF), BF16)], axis=1))
+    ends = mm_by_two(lt_ref[...], jnp.concatenate([later, jnp.ones((length, HALF), BF16)], axis=1))
     second.wait()
     b_turned = turned(b_ref[...])
     hi, lo = split2(jnp.exp(ends))
@@ -411,7 +417,7 @@
     mine = iota((heads, width), 1) // P_SIZE == iota((heads, width), 0)
     start = jnp.sum(jnp.where(mine, start, 0.0), axis=1, keepdims=True)
     whole = jnp.exp(jnp.sum(lt_ref[...], axis=1, keepdims=True))
-    ol_ref[...] = gl_ref[...] + mm_by(late, triangle(length, lambda i, j: i < j)) + whole * start
+    ol_ref[...] = gl_ref[...] + mm_by_two(late, triangle(length, lambda i, j: i < j)) + whole * start
     copies[2].start()
     for copy in copies[:5]:
         copy.wait()

time: 90.7 us -> 90.7 us (level)
  no operation moved by 1% of the time
where the time goes in v9:
time: 90.7 us; the launch traced here: 90 us
  blocking collectives  49.8 us (55%)
  Pallas kernels  17.7 us (20%)
  waiting for transfers between devices  11.2 us (12%)
  starting transfers between devices  10.6 us (12%)
    all_to_all x3, blocking collectives, exchange(): got = lax.all_to_all(messages.reshape(count, 1, rows * HALF), axes, 0, 0)  49.8 us
    pallas_call x8, Pallas kernels, call(): pl.pallas_call(kernel, name=name, out_shape=[space(o.shape, o.dtype) for...  17.7 us
    all_to_all x2, waiting for transfers between devices, exchange(): got = lax.all_to_all(messages.reshape(count, 1, rows * HALF), axes, 0, 0)  11.2 us
    all_to_all x2, starting transfers between devices, exchange(): got = lax.all_to_all(messages.reshape(count, 1, rows * HALF), axes, 0, 0)  10.6 us
  transfers between devices with their start and end apart: 2, of which 2 were waited for; matrix products, arithmetic and copies ran while one was open for 0% of the time, Pallas kernels for 12%

profile of v9, /device:TPU:1, one launch (start us, length us, event | category | flops | bytes accessed | tf_op | source)
XLA Modules:
  0.0 90.0 jit_solution(7993272766029889580)
XLA Ops:
  0.6 1.6 %start.1 = f32[1056,128]{1,0:T(8,128)S(1)} custom-call(f32[16,256]{1,0:T(8,128)} %bitcast.26, bf16[256,1024]{1,0:T(8,128)(2,1)} %x_hbm.5, bf16[256,128]{1,0:T(8,128)(2,1)} %b_hbm.5), custom_call_target="tpu_custom_call" | custom-call | flops 1000000000 | bytes 1146880 | tf_op jit(solution)/shard_map/start/pallas_call | solution.py:430
  2.3 19.6 %all_to_all.25 = f32[32,1,4224]{2,1,0:T(1,128)S(1)} all-to-all(f32[32,1,4224]{2,1,0:T(1,128)S(1)} %bitcast.20), channel_id=1, replica_groups=mesh['outer'=8,'inner'=4,'heads'=8] {'outer','inner'}, dimensions={0} | all-to-all | bytes 1081344 | tf_op jit(solution)/shard_map/all_to_all | solution.py:444
  21.8 0.9 prefix.1
  22.7 4.6 %all-to-all-start.1 = ((f32[32,1,4096]{2,1,0:T(1,128)}), f32[32,1,4096]{2,1,0:T(1,128)S(1)}, u32[]{:S(2)}, u32[]{:S(2)}) async-start(f32[32,1,4096]{2,1,0:T(1,128)} %bitcast.3), calls=%async_computation.1 | async-start | bytes 1048576 | tf_op jit(solution)/shard_map/all_to_all | solution.py:444
  27.3 4.0 %local.1 = (f32[256,1024]{1,0:T(8,128)S(1)}, f32[256,1024]{1,0:T(8,128)S(1)}, bf16[256,128]{1,0:T(8,128)(2,1)S(1)}, bf16[128,256]{1,0:T(8,128)(2,1)S(1)}, f32[1,...) custom-call(f32[16,256]{1,0:T(8,128)} %bitcast.27, bf16[256,1024]{1,0:T(8,128)(2,1)} %x_hbm.5, ...), custom_call_target="tpu_custom_call" | custom-call | flops 8000000000 | bytes 5529664 | tf_op jit(solution)/shard_map/local/pallas_call | solution.py:430
  31.3 7.1 %all-to-all-done.1 = f32[32,1,4096]{2,1,0:T(1,128)S(1)} async-done(((f32[32,1,4096]{2,1,0:T(1,128)}), f32[32,1,4096]{2,1,0:T(1,128)S(1)}, u32[]{:S(2)}, u32[]{:S(2)}) %all-to-all-start.1) | async-done | bytes 524320 | tf_op jit(solution)/shard_map/all_to_all | solution.py:444
  38.4 0.6 gated.1
  39.0 14.6 %all_to_all.26 = f32[8,1,512]{2,1,0:T(1,128)S(1)} all-to-all(f32[8,1,512]{2,1,0:T(1,128)S(1)} %bitcast.24), channel_id=1, replica_groups=mesh['outer'=8,'inner'=4,'heads'=8] {'heads'}, dimensions={0} | all-to-all | bytes 32768 | tf_op jit(solution)/shard_map/all_to_all | solution.py:444
  53.6 1.5 %back.1 = (f32[1056,128]{1,0:T(8,128)}, f32[8,128]{1,0:T(8,128)}, f32[1024,128]{1,0:T(8,128)}) custom-call(f32[32,128]{1,0:T(8,128)S(1)} %bitcast.23, f32[256,1024]{1,0:T(8,128)S(1)} %get-tuple-element.42.refs_1_, f32[256,1024]{1,0:T(8,128)S(1)} %get-tuple-element.38.esilu_ref.refs_2_, bf16[256,1024]{1,0:T(8,128)(2,1)S(1)} %get-tuple-element.39.dout_ref.refs_3_, ...), custom_call_target="tpu_custom_call" | custom-call | flops 1000000000 | bytes 4300800 | tf_op jit(solution)/shard_map/back/pallas_call | solution.py:430
  55.1 6.0 %all-to-all-start.3 = ((f32[32,1,4224]{2,1,0:T(1,128)}), f32[32,1,4224]{2,1,0:T(1,128)S(1)}, u32[]{:S(2)}, u32[]{:S(2)}) async-start(f32[32,1,4224]{2,1,0:T(1,128)} %bitcast.25), calls=%async_computation.3 | async-start | bytes 1081344 | tf_op jit(solution)/shard_map/all_to_all | solution.py:444
  61.1 7.1 %grads.1 = (f32[256,1024]{1,0:T(8,128)S(1)}, f32[256,128]{1,0:T(8,128)S(1)}, f32[16,256]{1,0:T(8,128)S(1)}, f32[256,1024]{1,0:T(8,128)S(1)}, bf16[256,1024]{1,0:...) custom-call(f32[16,256]{1,0:T(8,128)} %bitcast.28, ...), custom_call_target="tpu_custom_call" | custom-call | flops 16000000000 | bytes 6795328 | tf_op jit(solution)/shard_map/grads/pallas_call | solution.py:430
  68.2 4.2 %all-to-all-done.3 = f32[32,1,4224]{2,1,0:T(1,128)S(1)} async-done(((f32[32,1,4224]{2,1,0:T(1,128)}), f32[32,1,4224]{2,1,0:T(1,128)S(1)}, u32[]{:S(2)}, u32[]{:S(2)}) %all-to-all-start.3) | async-done | bytes 540704 | tf_op jit(solution)/shard_map/all_to_all | solution.py:444
  72.4 0.1 suffix.1
  72.4 15.7 %all_to_all.27 = f32[32,1,4352]{2,1,0:T(1,128)S(1)} all-to-all(f32[32,1,4352]{2,1,0:T(1,128)S(1)} %bitcast.16), channel_id=1, replica_groups=mesh['outer'=8,'inner'=4,'heads'=8] {'outer','inner'}, dimensions={0} | all-to-all | bytes 1114112 | tf_op jit(solution)/shard_map/all_to_all | solution.py:444
  88.1 1.9 %final.1 = (bf16[256,1024]{1,0:T(8,128)(2,1)}, f32[256,128]{1,0:T(8,128)}, f32[16,256]{1,0:T(8,128)}, f32[1,16]{1,0:T(1,128)}, f32[8,128]{1,0:T(8,128)}) custom-call(f32[1088,128]{1,0:T(8,128)S(1)} %bitcast.19, f32[1024,128]{1,0:T(8,128)} %get-tuple-element.48.s_hbm, f32[16,256]{1,0:T(8,128)} %bitcast.29, f32[256,1024]{1,0:T(8,128)S(1)} %get-tuple-element.50.tail_ref, ...), custom_call_target="tpu_custom_call" | custom-call | flops 2000000000 | bytes 4608064 | tf_op jit(solution)/shard_map/final/pallas_call | solution.py:430
Async XLA Ops:
  22.7 15.7 %all-to-all-start.1 = ((f32[32,1,4096]{2,1,0:T(1,128)}), f32[32,1,4096]{2,1,0:T(1,128)S(1)}, u32[]{:S(2)}, u32[]{:S(2)}) async-start(f32[32,1,4096]{2,1,0:T(1,128)} %bitcast.3), calls=%async_computation.1 | async-start | bytes 1048576 | tf_op jit(solution)/shard_map/all_to_all | solution.py:444
  55.1 17.3 %all-to-all-start.3 = ((f32[32,1,4224]{2,1,0:T(1,128)}), f32[32,1,4224]{2,1,0:T(1,128)S(1)}, u32[]{:S(2)}, u32[]{:S(2)}) async-start(f32[32,1,4224]{2,1,0:T(1,128)} %bitcast.25), calls=%async_computation.3 | async-start | bytes 1081344 | tf_op jit(solution)/shard_map/all_to_all | solution.py:444
